TPU v7x, 512 devices: a whole 4x4x16 slice. The times are simulated.
512 devices in a mesh: ctx: 64 (over x, z_lo, core), tp: 8 (over z_hi, y).
Axes of the slice: x: 4, y: 4, z: 16 (z_hi: 2, z_lo: 8; z = z_hi * 8 + z_lo), core: 2. Of those that a mesh axis runs over, the one named last changes fastest.
Arguments:
- states: bfloat16 [4096, 8192], P(None, 'ctx'), may hold values from -6 to 6
- qkv: bfloat16 [4096, 6144], P('ctx', 'tp'), may hold values from -40 to 40
- grad_out: bfloat16 [4096, 4096], P('ctx', 'tp'), may hold values from -6 to 6
- weight: bfloat16 [8192, 6144], P('ctx', 'tp'), may hold values from -0.0625 to 0.0625
- offsets: int32 [128], replicated, may hold values from 0 to 4064, as said below
Outputs:
- grad_states: bfloat16 [4096, 8192], P(None, 'ctx')
- grad_weight: float32 [8192, 6144], P('ctx', 'tp')
Inputs may be any that keep to these rules, and one draw needn't show every extreme that they name: `offsets`: for each index i of ctx the two slabs are some slab p and slab 2 * 64 - 1 - p, each slab once, times 32.
All inputs are finite; a program needn't handle non-finite values.
Results may differ from a plain program's by a relative error of at most 0.017.
Values may be sent and summed in bfloat16 or wider, within the bound.
No kernel may reach another device: no remote copies, remote signals or barrier semaphores. Data moves between devices by JAX's collectives and lax.ppermute only.
A program may use at most 64 MiB of HBM per device.

v0:
```python
import jax
import jax.numpy as jnp
from jax import lax
from jax.sharding import PartitionSpec as P

HEADS = 32
KV_HEADS = 8
HEAD_DIM = 128


def body(states, qkv, grad_out, weight, offsets):
    rows, columns = qkv.shape
    group = HEADS // KV_HEADS
    width = (group + 2) * HEAD_DIM
    local_heads = columns // width
    half = rows // 2
    scale = HEAD_DIM ** (-0.5)
    index = lax.axis_index("ctx")
    mine = lax.dynamic_slice_in_dim(offsets, index * 2, 2)
    steps_arr = jnp.arange(half, dtype=jnp.int32)
    query_pos = (mine[:, None] + steps_arr[None, :]).reshape(-1)
    key_pos = (offsets[:, None] + steps_arr[None, :]).reshape(-1)
    blocks = qkv.reshape(rows, local_heads, group + 2, HEAD_DIM)
    queries = blocks[:, :, :group]
    pairs = blocks[:, :, group:].reshape(rows, local_heads * 2 * HEAD_DIM)
    pairs_all = lax.all_gather(pairs, "ctx", axis=0, tiled=True)
    total = pairs_all.shape[0]
    pairs_all = pairs_all.reshape(total, local_heads, 2, HEAD_DIM)
    cotangent = grad_out.reshape(rows, local_heads, group, HEAD_DIM)
    visible = key_pos[None, :] <= query_pos[:, None]
    key_rows = pairs_all[:, 0, 0]
    value_rows = pairs_all[:, 0, 1]
    query_heads = jnp.moveaxis(queries[:, 0], 1, 0)
    grad_heads = jnp.moveaxis(cotangent[:, 0], 1, 0)

    def head_step(carry, xs):
        dkey_acc, dvalue_acc = carry
        query_one, grad_one = xs
        scores = (
            jnp.einsum("td,sd->ts", query_one, key_rows, preferred_element_type=jnp.float32) * scale
        )
        scores = jnp.where(visible, scores, -jnp.inf)
        top = jnp.max(scores, axis=-1, keepdims=True)
        expd = jnp.exp(scores - top)
        probs = expd / jnp.sum(expd, axis=-1, keepdims=True)
        rounded = probs.astype(jnp.bfloat16)
        output = jnp.dot(rounded, value_rows, preferred_element_type=jnp.float32)
        delta = jnp.sum(grad_one.astype(jnp.float32) * output, axis=-1)
        dprob = jnp.einsum("td,sd->ts", grad_one, value_rows, preferred_element_type=jnp.float32)
        dscore = (probs * (dprob - delta[:, None]) * scale).astype(jnp.bfloat16)
        dquery_one = jnp.dot(dscore, key_rows, preferred_element_type=jnp.float32).astype(
            jnp.bfloat16
        )
        dkey_acc = dkey_acc + jnp.einsum(
            "ts,td->sd", dscore, query_one, preferred_element_type=jnp.float32
        )
        dvalue_acc = dvalue_acc + jnp.einsum(
            "ts,td->sd", rounded, grad_one, preferred_element_type=jnp.float32
        )
        return ((dkey_acc, dvalue_acc), dquery_one)

    start = (jnp.zeros((total, HEAD_DIM), jnp.float32), jnp.zeros((total, HEAD_DIM), jnp.float32))
    (dkey_head, dvalue_head), dquery_heads = lax.scan(head_step, start, (query_heads, grad_heads))
    dquery_list = [jnp.moveaxis(dquery_heads, 0, 1)]
    dpair_list = [jnp.stack([dkey_head, dvalue_head], axis=1)]
    dquery = jnp.stack(dquery_list, axis=1)
    dpair_part = jnp.stack(dpair_list, axis=1).reshape(total, local_heads * 2 * HEAD_DIM)
    dpair_own = lax.psum_scatter(dpair_part, "ctx", scatter_dimension=0, tiled=True)
    dpair_own = dpair_own.astype(jnp.bfloat16).reshape(rows, local_heads, 2, HEAD_DIM)
    local_grads = jnp.concatenate([dquery, dpair_own], axis=2).reshape(rows, columns)
    row_grads = lax.all_gather(local_grads, "ctx", axis=0, tiled=True)
    input_part = jnp.einsum("tc,dc->td", row_grads, weight, preferred_element_type=jnp.float32)
    grad_states = lax.psum(input_part.astype(jnp.bfloat16), "tp")
    grad_weight = jnp.einsum("td,tc->dc", states, row_grads, preferred_element_type=jnp.float32)
    return (grad_states, grad_weight)


def solution(mesh):
    placed = (P(None, "ctx"), P("ctx", "tp"), P("ctx", "tp"), P("ctx", "tp"), P())
    return jax.shard_map(
        body,
        mesh=mesh,
        in_specs=placed,
        out_specs=(P(None, "ctx"), P("ctx", "tp")),
        check_vma=False,
    )
```

profile of v0, /device:TPU:40, one launch (start us, length us, event | category | flops | bytes accessed | tf_op | source)
XLA Modules:
  0.0 932.5 jit_solution(7807841241549359207)
XLA Ops:
  7.2 1.1 reshape.52
  11.8 123.7 %all-gather.3.cloned.1.call-done = bf16[4096,256]{1,0:T(8,128)(2,1)} async-done(((bf16[64,256]{1,0:T(8,128)(2,1)}), bf16[4096,256]{1,0:T(8,128)(2,1)}) %all-gather.3.cloned.1.call-update) | async-done | bytes 2097168 | tf_op jit(solution)/shard_map/all_gather | solution.py:26
  135.4 2.9 copy.30
  138.3 1.5 slice_bitcast_fusion
  139.8 2.3 copy.34
  142.8 30.2 %while.15 = (s32[]{:T(128)}, f32[4096,128]{1,0:T(8,128)}, f32[4096,128]{1,0:T(8,128)}, bf16[4,64,128]{2,1,0:T(8,128)(2,1)S(1)}, bf16[4,64,128]{2,1,0:T(8,128)(2,...) while((s32[]{:T(128)}, f32[4096,128]{1,0:T(8,128)}, ...), condition=%wide.region_4.5_spmd.clone, body=%wide.region_0.4_spmd.clone.sunk | while | flops 409501504 | bytes 57266984 | solution.py:63
  146.2 1.0 convolution_add_fusion.5
  149.1 1.3 copy-done.2
  153.7 1.0 convolution_add_fusion.5
  156.6 1.3 copy-done.2
  161.2 1.0 convolution_add_fusion.5
  164.1 1.3 copy-done.2
  168.8 1.0 convolution_add_fusion.5
  171.7 1.3 copy-done.2
  173.0 1.9 copy.35
  174.9 2.9 copy.36
  177.9 3.9 pad_maximum_fusion
  181.7 5.6 copy.41
  187.4 428.5 %reduce-scatter.4.cloned.1.call-done = f32[64,256]{1,0:T(8,128)} async-done(((f32[4096,256]{1,0:T(8,128)}), f32[64,256]{1,0:T(8,128)}) %reduce-scatter.4.cloned.1.call-update) | async-done | bytes 65552 | tf_op jit(solution)/shard_map/reduce_scatter | solution.py:68
  617.6 129.8 %all-gather.5.cloned.1.call-done = bf16[4096,768]{1,0:T(8,128)(2,1)} async-done(((bf16[64,768]{1,0:T(8,128)(2,1)}), bf16[4096,768]{1,0:T(8,128)(2,1)}) %all-gather.5.cloned.1.call-update) | async-done | bytes 6291472 | tf_op jit(solution)/shard_map/all_gather | solution.py:71
  747.4 5.5 convolution_convert_fusion.1
  753.0 4.6 convolution_bitcast_fusion
  758.5 165.1 %all-reduce.2.cloned.1.call-done = bf16[4096,128]{1,0:T(8,128)(2,1)} async-done(((bf16[4096,128]{1,0:T(8,128)(2,1)}), bf16[4096,128]{1,0:T(8,128)(2,1)}) %all-reduce.2.cloned.1.call-update) | async-done | bytes 1048592 | tf_op jit(solution)/shard_map/psum | solution.py:73
  923.7 2.3 copy.63
  (96 shorter events, 27.2 us)
Async XLA Ops:
  7.2 745.8 %copy-start = (bf16[4096,128]{1,0:T(8,128)(2,1)S(1)}, bf16[4096,128]{1,0:T(8,128)(2,1)}, u32[]{:S(2)}) copy-start(bf16[4096,128]{1,0:T(8,128)(2,1)} %param.7) | copy-start | bytes 3145732
  7.2 128.2 %all-gather.3.cloned.1.call-start = ((), (), s32[]{:S(2)}) async-start(), calls=%async_computation.1 | async-start | bytes 2129920 | tf_op jit(solution)/shard_map/all_gather | solution.py:26
  9.0 606.9 %reduce-scatter.4.cloned.1.call-start = ((), (), s32[]{:S(2)}) async-start(), calls=%async_computation.4 | async-start | bytes 4259840 | tf_op jit(solution)/shard_map/reduce_scatter | solution.py:68
  139.8 2.4 copy-start.3
  142.9 1.2 copy-start.6
  144.6 1.6 copy-start.4
  146.2 1.6 copy-start.1
  147.7 1.3 copy-start.5
  149.1 1.3 copy-start.2
  152.1 1.6 copy-start.4
  153.7 1.6 copy-start.1
  155.3 1.3 copy-start.5
  156.6 1.3 copy-start.2
  159.6 1.6 copy-start.4
  161.2 1.6 copy-start.1
  162.8 1.3 copy-start.5
  164.1 1.3 copy-start.2
  167.2 1.6 copy-start.4
  168.8 1.6 copy-start.1
  170.4 1.3 copy-start.5
  171.7 1.3 copy-start.2
  187.4 560.0 %copy-start.7 = (bf16[128,768]{1,0:T(8,128)(2,1)S(1)}, bf16[128,768]{1,0:T(8,128)(2,1)}, u32[]{:S(2)}) copy-start(bf16[128,768]{1,0:T(8,128)(2,1)} %param.10) | copy-start | bytes 589828
  187.4 560.0 %all-gather.5.cloned.1.call-start = ((), (), s32[]{:S(2)}) async-start(), calls=%async_computation.2 | async-start | bytes 6389760 | tf_op jit(solution)/shard_map/all_gather | solution.py:71
  617.6 306.1 %all-reduce.2.cloned.1.call-start = ((), (), s32[]{:S(2)}) async-start(), calls=%async_computation.3 | async-start | bytes 2097152 | tf_op jit(solution)/shard_map/psum | solution.py:73
  (3 other events, 3.7 us)
Sparse Core Ops, SparseCore 0:
  10.7 124.6 all-gather.2
  187.5 428.3 reduce-scatter.3
  618.9 128.4 all-gather.4
  753.1 170.5 all-reduce.1
where the time goes:
time: 933 us; the launch traced here: 932 us
  waiting for transfers between devices  847 us (91%)
  local copies, waits for them, and re-layouts  38.9 us (4%)
  matrix products  25.3 us (3%)
  between operations  13.9 us (1%)
    reduce_scatter x1, waiting for transfers between devices, body(): lax.psum_scatter(dpair_part, 'ctx', scatter_dimension=0, tiled=True)  428 us
    psum x1, waiting for transfers between devices, body(): grad_states = lax.psum(input_part.astype(jnp.bfloat16), 'tp')  165 us
    all_gather x1, waiting for transfers between devices, body(): row_grads = lax.all_gather(local_grads, 'ctx', axis=0, tiled=True)  130 us
    all_gather x1, waiting for transfers between devices, body(): pairs_all = lax.all_gather(pairs, 'ctx', axis=0, tiled=True)  124 us
  transfers between devices with their start and end apart: 4, of which 4 were waited for; matrix products, arithmetic and copies ran while one was open for 1% of the time, Pallas kernels for 0%

commit v1 on v0

v1 whole, which is shorter than its diff:
```python
import functools

import jax
import jax.numpy as jnp
from jax import lax
from jax.experimental import pallas as pl
from jax.experimental.pallas import tpu as pltpu
from jax.sharding import Mesh
from jax.sharding import PartitionSpec as P

HEADS = 32
KV_HEADS = 8
HEAD_DIM = 128
GROUP = HEADS // KV_HEADS
X, Z, C, W, Y = 4, 8, 2, 2, 4
CHUNK = 512
BF = jnp.bfloat16
F32 = jnp.float32


def dot(a, b, contract):
    return lax.dot_general(a, b, (contract, ((), ())), preferred_element_type=F32)


def attention_kernel(q_ref, g_ref, own_ref, other_ref, qpos_ref, kpos_ref, dq_ref, down_ref, dother_ref, s_ref):
    half = own_ref.shape[0]
    steps = half // CHUNK
    scale = HEAD_DIM ** (-0.5)
    q = q_ref[...]
    g = g_ref[...]
    qpos = qpos_ref[...]
    rows = q.shape[0]
    sides = ((own_ref, down_ref), (other_ref, dother_ref))

    top = jnp.full((1, rows), -jnp.inf, F32)
    for side, (kv_ref, _) in enumerate(sides):
        for n in range(steps):
            at = n * CHUNK
            keys = kv_ref[at : at + CHUNK, :HEAD_DIM]
            scores = dot(keys, q, ((1,), (1,))) * scale
            visible = kpos_ref[side * half + at : side * half + at + CHUNK, :] <= qpos
            scores = jnp.where(visible, scores, -jnp.inf)
            s_ref[side * half + at : side * half + at + CHUNK, :] = scores
            top = jnp.maximum(top, jnp.max(scores, axis=0, keepdims=True))

    total = jnp.zeros((1, rows), F32)
    for n in range(2 * steps):
        at = n * CHUNK
        expd = jnp.exp(s_ref[at : at + CHUNK, :] - top)
        s_ref[at : at + CHUNK, :] = expd
        total = total + jnp.sum(expd, axis=0, keepdims=True)
    inverse = 1.0 / total

    output = jnp.zeros((HEAD_DIM, rows), F32)
    for side, (kv_ref, dkv_ref) in enumerate(sides):
        for n in range(steps):
            at = n * CHUNK
            values = kv_ref[at : at + CHUNK, HEAD_DIM:]
            probs = s_ref[side * half + at : side * half + at + CHUNK, :] * inverse
            s_ref[side * half + at : side * half + at + CHUNK, :] = probs
            rounded = probs.astype(BF)
            output = output + dot(values, rounded, ((0,), (0,)))
            dkv_ref[at : at + CHUNK, HEAD_DIM:] = dot(rounded, g, ((1,), (0,))).astype(dkv_ref.dtype)
    delta = jnp.sum(output * g.astype(F32).T, axis=0, keepdims=True)

    dquery = jnp.zeros((HEAD_DIM, rows), F32)
    for side, (kv_ref, dkv_ref) in enumerate(sides):
        for n in range(steps):
            at = n * CHUNK
            keys = kv_ref[at : at + CHUNK, :HEAD_DIM]
            values = kv_ref[at : at + CHUNK, HEAD_DIM:]
            dprob = dot(values, g, ((1,), (1,)))
            probs = s_ref[side * half + at : side * half + at + CHUNK, :]
            dscore = (probs * (dprob - delta) * scale).astype(BF)
            dquery = dquery + dot(keys, dscore, ((0,), (0,)))
            dkv_ref[at : at + CHUNK, :HEAD_DIM] = dot(dscore, q, ((1,), (0,))).astype(dkv_ref.dtype)
    dq_ref[...] = dquery.T.astype(BF)


def attention(q, g, own, other, qpos, kpos, interpret=False):
    rows = q.shape[0]
    half = own.shape[0]
    vmem = pl.BlockSpec(memory_space=pltpu.VMEM)
    return pl.pallas_call(
        attention_kernel,
        out_shape=(
            jax.ShapeDtypeStruct((rows, HEAD_DIM), BF),
            jax.ShapeDtypeStruct((half, 2 * HEAD_DIM), F32),
            jax.ShapeDtypeStruct((half, 2 * HEAD_DIM), BF),
        ),
        in_specs=[vmem] * 6,
        out_specs=(vmem,) * 3,
        scratch_shapes=[pltpu.VMEM((2 * half, rows), F32)],
        compiler_params=pltpu.CompilerParams(vmem_limit_bytes=40 * 1024 * 1024),
        interpret=interpret,
    )(q, g, own, other, qpos, kpos)


def gather(x, axis, size):
    copies = jnp.broadcast_to(x[None], (size,) + x.shape)
    return lax.all_to_all(copies, axis, 0, 0, tiled=True)


def swap(x, axis):
    return lax.ppermute(x, axis, [(0, 1), (1, 0)])


def body(states, qkv, grad_out, weight, offsets):
    rows, columns = qkv.shape
    half = rows // 2
    core = lax.axis_index("c")
    place = lax.axis_index("x") * (Z * C) + lax.axis_index("z") * C + core
    slab = jnp.arange(half, dtype=jnp.int32)
    mine = lax.dynamic_slice_in_dim(offsets, place * 2, 2)
    query_pos = (mine[:, None] + slab[None, :]).reshape(rows)
    query_pos = jnp.repeat(query_pos, GROUP)[None, :]
    key_off = jnp.moveaxis(offsets.reshape(X * Z, C, 2), 1, 0)
    key_off = jnp.where(core == 0, key_off, key_off[::-1])
    key_pos = (key_off.reshape(-1)[:, None] + slab[None, :]).reshape(-1, 1)

    wide = GROUP * HEAD_DIM
    pairs = qkv[:, wide:]
    pairs_z = gather(pairs, "z", Z)
    own = gather(pairs_z, "x", X).reshape(X * Z * rows, 2 * HEAD_DIM)
    other = swap(own, "c")

    q = qkv[:, :wide].reshape(rows * GROUP, HEAD_DIM)
    g = grad_out.reshape(rows * GROUP, HEAD_DIM)
    dq, dkv_own, dkv_other = attention(q, g, own, other, query_pos, key_pos)

    dkv = dkv_own + swap(dkv_other, "c").astype(F32)
    dkv = lax.all_to_all(dkv.astype(BF).reshape(X, Z * rows, 2 * HEAD_DIM), "x", 0, 0, tiled=True)
    dkv = jnp.sum(dkv.astype(F32), axis=0).astype(BF)
    dkv = lax.all_to_all(dkv.reshape(Z, rows, 2 * HEAD_DIM), "z", 0, 0, tiled=True)
    dkv = jnp.sum(dkv.astype(F32), axis=0).astype(BF)

    grads = jnp.concatenate([dq.reshape(rows, wide), dkv], axis=1)
    grads = gather(grads, "z", Z)
    grads_own = gather(grads, "x", X).reshape(X * Z * rows, columns)
    grads_other = swap(grads_own, "c")

    depth = weight.shape[0]
    part_own = dot(grads_own, weight, ((1,), (1,))).astype(BF).reshape(X * Z, rows, depth)
    part_other = dot(grads_other, weight, ((1,), (1,))).astype(BF).reshape(X * Z, rows, depth)
    first = jnp.where(core == 0, part_own, part_other)
    second = jnp.where(core == 0, part_other, part_own)
    part = jnp.stack([first, second], axis=1).reshape(Y, X * Z * C * rows // Y, depth)
    part = lax.all_to_all(part, "y", 0, 0, tiled=True)
    part = jnp.sum(part.astype(F32), axis=0).astype(BF)
    part = (part.astype(F32) + swap(part, "w").astype(F32)).astype(BF)
    grad_states = gather(part, "y", Y).reshape(X * Z * C * rows, depth)

    split = states.reshape(X * Z, C, rows, depth)
    states_own = lax.dynamic_index_in_dim(split, core, 1, keepdims=False).reshape(-1, depth)
    states_other = lax.dynamic_index_in_dim(split, 1 - core, 1, keepdims=False).reshape(-1, depth)
    grad_weight = dot(states_own, grads_own, ((0,), (0,))) + dot(states_other, grads_other, ((0,), (0,)))
    return grad_states, grad_weight


def solution(mesh):
    fine = Mesh(mesh.devices.reshape(X, Z, C, W, Y), ("x", "z", "c", "w", "y"))
    ctx, tp = ("x", "z", "c"), ("w", "y")
    return jax.shard_map(
        body,
        mesh=fine,
        in_specs=(P(None, ctx), P(ctx, tp), P(ctx, tp), P(ctx, tp), P()),
        out_specs=(P(None, ctx), P(ctx, tp)),
        check_vma=False,
    )
```

time: 933 us -> 279 us (0.30)
  the two profiles are of different devices: /device:TPU:40 before, /device:TPU:2 now
where the time goes in v1:
time: 279 us; the launch traced here: 278 us
  blocking collectives  163 us (58%)
  waiting for transfers between devices  60.5 us (22%)
  starting transfers between devices  27.5 us (10%)
  local copies, waits for them, and re-layouts  10.8 us (4%)
  Pallas kernels  6.12 us (2%)
  other arithmetic  4.71 us (2%)
  matrix products  3.98 us (1%)
    all_to_all x4, blocking collectives, gather(): return lax.all_to_all(copies, axis, 0, 0, tiled=True)  125 us
    ppermute x4, waiting for transfers between devices, swap(): return lax.ppermute(x, axis, [(0, 1), (1, 0)])  33.4 us
    all_to_all x1, blocking collectives, body(): part = lax.all_to_all(part, 'y', 0, 0, tiled=True)  19.8 us
    all_to_all x1, blocking collectives, body(): lax.all_to_all(dkv.astype(BF).reshape(X, Z * rows, 2 * HEAD_DIM), 'x', 0,...  18.3 us
    all_to_all x1, waiting for transfers between devices, body(): lax.all_to_all(dkv.reshape(Z, rows, 2 * HEAD_DIM), 'z', 0, 0, tiled=True)  16.1 us
    ppermute x4, starting transfers between devices, swap(): return lax.ppermute(x, axis, [(0, 1), (1, 0)])  14.4 us
    all_to_all x1, waiting for transfers between devices, gather(): return lax.all_to_all(copies, axis, 0, 0, tiled=True)  11 us
    all_to_all x1, starting transfers between devices, body(): lax.all_to_all(dkv.reshape(Z, rows, 2 * HEAD_DIM), 'z', 0, 0, tiled=True)  8.85 us
  transfers between devices with their start and end apart: 6, of which 5 were waited for; matrix products, arithmetic and copies ran while one was open for 3% of the time, Pallas kernels for 0%

profile of v1, /device:TPU:2, one launch (start us, length us, event | category | flops | bytes accessed | tf_op | source)
XLA Modules:
  0.0 277.7 jit_solution(11153642556870538906)
XLA Ops:
  1.5 29.0 %all_to_all.40 = bf16[8,64,256]{2,1,0:T(8,128)(2,1)S(1)} all-to-all(bf16[8,64,256]{2,1,0:T(8,128)(2,1)S(1)} %broadcast_in_dim.12), channel_id=1, replica_groups=mesh['x'=4,'z'=8,'c'=2,'w'=2,'y'=4] {'z'}, dimensions={0} | all-to-all | bytes 524288 | tf_op jit(solution)/shard_map/all_to_all | solution.py:101
  30.6 14.1 %all_to_all.41 = bf16[4,8,64,256]{3,2,1,0:T(8,128)(2,1)S(1)} all-to-all(bf16[4,8,64,256]{3,2,1,0:T(8,128)(2,1)S(1)} %broadcast_in_dim.13), channel_id=1, replica_groups=mesh['x'=4,'z'=8,'c'=2,'w'=2,'y'=4] {'x'}, dimensions={0} | all-to-all | bytes 2097152 | tf_op jit(solution)/shard_map/all_to_all | solution.py:101
  44.7 1.9 collective-permute-start
  47.6 2.1 add.85.kpos_ref
  50.7 6.1 %shard_map.68 = (bf16[256,128]{1,0:T(8,128)(2,1)S(1)}, f32[2048,256]{1,0:T(8,128)S(1)}, bf16[2048,256]{1,0:T(8,128)(2,1)S(1)}) custom-call(bf16[256,128]{1,0:T(8,128)(2,1)S(1)} %reshape.119.q_ref, bf16[256,128]{1,0:T(8,128)(2,1)S(1)} %reshape.120.g_ref, bf16[2048,256]{1,0:T(8,128)(2,1)S(1)} %bitcast.26, bf16[2048,256]{1,0:T(8,128)(2,1)} %collective-permute-done.other_ref, ...), custom_call_target="tpu_custom_call" | custom-call | tf_op jit(solution)/shard_map/pallas_call | solution.py:84
  56.8 2.4 collective-permute-start.1
  59.2 2.3 collective-permute-done.1
  61.7 18.3 %all_to_all.42 = bf16[4,512,256]{2,1,0:T(8,128)(2,1)S(1)} all-to-all(bf16[4,512,256]{2,1,0:T(8,128)(2,1)S(1)} %bitcast.31), channel_id=1, replica_groups=mesh['x'=4,'z'=8,'c'=2,'w'=2,'y'=4] {'x'}, dimensions={0} | all-to-all | bytes 2097152 | tf_op jit(solution)/shard_map/all_to_all | solution.py:132
  81.0 8.9 %all-to-all-start.3 = ((bf16[8,64,256]{2,1,0:T(8,128)(2,1)}), bf16[8,64,256]{2,1,0:T(8,128)(2,1)S(1)}, u32[]{:S(2)}, u32[]{:S(2)}) async-start(bf16[8,64,256]{2,1,0:T(8,128)(2,1)} %bitcast.3), calls=%async_computation.3 | async-start | bytes 524288 | tf_op jit(solution)/shard_map/all_to_all | solution.py:134
  89.9 16.1 %all-to-all-done.3 = bf16[8,64,256]{2,1,0:T(8,128)(2,1)S(1)} async-done(((bf16[8,64,256]{2,1,0:T(8,128)(2,1)}), bf16[8,64,256]{2,1,0:T(8,128)(2,1)S(1)}, u32[]{:S(2)}, u32[]{:S(2)}) %all-to-all-start.3) | async-done | bytes 262176 | tf_op jit(solution)/shard_map/all_to_all | solution.py:134
  106.1 44.4 %all_to_all.43 = bf16[8,64,768]{2,1,0:T(8,128)(2,1)S(1)} all-to-all(bf16[8,64,768]{2,1,0:T(8,128)(2,1)S(1)} %broadcast_in_dim.15), channel_id=1, replica_groups=mesh['x'=4,'z'=8,'c'=2,'w'=2,'y'=4] {'z'}, dimensions={0} | all-to-all | bytes 1572864 | tf_op jit(solution)/shard_map/all_to_all | solution.py:101
  150.8 37.6 %all_to_all.44 = bf16[4,8,64,768]{3,2,1,0:T(8,128)(2,1)S(1)} all-to-all(bf16[4,8,64,768]{3,2,1,0:T(8,128)(2,1)S(1)} %broadcast_in_dim.16), channel_id=1, replica_groups=mesh['x'=4,'z'=8,'c'=2,'w'=2,'y'=4] {'x'}, dimensions={0} | all-to-all | bytes 6291456 | tf_op jit(solution)/shard_map/all_to_all | solution.py:101
  188.4 1.9 collective-permute-start.2
  191.3 4.6 %collective-permute-done.2 = bf16[2048,768]{1,0:T(8,128)(2,1)S(1)} collective-permute-done((bf16[2048,768]{1,0:T(8,128)(2,1)S(1)}, bf16[2048,768]{1,0:T(8,128)(2,1)S(1)}, u32[]{:S(2)}, u32[]{:S(2)}) %collective-permute-start.2) | collective-permute-done | bytes 3145760 | tf_op jit(solution)/shard_map/ppermute | solution.py:105
  197.7 19.8 %all_to_all.45 = bf16[4,1024,128]{2,1,0:T(8,128)(2,1)} all-to-all(bf16[4,1024,128]{2,1,0:T(8,128)(2,1)S(1)} %bitcast.30), channel_id=1, replica_groups=mesh['x'=4,'z'=8,'c'=2,'w'=2,'y'=4] {'y'}, dimensions={0} | all-to-all | bytes 2097152 | tf_op jit(solution)/shard_map/all_to_all | solution.py:148
  217.4 2.1 reduce_sum.38
  219.6 8.2 %collective-permute-start.3 = (bf16[1024,128]{1,0:T(8,128)(2,1)}, bf16[1024,128]{1,0:T(8,128)(2,1)}, u32[]{:S(2)}, u32[]{:S(2)}) collective-permute-start(bf16[1024,128]{1,0:T(8,128)(2,1)} %reduce_sum.38), channel_id=1, source_target_pairs={{0,4},{4,0},{1,5},{5,1},{2,6},{6,2},{3,7},{7,3},{8,12},{12,8},{9,1... | collective-permute-start | bytes 786440 | tf_op jit(solution)/shard_map/ppermute | solution.py:105
  227.8 26.6 %collective-permute-done.3 = bf16[1024,128]{1,0:T(8,128)(2,1)} collective-permute-done((bf16[1024,128]{1,0:T(8,128)(2,1)}, bf16[1024,128]{1,0:T(8,128)(2,1)}, u32[]{:S(2)}, u32[]{:S(2)}) %collective-permute-start.3) | collective-permute-done | bytes 262176 | tf_op jit(solution)/shard_map/ppermute | solution.py:105
  255.5 1.1 broadcast_in_dim.17
  256.6 4.3 %all-to-all-start.7 = ((bf16[4,1024,128]{2,1,0:T(8,128)(2,1)}), bf16[4,1024,128]{2,1,0:T(8,128)(2,1)}, u32[]{:S(2)}, u32[]{:S(2)}) async-start(bf16[4,1024,128]{2,1,0:T(8,128)(2,1)} %broadcast_in_dim.17), calls=%async_computation.7 | async-start | bytes 2097152 | tf_op jit(solution)/shard_map/all_to_all | solution.py:101
  260.8 1.4 constant_dynamic-slice_fusion
  263.0 1.4 convolution_add_fusion
  264.4 11.0 %all-to-all-done.7 = bf16[4,1024,128]{2,1,0:T(8,128)(2,1)} async-done(((bf16[4,1024,128]{2,1,0:T(8,128)(2,1)}), bf16[4,1024,128]{2,1,0:T(8,128)(2,1)}, u32[]{:S(2)}, u32[]{:S(2)}) %all-to-all-start.7) | async-done | bytes 1048608 | tf_op jit(solution)/shard_map/all_to_all | solution.py:101
  275.4 2.3 copy.17
  (39 shorter events, 9.0 us)
Async XLA Ops:
  0.6 189.7 %copy-start = (bf16[128,768]{1,0:T(8,128)(2,1)S(1)}, bf16[128,768]{1,0:T(8,128)(2,1)}, u32[]{:S(2)}) copy-start(bf16[128,768]{1,0:T(8,128)(2,1)} %param.8) | copy-start | bytes 589828
  0.6 46.0 %copy-start.3 = (s32[128]{0:T(128)S(1)}, s32[128]{0:T(128)}, u32[]{:S(2)}) copy-start(s32[128]{0:T(128)} %param.9) | copy-start | bytes 1540
  30.5 19.2 %slice-start = ((bf16[64,768]{1,0:T(8,128)(2,1)}), bf16[64,512]{1,0:T(8,128)(2,1)S(1)}, s32[]{:S(2)}) async-start(bf16[64,768]{1,0:T(8,128)(2,1)} %param.6), calls=%async_computation.8 | async-start | bytes 131072 | tf_op jit(solution)/shard_map/slice | solution.py:127
  44.7 6.0 %collective-permute-start = (bf16[2048,256]{1,0:T(8,128)(2,1)S(1)}, bf16[2048,256]{1,0:T(8,128)(2,1)}, u32[]{:S(2)}, u32[]{:S(2)}) collective-permute-start(bf16[2048,256]{1,0:T(8,128)(2,1)S(1)} %bitcast.25), channel_id=1, source_target_pairs={{0,8},{8,0},{1,9},{9,1},{2,10},{10,2},{3,11},{11,3},{4,12},{12,4},... | collective-permute-start | bytes 3145736 | tf_op jit(solution)/shard_map/ppermute | solution.py:105
  56.8 4.7 %collective-permute-start.1 = (bf16[2048,256]{1,0:T(8,128)(2,1)S(1)}, bf16[2048,256]{1,0:T(8,128)(2,1)S(1)}, u32[]{:S(2)}, u32[]{:S(2)}) collective-permute-start(bf16[2048,256]{1,0:T(8,128)(2,1)S(1)} %get-tuple-element.7), channel_id=1, source_target_pairs={{0,8},{8,0},{1,9},{9,1},{2,10},{10,2},{3,11},{11,3},{4,12},{12,4},... | collective-permute-start | bytes 3145736 | tf_op jit(solution)/shard_map/ppermute | solution.py:105
  81.0 25.0 %all-to-all-start.3 = ((bf16[8,64,256]{2,1,0:T(8,128)(2,1)}), bf16[8,64,256]{2,1,0:T(8,128)(2,1)S(1)}, u32[]{:S(2)}, u32[]{:S(2)}) async-start(bf16[8,64,256]{2,1,0:T(8,128)(2,1)} %bitcast.3), calls=%async_computation.3 | async-start | bytes 524288 | tf_op jit(solution)/shard_map/all_to_all | solution.py:134
  188.4 7.5 %collective-permute-start.2 = (bf16[2048,768]{1,0:T(8,128)(2,1)S(1)}, bf16[2048,768]{1,0:T(8,128)(2,1)S(1)}, u32[]{:S(2)}, u32[]{:S(2)}) collective-permute-start(bf16[2048,768]{1,0:T(8,128)(2,1)S(1)} %bitcast.27), channel_id=1, source_target_pairs={{0,8},{8,0},{1,9},{9,1},{2,10},{10,2},{3,11},{11,3},{4,12},{12,4},... | collective-permute-start | bytes 9437192 | tf_op jit(solution)/shard_map/ppermute | solution.py:105
  195.9 1.6 copy-start.1
  219.6 34.8 %collective-permute-start.3 = (bf16[1024,128]{1,0:T(8,128)(2,1)}, bf16[1024,128]{1,0:T(8,128)(2,1)}, u32[]{:S(2)}, u32[]{:S(2)}) collective-permute-start(bf16[1024,128]{1,0:T(8,128)(2,1)} %reduce_sum.38), channel_id=1, source_target_pairs={{0,4},{4,0},{1,5},{5,1},{2,6},{6,2},{3,7},{7,3},{8,12},{12,8},{9,1... | collective-permute-start | bytes 786440 | tf_op jit(solution)/shard_map/ppermute | solution.py:105
  256.6 18.8 %all-to-all-start.7 = ((bf16[4,1024,128]{2,1,0:T(8,128)(2,1)}), bf16[4,1024,128]{2,1,0:T(8,128)(2,1)}, u32[]{:S(2)}, u32[]{:S(2)}) async-start(bf16[4,1024,128]{2,1,0:T(8,128)(2,1)} %broadcast_in_dim.17), calls=%async_computation.7 | async-start | bytes 2097152 | tf_op jit(solution)/shard_map/all_to_all | solution.py:101
  260.8 2.2 copy-start.2

commit v2 on v1

--- a/solution.py
+++ b/solution.py
@@ -85,7 +85,7 @@
         attention_kernel,
         out_shape=(
             jax.ShapeDtypeStruct((rows, HEAD_DIM), BF),
-            jax.ShapeDtypeStruct((half, 2 * HEAD_DIM), F32),
+            jax.ShapeDtypeStruct((half, 2 * HEAD_DIM), BF),
             jax.ShapeDtypeStruct((half, 2 * HEAD_DIM), BF),
         ),
         in_specs=[vmem] * 6,
@@ -96,70 +96,127 @@
     )(q, g, own, other, qpos, kpos)
 
 
+def project_kernel(at_ref, dq_own_ref, dq_other_ref, dkv_own_ref, dkv_other_ref, weight_ref, *out_refs):
+    mine = at_ref[0]
+    core = at_ref[1]
+    target = at_ref[2]
+    wide = GROUP * HEAD_DIM
+    for k, out_ref in enumerate(out_refs):
+        place = target ^ k
+        for side, (dq_ref, dkv_ref) in enumerate(((dq_own_ref, dkv_own_ref), (dq_other_ref, dkv_other_ref))):
+            part = dot(dq_ref[mine ^ place], weight_ref[:, :wide], ((1,), (1,)))
+            part = part + dot(dkv_ref[place], weight_ref[:, wide:], ((1,), (1,)))
+            out_ref[:, core ^ side] = part.astype(BF).reshape(out_ref.shape[0], out_ref.shape[2], part.shape[1])
+
+
+def place_kernel(at_ref, *refs):
+    out_ref = refs[-1]
+    for k in range(Y):
+        out_ref[at_ref[2] ^ k] = refs[k][...]
+
+
+def weight_kernel(at_ref, dq_own_ref, dq_other_ref, dkv_own_ref, dkv_other_ref, states_ref, out_ref):
+    mine = at_ref[0]
+    core = at_ref[1]
+    wide = GROUP * HEAD_DIM
+    depth = out_ref.shape[0]
+    dq_sum = jnp.zeros((depth, wide), F32)
+    dkv_sum = jnp.zeros((depth, 2 * HEAD_DIM), F32)
+    for k in range(X):
+        place = mine ^ k
+        for side, (dq_ref, dkv_ref) in enumerate(((dq_own_ref, dkv_own_ref), (dq_other_ref, dkv_other_ref))):
+            rows = states_ref[place, :, core ^ side].reshape(dq_ref.shape[1], depth)
+            dq_sum = dq_sum + dot(rows, dq_ref[k], ((0,), (0,)))
+            dkv_sum = dkv_sum + dot(rows, dkv_ref[place], ((0,), (0,)))
+    out_ref[:, :wide] = dq_sum
+    out_ref[:, wide:] = dkv_sum
+
+
+def local_call(kernel, count, shape, dtype, *operands):
+    vmem = pl.BlockSpec(memory_space=pltpu.VMEM)
+    return pl.pallas_call(
+        kernel,
+        out_shape=[jax.ShapeDtypeStruct(shape, dtype)] * count,
+        in_specs=[pl.BlockSpec(memory_space=pltpu.SMEM)] + [vmem] * (len(operands) - 1),
+        out_specs=[vmem] * count,
+        compiler_params=pltpu.CompilerParams(vmem_limit_bytes=40 * 1024 * 1024),
+    )(*operands)
+
+
 def gather(x, axis, size):
     copies = jnp.broadcast_to(x[None], (size,) + x.shape)
     return lax.all_to_all(copies, axis, 0, 0, tiled=True)
 
 
-def swap(x, axis):
-    return lax.ppermute(x, axis, [(0, 1), (1, 0)])
+def swap(x, axis, size=2, bit=1):
+    return lax.ppermute(x, axis, [(n, n ^ bit) for n in range(size)])
 
 
 def body(states, qkv, grad_out, weight, offsets):
     rows, columns = qkv.shape
     half = rows // 2
+    wide = GROUP * HEAD_DIM
+    pair = 2 * HEAD_DIM
     core = lax.axis_index("c")
-    place = lax.axis_index("x") * (Z * C) + lax.axis_index("z") * C + core
+    mine = lax.axis_index("x")
+    place = mine * (Z * C) + lax.axis_index("h") * (Z // 2 * C) + lax.axis_index("l") * C + core
     slab = jnp.arange(half, dtype=jnp.int32)
-    mine = lax.dynamic_slice_in_dim(offsets, place * 2, 2)
-    query_pos = (mine[:, None] + slab[None, :]).reshape(rows)
+    at = lax.dynamic_slice_in_dim(offsets, place * 2, 2)
+    query_pos = (at[:, None] + slab[None, :]).reshape(rows)
     query_pos = jnp.repeat(query_pos, GROUP)[None, :]
     key_off = jnp.moveaxis(offsets.reshape(X * Z, C, 2), 1, 0)
     key_off = jnp.where(core == 0, key_off, key_off[::-1])
     key_pos = (key_off.reshape(-1)[:, None] + slab[None, :]).reshape(-1, 1)
 
-    wide = GROUP * HEAD_DIM
-    pairs = qkv[:, wide:]
-    pairs_z = gather(pairs, "z", Z)
-    own = gather(pairs_z, "x", X).reshape(X * Z * rows, 2 * HEAD_DIM)
+    pairs_z = gather(qkv[:, wide:], ("h", "l"), Z)
+    own = gather(pairs_z, "x", X).reshape(X * Z * rows, pair)
     other = swap(own, "c")
 
     q = qkv[:, :wide].reshape(rows * GROUP, HEAD_DIM)
     g = grad_out.reshape(rows * GROUP, HEAD_DIM)
     dq, dkv_own, dkv_other = attention(q, g, own, other, query_pos, key_pos)
 
-    dkv = dkv_own + swap(dkv_other, "c").astype(F32)
-    dkv = lax.all_to_all(dkv.astype(BF).reshape(X, Z * rows, 2 * HEAD_DIM), "x", 0, 0, tiled=True)
-    dkv = jnp.sum(dkv.astype(F32), axis=0).astype(BF)
-    dkv = lax.all_to_all(dkv.reshape(Z, rows, 2 * HEAD_DIM), "z", 0, 0, tiled=True)
-    dkv = jnp.sum(dkv.astype(F32), axis=0).astype(BF)
-
-    grads = jnp.concatenate([dq.reshape(rows, wide), dkv], axis=1)
-    grads = gather(grads, "z", Z)
-    grads_own = gather(grads, "x", X).reshape(X * Z * rows, columns)
-    grads_other = swap(grads_own, "c")
+    dkv_in = swap(dkv_other, "c")
+    dq_z = gather(dq.reshape(rows, wide), ("h", "l"), Z).reshape(Z * rows, wide)
+    dkv = (dkv_own.astype(F32) + dkv_in.astype(F32)).astype(BF).reshape(X, Z * rows, pair)
+    blocks = [lax.dynamic_index_in_dim(dkv, mine ^ k, 0, keepdims=False) for k in range(X)]
+    total = blocks[0].astype(F32)
+    for k in range(1, X):
+        total = total + swap(blocks[k], "x", X, k).astype(F32)
+    dkv = total.astype(BF)
+    dkv, dq_z = lax.optimization_barrier((dkv, dq_z))
+
+    dq_x = [dq_z] + [swap(dq_z, "x", X, k) for k in range(1, X)]
+    dkv = lax.all_to_all(dkv.reshape(2, Z // 2, rows, pair), "l", 1, 1, tiled=True)
+    dkv = jnp.sum(dkv.astype(F32), axis=1).astype(BF)
+    dkv = (dkv.astype(F32) + swap(dkv, "h").astype(F32)).astype(BF)
+    dkv_z = jnp.moveaxis(gather(dkv, "l", Z // 2), 0, 1).reshape(Z * rows, pair)
+
+    dkv_own = gather(dkv_z, "x", X)
+    dq_own = jnp.stack(dq_x)
+    dq_other = swap(dq_own, "c")
+    dkv_other = swap(dkv_own, "c")
 
     depth = weight.shape[0]
-    part_own = dot(grads_own, weight, ((1,), (1,))).astype(BF).reshape(X * Z, rows, depth)
-    part_other = dot(grads_other, weight, ((1,), (1,))).astype(BF).reshape(X * Z, rows, depth)
-    first = jnp.where(core == 0, part_own, part_other)
-    second = jnp.where(core == 0, part_other, part_own)
-    part = jnp.stack([first, second], axis=1).reshape(Y, X * Z * C * rows // Y, depth)
-    part = lax.all_to_all(part, "y", 0, 0, tiled=True)
-    part = jnp.sum(part.astype(F32), axis=0).astype(BF)
-    part = (part.astype(F32) + swap(part, "w").astype(F32)).astype(BF)
-    grad_states = gather(part, "y", Y).reshape(X * Z * C * rows, depth)
-
-    split = states.reshape(X * Z, C, rows, depth)
-    states_own = lax.dynamic_index_in_dim(split, core, 1, keepdims=False).reshape(-1, depth)
-    states_other = lax.dynamic_index_in_dim(split, 1 - core, 1, keepdims=False).reshape(-1, depth)
-    grad_weight = dot(states_own, grads_own, ((0,), (0,))) + dot(states_other, grads_other, ((0,), (0,)))
-    return grad_states, grad_weight
+    where = jnp.stack([mine, core, lax.axis_index("y")]).astype(jnp.int32)
+    pieces = (where, dq_own, dq_other, dkv_own, dkv_other)
+    parts = local_call(project_kernel, Y, (Z, C, rows, depth), BF, *pieces, weight)
+    part = parts[0].astype(F32)
+    for k in range(1, Y):
+        part = part + swap(parts[k], "y", Y, k).astype(F32)
+    part = part.astype(BF)
+    part = (part.astype(F32) + swap(part, "w").astype(F32)).astype(BF).reshape(Z * C * rows, depth)
+    shares = [part] + [swap(part, "y", Y, k) for k in range(1, Y)]
+    (grad_states,) = local_call(place_kernel, 1, (Y,) + part.shape, BF, where, *shares)
+    (grad_weight,) = local_call(
+        weight_kernel, 1, (depth, columns), F32, *pieces, states.reshape(X, Z, C, rows, depth)
+    )
+    return grad_states.reshape(-1, depth), grad_weight
 
 
 def solution(mesh):
-    fine = Mesh(mesh.devices.reshape(X, Z, C, W, Y), ("x", "z", "c", "w", "y"))
-    ctx, tp = ("x", "z", "c"), ("w", "y")
+    fine = Mesh(mesh.devices.reshape(X, 2, Z // 2, C, W, Y), ("x", "h", "l", "c", "w", "y"))
+    ctx, tp = ("x", "h", "l", "c"), ("w", "y")
     return jax.shard_map(
         body,
         mesh=fine,

time: 279 us -> 254 us (0.910)
  the two profiles are of different devices: /device:TPU:2 before, /device:TPU:32 now
where the time goes in v2:
time: 254 us; the launch traced here: 253 us
  waiting for transfers between devices  77.5 us (31%)
  starting transfers between devices  75.9 us (30%)
  blocking collectives  72.7 us (29%)
  Pallas kernels  15.9 us (6%)
  local copies, waits for them, and re-layouts  6.66 us (3%)
  other arithmetic  3.64 us (1%)
    ppermute x18, waiting for transfers between devices, swap(): return lax.ppermute(x, axis, [(n, n ^ bit) for n in range(size)])  70.8 us
    all_to_all x3, blocking collectives, gather(): return lax.all_to_all(copies, axis, 0, 0, tiled=True)  62.1 us
    ppermute x18, starting transfers between devices, swap(): return lax.ppermute(x, axis, [(n, n ^ bit) for n in range(size)])  61.5 us
    all_to_all x2, starting transfers between devices, gather(): return lax.all_to_all(copies, axis, 0, 0, tiled=True)  14.4 us
    all_to_all x1, blocking collectives, body(): lax.all_to_all(dkv.reshape(2, Z // 2, rows, pair), 'l', 1, 1, tiled=True)  10.6 us
    pallas_call x3, Pallas kernels, local_call(): pl.pallas_call(kernel, out_shape=[jax.ShapeDtypeStruct(shape, dtype)] * c...  8.92 us
    pallas_call x1, Pallas kernels, attention(): pl.pallas_call(attention_kernel, out_shape=(jax.ShapeDtypeStruct((rows, H...  6.95 us
    all_to_all x2, waiting for transfers between devices, gather(): return lax.all_to_all(copies, axis, 0, 0, tiled=True)  6.65 us
  transfers between devices with their start and end apart: 20, of which 11 were waited for; matrix products, arithmetic and copies ran while one was open for 3% of the time, Pallas kernels for 1%

profile of v2, /device:TPU:32, one launch (start us, length us, event | category | flops | bytes accessed | tf_op | source)
XLA Modules:
  0.0 253.3 jit_solution(6270066485525525837)
XLA Ops:
  1.4 28.7 %all_to_all.30 = bf16[8,64,256]{2,1,0:T(8,128)(2,1)S(1)} all-to-all(bf16[8,64,256]{2,1,0:T(8,128)(2,1)S(1)} %broadcast_in_dim.16), channel_id=1, replica_groups=mesh['x'=4,'h'=2,'l'=4,'c'=2,'w'=2,'y'=4] {'h','l'}, dimensions={0} | all-to-all | bytes 524288 | tf_op jit(solution)/shard_map/all_to_all | solution.py:148
  30.3 15.0 %all_to_all.31 = bf16[4,8,64,256]{3,2,1,0:T(8,128)(2,1)S(1)} all-to-all(bf16[4,8,64,256]{3,2,1,0:T(8,128)(2,1)S(1)} %broadcast_in_dim.17), channel_id=1, replica_groups=mesh['x'=4,'h'=2,'l'=4,'c'=2,'w'=2,'y'=4] {'x'}, dimensions={0} | all-to-all | bytes 2097152 | tf_op jit(solution)/shard_map/all_to_all | solution.py:148
  50.4 6.9 %shard_map.68 = (bf16[256,128]{1,0:T(8,128)(2,1)S(1)}, bf16[2048,256]{1,0:T(8,128)(2,1)S(1)}, bf16[2048,256]{1,0:T(8,128)(2,1)}) custom-call(bf16[256,128]{1,0:T(8,128)(2,1)S(1)} %reshape.70.q_ref, bf16[256,128]{1,0:T(8,128)(2,1)S(1)} %reshape.71.g_ref, bf16[2048,256]{1,0:T(8,128)(2,1)S(1)} %bitcast.29, bf16[2048,256]{1,0:T(8,128)(2,1)} %collective-permute-done.other_ref, ...), custom_call_target="tpu_custom_call" | custom-call | tf_op jit(solution)/shard_map/pallas_call | solution.py:84
  61.8 9.3 %all-to-all-start.2 = ((bf16[8,64,512]{2,1,0:T(8,128)(2,1)}), bf16[8,64,512]{2,1,0:T(8,128)(2,1)S(1)}, u32[]{:S(2)}, u32[]{:S(2)}) async-start(bf16[8,64,512]{2,1,0:T(8,128)(2,1)} %broadcast_in_dim.20), calls=%async_computation.2 | async-start | bytes 1048576 | tf_op jit(solution)/shard_map/all_to_all | solution.py:148
  77.8 4.6 %collective-permute-start.3 = (bf16[512,256]{1,0:T(8,128)(2,1)S(1)}, bf16[512,256]{1,0:T(8,128)(2,1)S(1)}, u32[]{:S(2)}, u32[]{:S(2)}) collective-permute-start(bf16[512,256]{1,0:T(8,128)(2,1)S(1)} %get-tuple-element.22), channel_id=1, source_target_pairs={{0,256},{128,384},{256,0},{384,128},{1,257},{129,385},{257,1},{385... | collective-permute-start | bytes 786440 | tf_op jit(solution)/shard_map/ppermute | solution.py:152
  82.5 8.7 %collective-permute-done.4 = bf16[512,256]{1,0:T(8,128)(2,1)S(1)} collective-permute-done((bf16[512,256]{1,0:T(8,128)(2,1)S(1)}, bf16[512,256]{1,0:T(8,128)(2,1)S(1)}, u32[]{:S(2)}, u32[]{:S(2)}) %collective-permute-start.4) | collective-permute-done | bytes 262176 | tf_op jit(solution)/shard_map/ppermute | solution.py:152
  91.3 6.6 %all-to-all-done.2 = bf16[8,64,512]{2,1,0:T(8,128)(2,1)S(1)} async-done(((bf16[8,64,512]{2,1,0:T(8,128)(2,1)}), bf16[8,64,512]{2,1,0:T(8,128)(2,1)S(1)}, u32[]{:S(2)}, u32[]{:S(2)}) %all-to-all-start.2) | async-done | bytes 524320 | tf_op jit(solution)/shard_map/all_to_all | solution.py:148
  98.0 10.6 %all_to_all.32 = bf16[2,4,64,256]{3,2,0,1:T(8,128)(2,1)S(1)} all-to-all(bf16[2,4,64,256]{3,2,0,1:T(8,128)(2,1)S(1)} %copy.14), channel_id=1, replica_groups=mesh['x'=4,'h'=2,'l'=4,'c'=2,'w'=2,'y'=4] {'l'}, dimensions={1} | all-to-all | bytes 524288 | tf_op jit(solution)/shard_map/all_to_all | solution.py:190
  108.6 4.8 %collective-permute-start.9 = (bf16[2,64,256]{2,1,0:T(8,128)(2,1)S(1)}, bf16[2,64,256]{2,1,0:T(8,128)(2,1)S(1)}, u32[]{:S(2)}, u32[]{:S(2)}) collective-permute-start(bf16[2,64,256]{2,1,0:T(8,128)(2,1)S(1)} %reduce_sum.12), channel_id=1, source_target_pairs={{0,64},{64,0},{1,65},{65,1},{2,66},{66,2},{3,67},{67,3},{4,68},{68... | collective-permute-start | bytes 196616 | tf_op jit(solution)/shard_map/ppermute | solution.py:152
  116.6 3.4 %collective-permute-start.6 = (bf16[512,512]{1,0:T(8,128)(2,1)S(1)}, bf16[512,512]{1,0:T(8,128)(2,1)}, u32[]{:S(2)}, u32[]{:S(2)}) collective-permute-start(bf16[512,512]{1,0:T(8,128)(2,1)S(1)} %bitcast.38), channel_id=1, source_target_pairs={{0,256},{128,384},{256,0},{384,128},{1,257},{129,385},{257,1},{385... | collective-permute-start | bytes 1572872 | tf_op jit(solution)/shard_map/ppermute | solution.py:152
  119.9 3.4 %collective-permute-start.5 = (bf16[512,512]{1,0:T(8,128)(2,1)S(1)}, bf16[512,512]{1,0:T(8,128)(2,1)}, u32[]{:S(2)}, u32[]{:S(2)}) collective-permute-start(bf16[512,512]{1,0:T(8,128)(2,1)S(1)} %bitcast.39), channel_id=1, source_target_pairs={{0,128},{128,0},{256,384},{384,256},{1,129},{129,1},{257,385},{385... | collective-permute-start | bytes 1572872 | tf_op jit(solution)/shard_map/ppermute | solution.py:152
  124.1 5.2 %all-to-all-start.4 = ((bf16[4,2,64,256]{3,2,1,0:T(8,128)(2,1)}), bf16[4,2,64,256]{3,2,1,0:T(8,128)(2,1)S(1)}, u32[]{:S(2)}, u32[]{:S(2)}) async-start(bf16[4,2,64,256]{3,2,1,0:T(8,128)(2,1)} %broadcast_in_dim.21), calls=%async_computation.4 | async-start | bytes 524288 | tf_op jit(solution)/shard_map/all_to_all | solution.py:148
  129.3 10.1 %collective-permute-done.7 = bf16[512,512]{1,0:T(8,128)(2,1)S(1)} collective-permute-done((bf16[512,512]{1,0:T(8,128)(2,1)S(1)}, bf16[512,512]{1,0:T(8,128)(2,1)S(1)}, u32[]{:S(2)}, u32[]{:S(2)}) %collective-permute-start.7) | collective-permute-done | bytes 524320 | tf_op jit(solution)/shard_map/ppermute | solution.py:152
  145.7 18.5 %all_to_all.33.dkv_own_ref = bf16[4,512,256]{2,1,0:T(8,128)(2,1)S(1)} all-to-all(bf16[4,512,256]{2,1,0:T(8,128)(2,1)S(1)} %broadcast_in_dim.45), channel_id=1, replica_groups=mesh['x'=4,'h'=2,'l'=4,'c'=2,'w'=2,'y'=4] {'x'}, dimensions={0} | all-to-all | bytes 2097152 | tf_op jit(solution)/shard_map/all_to_all | solution.py:148
  168.8 3.7 %shard_map.69 = (bf16[8,2,64,128]{3,2,1,0:T(8,128)(2,1)S(1)}, bf16[8,2,64,128]{3,2,1,0:T(8,128)(2,1)S(1)}, bf16[8,2,64,128]{3,2,1,0:T(8,128)(2,1)S(1)}, bf16[8,2,64,128]{3,2,1,0:T(8,128)(2,1)S(1)}) custom-call(s32[3]{0:T(128)S(1)} %pad_add_fusion.at_ref, bf16[4,512,512]{2,1,0:T(8,128)(2,1)S(1)} %pad_maximum_fusion.dq_own_ref, ...), custom_call_target="tpu_custom_call" | custom-call | tf_op jit(solution)/shard_map/pallas_call | solution.py:137
  172.5 3.6 %collective-permute-start.11 = (bf16[8,2,64,128]{3,2,1,0:T(8,128)(2,1)S(1)}, bf16[8,2,64,128]{3,2,1,0:T(8,128)(2,1)S(1)}, u32[]{:S(2)}, u32[]{:S(2)}) collective-permute-start(bf16[8,2,64,128]{3,2,1,0:T(8,128)(2,1)S(1)} %get-tuple-element.17), channel_id=1, source_target_pairs={{0,1},{1,0},{2,3},{3,2},{4,5},{5,4},{6,7},{7,6},{8,9},{9,8},{10,11... | collective-permute-start | bytes 786440 | tf_op jit(solution)/shard_map/ppermute | solution.py:152
  176.1 4.8 %collective-permute-start.12 = (bf16[8,2,64,128]{3,2,1,0:T(8,128)(2,1)S(1)}, bf16[8,2,64,128]{3,2,1,0:T(8,128)(2,1)S(1)}, u32[]{:S(2)}, u32[]{:S(2)}) collective-permute-start(bf16[8,2,64,128]{3,2,1,0:T(8,128)(2,1)S(1)} %get-tuple-element.18), channel_id=1, source_target_pairs={{0,2},{1,3},{2,0},{3,1},{4,6},{5,7},{6,4},{7,5},{8,10},{9,11},{10,... | collective-permute-start | bytes 786440 | tf_op jit(solution)/shard_map/ppermute | solution.py:152
  183.7 7.4 %collective-permute-done.12 = bf16[8,2,64,128]{3,2,1,0:T(8,128)(2,1)S(1)} collective-permute-done((bf16[8,2,64,128]{3,2,1,0:T(8,128)(2,1)S(1)}, bf16[8,2,64,128]{3,2,1,0:T(8,128)(2,1)S(1)}, u32[]{:S(2)}, u32[]{:S(2)}) %collective-permute-start.12) | collective-permute-done | bytes 262176 | tf_op jit(solution)/shard_map/ppermute | solution.py:152
  191.0 5.5 %collective-permute-done.13 = bf16[8,2,64,128]{3,2,1,0:T(8,128)(2,1)S(1)} collective-permute-done((bf16[8,2,64,128]{3,2,1,0:T(8,128)(2,1)S(1)}, bf16[8,2,64,128]{3,2,1,0:T(8,128)(2,1)S(1)}, u32[]{:S(2)}, u32[]{:S(2)}) %collective-permute-start.13) | collective-permute-done | bytes 262176 | tf_op jit(solution)/shard_map/ppermute | solution.py:152
  196.7 8.2 %collective-permute-start.14 = (bf16[8,2,64,128]{3,2,1,0:T(8,128)(2,1)S(1)}, bf16[8,2,64,128]{3,2,1,0:T(8,128)(2,1)S(1)}, u32[]{:S(2)}, u32[]{:S(2)}) collective-permute-start(bf16[8,2,64,128]{3,2,1,0:T(8,128)(2,1)S(1)} %add_convert_fusion.2), channel_id=1, source_target_pairs={{0,4},{4,0},{1,5},{5,1},{2,6},{6,2},{3,7},{7,3},{8,12},{12,8},{9,1... | collective-permute-start | bytes 786440 | tf_op jit(solution)/shard_map/ppermute | solution.py:152
  204.9 27.6 %collective-permute-done.14 = bf16[8,2,64,128]{3,2,1,0:T(8,128)(2,1)S(1)} collective-permute-done((bf16[8,2,64,128]{3,2,1,0:T(8,128)(2,1)S(1)}, bf16[8,2,64,128]{3,2,1,0:T(8,128)(2,1)S(1)}, u32[]{:S(2)}, u32[]{:S(2)}) %collective-permute-start.14) | collective-permute-done | bytes 262176 | tf_op jit(solution)/shard_map/ppermute | solution.py:152
  237.5 5.0 %collective-permute-start.15 = (bf16[1024,128]{1,0:T(8,128)(2,1)S(1)}, bf16[1024,128]{1,0:T(8,128)(2,1)S(1)}, u32[]{:S(2)}, u32[]{:S(2)}) collective-permute-start(bf16[1024,128]{1,0:T(8,128)(2,1)S(1)} %bitcast.32), channel_id=1, source_target_pairs={{0,1},{1,0},{2,3},{3,2},{4,5},{5,4},{6,7},{7,6},{8,9},{9,8},{10,11... | collective-permute-start | bytes 786440 | tf_op jit(solution)/shard_map/ppermute | solution.py:152
  242.4 3.7 %shard_map.71 = f32[128,768]{1,0:T(8,128)} custom-call(s32[3]{0:T(128)S(1)} %pad_add_fusion.at_ref, bf16[4,512,512]{2,1,0:T(8,128)(2,1)S(1)} %pad_maximum_fusion.dq_own_ref, bf16[4,512,512]{2,1,0:T(8,128)(2,1)} %collective-permute-done.8.dq_other_ref, bf16[4,512,256]{2,1,0:T(8,128)(2,1)S(1)} %all_to_all.33.dkv_own_ref, ...), custom_call_target="tpu_custom_call" | custom-call | tf_op jit(solution)/shard_map/pallas_call | solution.py:137
  246.1 3.1 %collective-permute-done.17.refs_3_ = bf16[1024,128]{1,0:T(8,128)(2,1)S(1)} collective-permute-done((bf16[1024,128]{1,0:T(8,128)(2,1)S(1)}, bf16[1024,128]{1,0:T(8,128)(2,1)S(1)}, u32[]{:S(2)}, u32[]{:S(2)}) %collective-permute-start.17) | collective-permute-done | bytes 262176 | tf_op jit(solution)/shard_map/ppermute | solution.py:152
  (70 shorter events, 44.0 us)
Async XLA Ops:
  1.4 45.8 %copy-start.5 = (s32[128]{0:T(128)S(1)}, s32[128]{0:T(128)}, u32[]{:S(2)}) copy-start(s32[128]{0:T(128)} %param.9) | copy-start | bytes 1540
  30.1 18.0 %slice-start = ((bf16[64,768]{1,0:T(8,128)(2,1)}), bf16[64,512]{1,0:T(8,128)(2,1)S(1)}, s32[]{:S(2)}) async-start(bf16[64,768]{1,0:T(8,128)(2,1)} %param.6), calls=%async_computation.6 | async-start | bytes 131072 | tf_op jit(solution)/shard_map/slice | solution.py:175
  45.2 5.2 %collective-permute-start = (bf16[2048,256]{1,0:T(8,128)(2,1)S(1)}, bf16[2048,256]{1,0:T(8,128)(2,1)}, u32[]{:S(2)}, u32[]{:S(2)}) collective-permute-start(bf16[2048,256]{1,0:T(8,128)(2,1)S(1)} %bitcast.28), channel_id=1, source_target_pairs={{0,8},{8,0},{1,9},{9,1},{2,10},{10,2},{3,11},{11,3},{4,12},{12,4},... | collective-permute-start | bytes 3145736 | tf_op jit(solution)/shard_map/ppermute | solution.py:152
  58.3 12.7 %collective-permute-start.1 = (bf16[2048,256]{1,0:T(8,128)(2,1)}, bf16[2048,256]{1,0:T(8,128)(2,1)}, u32[]{:S(2)}, u32[]{:S(2)}) collective-permute-start(bf16[2048,256]{1,0:T(8,128)(2,1)} %get-tuple-element.12), channel_id=1, source_target_pairs={{0,8},{8,0},{1,9},{9,1},{2,10},{10,2},{3,11},{11,3},{4,12},{12,4},... | collective-permute-start | bytes 3145736 | tf_op jit(solution)/shard_map/ppermute | solution.py:152
  61.8 36.2 %all-to-all-start.2 = ((bf16[8,64,512]{2,1,0:T(8,128)(2,1)}), bf16[8,64,512]{2,1,0:T(8,128)(2,1)S(1)}, u32[]{:S(2)}, u32[]{:S(2)}) async-start(bf16[8,64,512]{2,1,0:T(8,128)(2,1)} %broadcast_in_dim.20), calls=%async_computation.2 | async-start | bytes 1048576 | tf_op jit(solution)/shard_map/all_to_all | solution.py:148
  72.6 9.8 %collective-permute-start.2 = (bf16[512,256]{1,0:T(8,128)(2,1)S(1)}, bf16[512,256]{1,0:T(8,128)(2,1)S(1)}, u32[]{:S(2)}, u32[]{:S(2)}) collective-permute-start(bf16[512,256]{1,0:T(8,128)(2,1)S(1)} %get-tuple-element.20), channel_id=1, source_target_pairs={{0,128},{128,0},{256,384},{384,256},{1,129},{129,1},{257,385},{385... | collective-permute-start | bytes 786440 | tf_op jit(solution)/shard_map/ppermute | solution.py:152
  75.1 16.1 %collective-permute-start.4 = (bf16[512,256]{1,0:T(8,128)(2,1)S(1)}, bf16[512,256]{1,0:T(8,128)(2,1)S(1)}, u32[]{:S(2)}, u32[]{:S(2)}) collective-permute-start(bf16[512,256]{1,0:T(8,128)(2,1)S(1)} %get-tuple-element.21), channel_id=1, source_target_pairs={{0,384},{128,256},{256,128},{384,0},{1,385},{129,257},{257,129},{3... | collective-permute-start | bytes 786440 | tf_op jit(solution)/shard_map/ppermute | solution.py:152
  77.8 13.4 %collective-permute-start.3 = (bf16[512,256]{1,0:T(8,128)(2,1)S(1)}, bf16[512,256]{1,0:T(8,128)(2,1)S(1)}, u32[]{:S(2)}, u32[]{:S(2)}) collective-permute-start(bf16[512,256]{1,0:T(8,128)(2,1)S(1)} %get-tuple-element.22), channel_id=1, source_target_pairs={{0,256},{128,384},{256,0},{384,128},{1,257},{129,385},{257,1},{385... | collective-permute-start | bytes 786440 | tf_op jit(solution)/shard_map/ppermute | solution.py:152
  108.6 14.7 %collective-permute-start.9 = (bf16[2,64,256]{2,1,0:T(8,128)(2,1)S(1)}, bf16[2,64,256]{2,1,0:T(8,128)(2,1)S(1)}, u32[]{:S(2)}, u32[]{:S(2)}) collective-permute-start(bf16[2,64,256]{2,1,0:T(8,128)(2,1)S(1)} %reduce_sum.12), channel_id=1, source_target_pairs={{0,64},{64,0},{1,65},{65,1},{2,66},{66,2},{3,67},{67,3},{4,68},{68... | collective-permute-start | bytes 196616 | tf_op jit(solution)/shard_map/ppermute | solution.py:152
  113.5 25.9 %collective-permute-start.7 = (bf16[512,512]{1,0:T(8,128)(2,1)S(1)}, bf16[512,512]{1,0:T(8,128)(2,1)S(1)}, u32[]{:S(2)}, u32[]{:S(2)}) collective-permute-start(bf16[512,512]{1,0:T(8,128)(2,1)S(1)} %bitcast.37), channel_id=1, source_target_pairs={{0,384},{128,256},{256,128},{384,0},{1,385},{129,257},{257,129},{3... | collective-permute-start | bytes 1572872 | tf_op jit(solution)/shard_map/ppermute | solution.py:152
  116.6 22.8 %collective-permute-start.6 = (bf16[512,512]{1,0:T(8,128)(2,1)S(1)}, bf16[512,512]{1,0:T(8,128)(2,1)}, u32[]{:S(2)}, u32[]{:S(2)}) collective-permute-start(bf16[512,512]{1,0:T(8,128)(2,1)S(1)} %bitcast.38), channel_id=1, source_target_pairs={{0,256},{128,384},{256,0},{384,128},{1,257},{129,385},{257,1},{385... | collective-permute-start | bytes 1572872 | tf_op jit(solution)/shard_map/ppermute | solution.py:152
  119.9 22.1 %collective-permute-start.5 = (bf16[512,512]{1,0:T(8,128)(2,1)S(1)}, bf16[512,512]{1,0:T(8,128)(2,1)}, u32[]{:S(2)}, u32[]{:S(2)}) collective-permute-start(bf16[512,512]{1,0:T(8,128)(2,1)S(1)} %bitcast.39), channel_id=1, source_target_pairs={{0,128},{128,0},{256,384},{384,256},{1,129},{129,1},{257,385},{385... | collective-permute-start | bytes 1572872 | tf_op jit(solution)/shard_map/ppermute | solution.py:152
  124.1 21.5 %all-to-all-start.4 = ((bf16[4,2,64,256]{3,2,1,0:T(8,128)(2,1)}), bf16[4,2,64,256]{3,2,1,0:T(8,128)(2,1)S(1)}, u32[]{:S(2)}, u32[]{:S(2)}) async-start(bf16[4,2,64,256]{3,2,1,0:T(8,128)(2,1)} %broadcast_in_dim.21), calls=%async_computation.4 | async-start | bytes 524288 | tf_op jit(solution)/shard_map/all_to_all | solution.py:148
  143.5 25.3 %copy-start.3 = (bf16[128,768]{1,0:T(8,128)(2,1)S(1)}, bf16[128,768]{1,0:T(8,128)(2,1)}, u32[]{:S(2)}) copy-start(bf16[128,768]{1,0:T(8,128)(2,1)} %weight_ref.1) | copy-start | bytes 589828
  143.5 22.6 %collective-permute-start.8 = (bf16[4,512,512]{2,1,0:T(8,128)(2,1)S(1)}, bf16[4,512,512]{2,1,0:T(8,128)(2,1)}, u32[]{:S(2)}, u32[]{:S(2)}) collective-permute-start(bf16[4,512,512]{2,1,0:T(8,128)(2,1)S(1)} %pad_maximum_fusion.dq_own_ref), channel_id=1, source_target_pairs={{0,8},{8,0},{1,9},{9,1},{2,10},{10,2},{3,11},{11,3},{4,12},{12,4},... | collective-permute-start | bytes 6291464 | tf_op jit(solution)/shard_map/ppermute | solution.py:152
  164.1 4.7 %collective-permute-start.10 = (bf16[4,512,256]{2,1,0:T(8,128)(2,1)S(1)}, bf16[4,512,256]{2,1,0:T(8,128)(2,1)}, u32[]{:S(2)}, u32[]{:S(2)}) collective-permute-start(bf16[4,512,256]{2,1,0:T(8,128)(2,1)S(1)} %all_to_all.33.dkv_own_ref), channel_id=1, source_target_pairs={{0,8},{8,0},{1,9},{9,1},{2,10},{10,2},{3,11},{11,3},{4,12},{12,4},... | collective-permute-start | bytes 3145736 | tf_op jit(solution)/shard_map/ppermute | solution.py:152
  172.5 70.0 %copy-start.2 = (bf16[4096,128]{1,0:T(8,128)(2,1)S(1)}, bf16[4096,128]{1,0:T(8,128)(2,1)}, u32[]{:S(2)}) copy-start(bf16[4096,128]{1,0:T(8,128)(2,1)} %param.5) | copy-start | bytes 3145732
  172.5 11.2 %collective-permute-start.11 = (bf16[8,2,64,128]{3,2,1,0:T(8,128)(2,1)S(1)}, bf16[8,2,64,128]{3,2,1,0:T(8,128)(2,1)S(1)}, u32[]{:S(2)}, u32[]{:S(2)}) collective-permute-start(bf16[8,2,64,128]{3,2,1,0:T(8,128)(2,1)S(1)} %get-tuple-element.17), channel_id=1, source_target_pairs={{0,1},{1,0},{2,3},{3,2},{4,5},{5,4},{6,7},{7,6},{8,9},{9,8},{10,11... | collective-permute-start | bytes 786440 | tf_op jit(solution)/shard_map/ppermute | solution.py:152
  176.1 14.9 %collective-permute-start.12 = (bf16[8,2,64,128]{3,2,1,0:T(8,128)(2,1)S(1)}, bf16[8,2,64,128]{3,2,1,0:T(8,128)(2,1)S(1)}, u32[]{:S(2)}, u32[]{:S(2)}) collective-permute-start(bf16[8,2,64,128]{3,2,1,0:T(8,128)(2,1)S(1)} %get-tuple-element.18), channel_id=1, source_target_pairs={{0,2},{1,3},{2,0},{3,1},{4,6},{5,7},{6,4},{7,5},{8,10},{9,11},{10,... | collective-permute-start | bytes 786440 | tf_op jit(solution)/shard_map/ppermute | solution.py:152
  180.9 15.6 %collective-permute-start.13 = (bf16[8,2,64,128]{3,2,1,0:T(8,128)(2,1)S(1)}, bf16[8,2,64,128]{3,2,1,0:T(8,128)(2,1)S(1)}, u32[]{:S(2)}, u32[]{:S(2)}) collective-permute-start(bf16[8,2,64,128]{3,2,1,0:T(8,128)(2,1)S(1)} %get-tuple-element.19), channel_id=1, source_target_pairs={{0,3},{1,2},{2,1},{3,0},{4,7},{5,6},{6,5},{7,4},{8,11},{9,10},{10,... | collective-permute-start | bytes 786440 | tf_op jit(solution)/shard_map/ppermute | solution.py:152
  196.7 35.8 %collective-permute-start.14 = (bf16[8,2,64,128]{3,2,1,0:T(8,128)(2,1)S(1)}, bf16[8,2,64,128]{3,2,1,0:T(8,128)(2,1)S(1)}, u32[]{:S(2)}, u32[]{:S(2)}) collective-permute-start(bf16[8,2,64,128]{3,2,1,0:T(8,128)(2,1)S(1)} %add_convert_fusion.2), channel_id=1, source_target_pairs={{0,4},{4,0},{1,5},{5,1},{2,6},{6,2},{3,7},{7,3},{8,12},{12,8},{9,1... | collective-permute-start | bytes 786440 | tf_op jit(solution)/shard_map/ppermute | solution.py:152
  232.6 16.6 %collective-permute-start.17 = (bf16[1024,128]{1,0:T(8,128)(2,1)S(1)}, bf16[1024,128]{1,0:T(8,128)(2,1)S(1)}, u32[]{:S(2)}, u32[]{:S(2)}) collective-permute-start(bf16[1024,128]{1,0:T(8,128)(2,1)S(1)} %bitcast.30), channel_id=1, source_target_pairs={{0,3},{1,2},{2,1},{3,0},{4,7},{5,6},{6,5},{7,4},{8,11},{9,10},{10,... | collective-permute-start | bytes 786440 | tf_op jit(solution)/shard_map/ppermute | solution.py:152
  234.7 14.5 %collective-permute-start.16 = (bf16[1024,128]{1,0:T(8,128)(2,1)S(1)}, bf16[1024,128]{1,0:T(8,128)(2,1)S(1)}, u32[]{:S(2)}, u32[]{:S(2)}) collective-permute-start(bf16[1024,128]{1,0:T(8,128)(2,1)S(1)} %bitcast.31), channel_id=1, source_target_pairs={{0,2},{1,3},{2,0},{3,1},{4,6},{5,7},{6,4},{7,5},{8,10},{9,11},{10,... | collective-permute-start | bytes 786440 | tf_op jit(solution)/shard_map/ppermute | solution.py:152
  237.5 14.3 %collective-permute-start.15 = (bf16[1024,128]{1,0:T(8,128)(2,1)S(1)}, bf16[1024,128]{1,0:T(8,128)(2,1)S(1)}, u32[]{:S(2)}, u32[]{:S(2)}) collective-permute-start(bf16[1024,128]{1,0:T(8,128)(2,1)S(1)} %bitcast.32), channel_id=1, source_target_pairs={{0,1},{1,0},{2,3},{3,2},{4,5},{5,4},{6,7},{7,6},{8,9},{9,8},{10,11... | collective-permute-start | bytes 786440 | tf_op jit(solution)/shard_map/ppermute | solution.py:152
  (3 other events, 31.6 us)

commit v3 on v0

v3 whole, which is shorter than its diff:
```python
import functools

import jax
import jax.numpy as jnp
from jax import lax
from jax.experimental import pallas as pl
from jax.experimental.pallas import tpu as pltpu
from jax.sharding import Mesh
from jax.sharding import PartitionSpec as P

HEADS = 32
KV_HEADS = 8
HEAD_DIM = 128
GROUP = HEADS // KV_HEADS
X, Z, C, W, Y = 4, 8, 2, 2, 4
LOWEST = -1e30
BF = jnp.bfloat16
F32 = jnp.float32


def dot(a, b, contract):
    return lax.dot_general(a, b, (contract, ((), ())), preferred_element_type=F32)


def heads_to_rows(ref, start):
    return jnp.concatenate([ref[:, start + n * HEAD_DIM : start + (n + 1) * HEAD_DIM] for n in range(GROUP)], axis=0)


def masked_scores(keys, q, kpos, qpos):
    scores = dot(keys, q, ((1,), (1,))) * HEAD_DIM ** (-0.5)
    return jnp.where(kpos <= qpos, scores, -jnp.inf)


def stats_kernel(own_ref, other_ref, kpos_ref, qpos_ref, *refs):
    out_ref = refs[X]
    wide = GROUP * HEAD_DIM
    half = own_ref.shape[0]
    for k in range(X):
        q = heads_to_rows(refs[k], 0)
        g = heads_to_rows(refs[k], wide)
        qpos = qpos_ref[k : k + 1, :]
        scores = [
            masked_scores(kv_ref[:, :HEAD_DIM], q, kpos_ref[side * half : (side + 1) * half, :], qpos)
            for side, kv_ref in enumerate((own_ref, other_ref))
        ]
        top = jnp.full(qpos.shape, LOWEST, F32)
        for part in scores:
            top = jnp.maximum(top, jnp.max(part, axis=0, keepdims=True))
        total = jnp.zeros(qpos.shape, F32)
        weighted = jnp.zeros(qpos.shape, F32)
        for part, kv_ref in zip(scores, (own_ref, other_ref)):
            expd = jnp.exp(part - top)
            total = total + jnp.sum(expd, axis=0, keepdims=True)
            dprob = dot(kv_ref[:, HEAD_DIM:], g, ((1,), (1,)))
            weighted = weighted + jnp.sum(expd * dprob, axis=0, keepdims=True)
        for n in range(X):
            out_ref[n, k : k + 1, :] = top
            out_ref[n, X + k : X + k + 1, :] = total
            out_ref[n, 2 * X + k : 2 * X + k + 1, :] = weighted
    for n in range(X):
        out_ref[n, 3 * X :, :] = jnp.zeros((X, out_ref.shape[2]), F32)


def grads_kernel(at_ref, stats_ref, own_ref, other_ref, kpos_ref, qpos_ref, *refs):
    qg_refs, dq_ref = refs[:X], refs[X]
    dkv_refs = refs[X + 1 : X + 3]
    dkv_sum_ref = refs[X + 3]
    mine = at_ref[0]
    scale = HEAD_DIM ** (-0.5)
    wide = GROUP * HEAD_DIM
    half, rows = own_ref.shape[0], dq_ref.shape[1]
    for k in range(X):
        stat = [[stats_ref[mine ^ d, n * X + (d ^ k) : n * X + (d ^ k) + 1, :] for n in range(3)] for d in range(X)]
        top = functools.reduce(jnp.maximum, [one[0] for one in stat])
        shift = [jnp.exp(one[0] - top) for one in stat]
        inverse = 1.0 / sum(one[1] * c for one, c in zip(stat, shift))
        delta = sum(one[2] * c for one, c in zip(stat, shift)) * inverse
        q = heads_to_rows(qg_refs[k], 0)
        g = heads_to_rows(qg_refs[k], wide)
        qpos = qpos_ref[k : k + 1, :]
        dquery = jnp.zeros((HEAD_DIM, q.shape[0]), F32)
        for side, kv_ref in enumerate((own_ref, other_ref)):
            keys = kv_ref[:, :HEAD_DIM]
            kpos = kpos_ref[side * half : (side + 1) * half, :]
            probs = jnp.exp(masked_scores(keys, q, kpos, qpos) - top) * inverse
            dprob = dot(kv_ref[:, HEAD_DIM:], g, ((1,), (1,)))
            dscore = (probs * (dprob - delta) * scale).astype(BF)
            dquery = dquery + dot(keys, dscore, ((0,), (0,)))
            dkey = dot(dscore, q, ((1,), (0,)))
            dvalue = dot(probs.astype(BF), g, ((1,), (0,)))
            if k > 0:
                dkey = dkey + dkv_sum_ref[side, :, :HEAD_DIM]
                dvalue = dvalue + dkv_sum_ref[side, :, HEAD_DIM:]
            if k < X - 1:
                dkv_sum_ref[side, :, :HEAD_DIM] = dkey
                dkv_sum_ref[side, :, HEAD_DIM:] = dvalue
            else:
                dkv_refs[side][:, :HEAD_DIM] = dkey.astype(BF)
                dkv_refs[side][:, HEAD_DIM:] = dvalue.astype(BF)
        dquery = dquery.T.astype(BF)
        for n in range(GROUP):
            dq_ref[mine ^ k, :, n * HEAD_DIM : (n + 1) * HEAD_DIM] = dquery[n * rows : (n + 1) * rows]


def attention_stats(own, other, kpos, qpos, qg, interpret=False):
    vmem = pl.BlockSpec(memory_space=pltpu.VMEM)
    return pl.pallas_call(
        stats_kernel,
        out_shape=jax.ShapeDtypeStruct((X, 4 * X, qpos.shape[1]), F32),
        in_specs=[vmem] * (4 + X),
        out_specs=vmem,
        compiler_params=pltpu.CompilerParams(vmem_limit_bytes=40 * 1024 * 1024),
        interpret=interpret,
    )(own, other, kpos, qpos, *qg)


def attention_grads(at, stats, own, other, kpos, qpos, qg, interpret=False):
    vmem = pl.BlockSpec(memory_space=pltpu.VMEM)
    dq_shape = jax.ShapeDtypeStruct((X, qg[0].shape[0], GROUP * HEAD_DIM), BF)
    return pl.pallas_call(
        grads_kernel,
        out_shape=[dq_shape] + [jax.ShapeDtypeStruct(own.shape, BF)] * 2,
        in_specs=[pl.BlockSpec(memory_space=pltpu.SMEM)] + [vmem] * (5 + X),
        out_specs=[vmem] * 3,
        scratch_shapes=[pltpu.VMEM((2,) + own.shape, F32)],
        compiler_params=pltpu.CompilerParams(vmem_limit_bytes=40 * 1024 * 1024),
        interpret=interpret,
    )(at, stats, own, other, kpos, qpos, *qg)


def project_kernel(at_ref, *refs):
    piece_refs, weight_ref, out_ref = refs[: 2 * X], refs[2 * X], refs[2 * X + 1]
    rows = out_ref.shape[3]
    for k in range(X):
        for side in range(C):
            part = dot(piece_refs[side * X + k][...], weight_ref[...], ((1,), (1,))).astype(BF)
            for n in range(Z):
                block = part[n * rows : (n + 1) * rows]
                out_ref[at_ref[0] ^ k, n % 2 * (Z // 2) + n // 2, at_ref[1] ^ side] = block


def weight_kernel(at_ref, *refs):
    piece_refs, states_ref, out_ref = refs[: 2 * X], refs[2 * X], refs[2 * X + 1]
    total = jnp.zeros(out_ref.shape, F32)
    for k in range(X):
        for side in range(C):
            place, core = at_ref[0] ^ k, at_ref[1] ^ side
            rows = [states_ref[place, n % 2 * (Z // 2) + n // 2, core] for n in range(Z)]
            total = total + dot(jnp.concatenate(rows, axis=0), piece_refs[side * X + k][...], ((0,), (0,)))
    out_ref[...] = total


def add_kernel(at_ref, mine_ref, other_ref, out_ref):
    total = (mine_ref[...].astype(F32) + other_ref[...].astype(F32)).astype(BF)
    for n in range(out_ref.shape[0]):
        out_ref[n] = total


def local_call(kernel, shape, dtype, *operands):
    vmem = pl.BlockSpec(memory_space=pltpu.VMEM)
    return pl.pallas_call(
        kernel,
        out_shape=jax.ShapeDtypeStruct(shape, dtype),
        in_specs=[pl.BlockSpec(memory_space=pltpu.SMEM)] + [vmem] * (len(operands) - 1),
        out_specs=vmem,
        compiler_params=pltpu.CompilerParams(vmem_limit_bytes=40 * 1024 * 1024),
    )(*operands)


def gather(x, axis, size):
    copies = jnp.broadcast_to(x[None], (size,) + x.shape)
    return lax.all_to_all(copies, axis, 0, 0, tiled=True)


def swap(x, axis, size=2, bit=1):
    return lax.ppermute(x, axis, [(n, n ^ bit) for n in range(size)])


def body(states, qkv, grad_out, weight, offsets):
    rows, columns = qkv.shape
    half = rows // 2
    wide = GROUP * HEAD_DIM
    pair = 2 * HEAD_DIM
    core = lax.axis_index("c")
    mine = lax.axis_index("x")
    high = lax.axis_index("h")
    deep = high * (Z // 2) + lax.axis_index("l")
    where = jnp.stack([mine, core]).astype(jnp.int32)
    slab = jnp.arange(half, dtype=jnp.int32)
    starts = offsets.reshape(X, Z, C, 2)
    row_start = lax.dynamic_index_in_dim(lax.dynamic_index_in_dim(starts, deep, 1, False), core, 1, False)
    row_start = jnp.stack([lax.dynamic_index_in_dim(row_start, mine ^ k, 0, False) for k in range(X)])
    query_pos = (row_start[:, :, None] + slab).reshape(X, rows)
    query_pos = jnp.tile(query_pos, (1, GROUP))
    key_start = lax.dynamic_index_in_dim(starts, mine, 0, False)
    key_start = jnp.stack([lax.dynamic_index_in_dim(key_start, core ^ k, 1, False) for k in range(C)])
    key_pos = (key_start.reshape(-1)[:, None] + slab[None, :]).reshape(-1, 1)

    qg = jnp.concatenate([qkv[:, :wide], grad_out], axis=1)
    pairs = qkv[:, wide:]
    qg, pairs, key_pos, query_pos = lax.optimization_barrier((qg, pairs, key_pos, query_pos))
    qg_x = [qg] + [swap(qg, "x", X, k) for k in range(1, X)]
    own = gather(pairs, ("h", "l"), Z).reshape(Z * rows, pair)
    own, *qg_x = lax.optimization_barrier((own, *qg_x))
    other = swap(own, "c")

    stats = attention_stats(own, other, key_pos, query_pos, qg_x)
    stats = lax.all_to_all(stats, "x", 0, 0, tiled=True)
    dq, dkv, dkv_give = attention_grads(where, stats, own, other, key_pos, query_pos, qg_x)

    dkv_in = swap(dkv_give, "c")
    dq = jnp.sum(lax.all_to_all(dq, "x", 0, 0, tiled=True).astype(F32), axis=0).astype(BF)
    dkv = (dkv.astype(F32) + dkv_in.astype(F32)).astype(BF)
    dkv, dq = lax.optimization_barrier((dkv, dq))
    dkv = lax.all_to_all(dkv.reshape(2, Z // 2, rows, pair), "l", 1, 1, tiled=True)
    dq_h = jnp.stack([dq, swap(dq, "h")])
    dq_h = jnp.where(high == 0, dq_h, dq_h[::-1])
    dkv = jnp.sum(dkv.astype(F32), axis=1).astype(BF)
    dkv, dq_h = lax.optimization_barrier((dkv, dq_h))
    dkv = (dkv.astype(F32) + swap(dkv, "h").astype(F32)).astype(BF)

    grads = gather(jnp.concatenate([dq_h, dkv], axis=2), "l", Z // 2).reshape(Z * rows, columns)
    pieces = [grads] + [swap(grads, "x", X, k) for k in range(1, X)]
    pieces = pieces + [swap(piece, "c") for piece in pieces]

    depth = weight.shape[0]
    part = local_call(project_kernel, (X, Z, C, rows, depth), BF, where, *pieces, weight)
    part = lax.all_to_all(part.reshape(Y, Z * C * rows, depth), "y", 0, 0, tiled=True)
    part = jnp.sum(part.astype(F32), axis=0).astype(BF)
    grad_weight = local_call(
        weight_kernel, (depth, columns), F32, where, *pieces, states.reshape(X, Z, C, rows, depth)
    )
    part = local_call(add_kernel, (Y,) + part.shape, BF, where, part, swap(part, "w"))
    part, grad_weight = lax.optimization_barrier((part, grad_weight))
    grad_states = lax.all_to_all(part, "y", 0, 0, tiled=True)
    return grad_states.reshape(-1, depth), grad_weight


def solution(mesh):
    fine = Mesh(mesh.devices.reshape(X, 2, Z // 2, C, W, Y), ("x", "h", "l", "c", "w", "y"))
    ctx, tp = ("x", "h", "l", "c"), ("w", "y")
    return jax.shard_map(
        body,
        mesh=fine,
        in_specs=(P(None, ctx), P(ctx, tp), P(ctx, tp), P(ctx, tp), P()),
        out_specs=(P(None, ctx), P(ctx, tp)),
        check_vma=False,
    )
```

time: 933 us -> 239 us (0.26)
  the two profiles are of different devices: /device:TPU:40 before, /device:TPU:160 now
where the time goes in v3:
time: 239 us; the launch traced here: 238 us
  blocking collectives  73.9 us (31%)
  waiting for transfers between devices  69.5 us (29%)
  starting transfers between devices  68.3 us (29%)
  Pallas kernels  12.2 us (5%)
  local copies, waits for them, and re-layouts  10.9 us (5%)
    ppermute x15, waiting for transfers between devices, swap(): return lax.ppermute(x, axis, [(n, n ^ bit) for n in range(size)])  63.9 us
    ppermute x15, starting transfers between devices, swap(): return lax.ppermute(x, axis, [(n, n ^ bit) for n in range(size)])  48.4 us
    all_to_all x1, blocking collectives, gather(): return lax.all_to_all(copies, axis, 0, 0, tiled=True)  26.2 us
    all_to_all x1, blocking collectives, body(): lax.all_to_all(part.reshape(Y, Z * C * rows, depth), 'y', 0, 0, tiled=True)  19.8 us
    all_to_all x1, blocking collectives, body(): grad_states = lax.all_to_all(part, 'y', 0, 0, tiled=True)  17.9 us
    all_to_all x1, starting transfers between devices, gather(): return lax.all_to_all(copies, axis, 0, 0, tiled=True)  10.8 us
    all_to_all x1, blocking collectives, body(): lax.all_to_all(dq, 'x', 0, 0, tiled=True).astype(F32)  10 us
    unnamed x25, local copies, waits for them, and re-layouts  7.35 us
  transfers between devices with their start and end apart: 18, of which 9 were waited for; matrix products, arithmetic and copies ran while one was open for 0% of the time, Pallas kernels for 1%

profile of v3, /device:TPU:160, one launch (start us, length us, event | category | flops | bytes accessed | tf_op | source)
XLA Modules:
  0.0 237.7 jit_solution(16715106637176863141)
XLA Ops:
  4.0 10.8 %all-to-all-start = ((bf16[8,64,256]{2,1,0:T(8,128)(2,1)}), bf16[8,64,256]{2,1,0:T(8,128)(2,1)S(1)}, u32[]{:S(2)}, u32[]{:S(2)}) async-start(bf16[8,64,256]{2,1,0:T(8,128)(2,1)} %broadcast_in_dim.4), calls=%async_computation | async-start | bytes 524288 | tf_op jit(solution)/shard_map/all_to_all | solution.py:172
  14.8 4.7 %collective-permute-start.2 = (bf16[64,1024]{1,0:T(8,128)(2,1)S(1)}, bf16[64,1024]{1,0:T(8,128)(2,1)S(1)}, u32[]{:S(2)}, u32[]{:S(2)}) collective-permute-start(bf16[64,1024]{1,0:T(8,128)(2,1)S(1)} %pad_maximum_fusion.1.refs_0_), channel_id=1, source_target_pairs={{0,384},{128,256},{256,128},{384,0},{1,385},{129,257},{257,129},{3... | collective-permute-start | bytes 393224 | tf_op jit(solution)/shard_map/ppermute | solution.py:176
  19.4 2.7 %collective-permute-start.1 = (bf16[64,1024]{1,0:T(8,128)(2,1)S(1)}, bf16[64,1024]{1,0:T(8,128)(2,1)S(1)}, u32[]{:S(2)}, u32[]{:S(2)}) collective-permute-start(bf16[64,1024]{1,0:T(8,128)(2,1)S(1)} %pad_maximum_fusion.1.refs_0_), channel_id=1, source_target_pairs={{0,256},{128,384},{256,0},{384,128},{1,257},{129,385},{257,1},{385... | collective-permute-start | bytes 393224 | tf_op jit(solution)/shard_map/ppermute | solution.py:176
  22.2 2.4 %collective-permute-start = (bf16[64,1024]{1,0:T(8,128)(2,1)S(1)}, bf16[64,1024]{1,0:T(8,128)(2,1)S(1)}, u32[]{:S(2)}, u32[]{:S(2)}) collective-permute-start(bf16[64,1024]{1,0:T(8,128)(2,1)S(1)} %pad_maximum_fusion.1.refs_0_), channel_id=1, source_target_pairs={{0,128},{128,0},{256,384},{384,256},{1,129},{129,1},{257,385},{385... | collective-permute-start | bytes 393224 | tf_op jit(solution)/shard_map/ppermute | solution.py:176
  24.6 4.2 %collective-permute-done.1.refs_2_ = bf16[64,1024]{1,0:T(8,128)(2,1)S(1)} collective-permute-done((bf16[64,1024]{1,0:T(8,128)(2,1)S(1)}, bf16[64,1024]{1,0:T(8,128)(2,1)S(1)}, u32[]{:S(2)}, u32[]{:S(2)}) %collective-permute-start.1) | collective-permute-done | bytes 131104 | tf_op jit(solution)/shard_map/ppermute | solution.py:176
  32.4 2.9 %shard_map.68 = f32[4,16,256]{2,1,0:T(8,128)} custom-call(bf16[512,256]{1,0:T(8,128)(2,1)S(1)} %bitcast.28, bf16[512,256]{1,0:T(8,128)(2,1)S(1)} %collective-permute-done.3.other_ref, s32[1024,1]{1,0:T(8,128)S(1)} %copy.18.kpos_ref, s32[4,256]{1,0:T(4,128)S(1)} %tile.9.qpos_ref, bf16[64,1024]{1,0:T(8,128)(2,1)S(1)} %pad_maximum_fusion.1.refs_0_, ...), custom_call_target="tpu_custom_call" | custom-call | tf_op jit(solution)/shard_map/pallas_call | solution.py:107
  35.3 4.0 %all-to-all-start.1 = ((f32[4,16,256]{2,1,0:T(8,128)}), f32[4,16,256]{2,1,0:T(8,128)S(1)}, u32[]{:S(2)}, u32[]{:S(2)}) async-start(f32[4,16,256]{2,1,0:T(8,128)} %shard_map.68), calls=%async_computation.1 | async-start | bytes 131072 | tf_op jit(solution)/shard_map/all_to_all | solution.py:208
  39.4 5.6 %all-to-all-done.1.stats_ref = f32[4,16,256]{2,1,0:T(8,128)S(1)} async-done(((f32[4,16,256]{2,1,0:T(8,128)}), f32[4,16,256]{2,1,0:T(8,128)S(1)}, u32[]{:S(2)}, u32[]{:S(2)}) %all-to-all-start.1) | async-done | bytes 65568 | tf_op jit(solution)/shard_map/all_to_all | solution.py:208
  45.0 4.0 %shard_map.69 = (bf16[4,64,512]{2,1,0:T(8,128)(2,1)S(1)}, bf16[512,256]{1,0:T(8,128)(2,1)S(1)}, bf16[512,256]{1,0:T(8,128)(2,1)S(1)}) custom-call(s32[2]{0:T(128)S(1)} %pad_add_fusion.2.at_ref, f32[4,16,256]{2,1,0:T(8,128)S(1)} %all-to-all-done.1.stats_ref, bf16[512,256]{1,0:T(8,128)(2,1)S(1)} %bitcast.29, ...), custom_call_target="tpu_custom_call" | custom-call | tf_op jit(solution)/shard_map/pallas_call | solution.py:120
  50.9 10.0 %all_to_all.35 = bf16[4,64,512]{2,1,0:T(8,128)(2,1)S(1)} all-to-all(bf16[4,64,512]{2,1,0:T(8,128)(2,1)S(1)} %get-tuple-element.31), channel_id=1, replica_groups=mesh['x'=4,'h'=2,'l'=4,'c'=2,'w'=2,'y'=4] {'x'}, dimensions={0} | all-to-all | bytes 524288 | tf_op jit(solution)/shard_map/all_to_all | solution.py:212
  61.8 5.1 %all-to-all-start.3 = ((bf16[2,4,64,256]{3,2,0,1:T(8,128)(2,1)}), bf16[2,4,64,256]{3,2,0,1:T(8,128)(2,1)S(1)}, u32[]{:S(2)}, u32[]{:S(2)}) async-start(bf16[2,4,64,256]{3,2,0,1:T(8,128)(2,1)} %copy.20), calls=%async_computation.3 | async-start | bytes 524288 | tf_op jit(solution)/shard_map/all_to_all | solution.py:215
  66.9 3.5 %collective-permute-start.5 = (bf16[64,512]{1,0:T(8,128)(2,1)S(1)}, bf16[64,512]{1,0:T(8,128)(2,1)S(1)}, u32[]{:S(2)}, u32[]{:S(2)}) collective-permute-start(bf16[64,512]{1,0:T(8,128)(2,1)S(1)} %reduce_sum.36), channel_id=1, source_target_pairs={{0,64},{64,0},{1,65},{65,1},{2,66},{66,2},{3,67},{67,3},{4,68},{68... | collective-permute-start | bytes 196616 | tf_op jit(solution)/shard_map/ppermute | solution.py:176
  70.4 6.8 %collective-permute-done.5 = bf16[64,512]{1,0:T(8,128)(2,1)S(1)} collective-permute-done((bf16[64,512]{1,0:T(8,128)(2,1)S(1)}, bf16[64,512]{1,0:T(8,128)(2,1)S(1)}, u32[]{:S(2)}, u32[]{:S(2)}) %collective-permute-start.5) | collective-permute-done | bytes 65568 | tf_op jit(solution)/shard_map/ppermute | solution.py:176
  77.3 5.1 %collective-permute-start.6 = (bf16[2,64,256]{2,1,0:T(8,128)(2,1)S(1)}, bf16[2,64,256]{2,1,0:T(8,128)(2,1)S(1)}, u32[]{:S(2)}, u32[]{:S(2)}) collective-permute-start(bf16[2,64,256]{2,1,0:T(8,128)(2,1)S(1)} %reduce_sum.37), channel_id=1, source_target_pairs={{0,64},{64,0},{1,65},{65,1},{2,66},{66,2},{3,67},{67,3},{4,68},{68... | collective-permute-start | bytes 196616 | tf_op jit(solution)/shard_map/ppermute | solution.py:176
  82.4 5.4 %collective-permute-done.6 = bf16[2,64,256]{2,1,0:T(8,128)(2,1)S(1)} collective-permute-done((bf16[2,64,256]{2,1,0:T(8,128)(2,1)S(1)}, bf16[2,64,256]{2,1,0:T(8,128)(2,1)S(1)}, u32[]{:S(2)}, u32[]{:S(2)}) %collective-permute-start.6) | collective-permute-done | bytes 65568 | tf_op jit(solution)/shard_map/ppermute | solution.py:176
  87.9 26.2 %all_to_all.36 = bf16[4,2,64,768]{3,2,1,0:T(8,128)(2,1)S(1)} all-to-all(bf16[4,2,64,768]{3,2,1,0:T(8,128)(2,1)S(1)} %broadcast_in_dim.5), channel_id=1, replica_groups=mesh['x'=4,'h'=2,'l'=4,'c'=2,'w'=2,'y'=4] {'l'}, dimensions={0} | all-to-all | bytes 1572864 | tf_op jit(solution)/shard_map/all_to_all | solution.py:172
  114.1 3.1 %collective-permute-start.9 = (bf16[512,768]{1,0:T(8,128)(2,1)S(1)}, bf16[512,768]{1,0:T(8,128)(2,1)S(1)}, u32[]{:S(2)}, u32[]{:S(2)}) collective-permute-start(bf16[512,768]{1,0:T(8,128)(2,1)S(1)} %bitcast.20), channel_id=1, source_target_pairs={{0,384},{128,256},{256,128},{384,0},{1,385},{129,257},{257,129},{3... | collective-permute-start | bytes 2359304 | tf_op jit(solution)/shard_map/ppermute | solution.py:176
  117.2 3.4 %collective-permute-start.8 = (bf16[512,768]{1,0:T(8,128)(2,1)S(1)}, bf16[512,768]{1,0:T(8,128)(2,1)S(1)}, u32[]{:S(2)}, u32[]{:S(2)}) collective-permute-start(bf16[512,768]{1,0:T(8,128)(2,1)S(1)} %bitcast.21), channel_id=1, source_target_pairs={{0,256},{128,384},{256,0},{384,128},{1,257},{129,385},{257,1},{385... | collective-permute-start | bytes 2359304 | tf_op jit(solution)/shard_map/ppermute | solution.py:176
  120.6 3.4 %collective-permute-start.7 = (bf16[512,768]{1,0:T(8,128)(2,1)S(1)}, bf16[512,768]{1,0:T(8,128)(2,1)S(1)}, u32[]{:S(2)}, u32[]{:S(2)}) collective-permute-start(bf16[512,768]{1,0:T(8,128)(2,1)S(1)} %bitcast.22), channel_id=1, source_target_pairs={{0,128},{128,0},{256,384},{384,256},{1,129},{129,1},{257,385},{385... | collective-permute-start | bytes 2359304 | tf_op jit(solution)/shard_map/ppermute | solution.py:176
  125.9 26.4 %collective-permute-done.9.refs_3_ = bf16[512,768]{1,0:T(8,128)(2,1)S(1)} collective-permute-done((bf16[512,768]{1,0:T(8,128)(2,1)S(1)}, bf16[512,768]{1,0:T(8,128)(2,1)S(1)}, u32[]{:S(2)}, u32[]{:S(2)}) %collective-permute-start.9) | collective-permute-done | bytes 786464 | tf_op jit(solution)/shard_map/ppermute | solution.py:176
  163.2 19.8 %all_to_all.37 = bf16[4,1024,128]{2,1,0:T(8,128)(2,1)} all-to-all(bf16[4,1024,128]{2,1,0:T(8,128)(2,1)S(1)} %bitcast.26), channel_id=1, replica_groups=mesh['x'=4,'h'=2,'l'=4,'c'=2,'w'=2,'y'=4] {'y'}, dimensions={0} | all-to-all | bytes 2097152 | tf_op jit(solution)/shard_map/all_to_all | solution.py:228
  184.4 8.2 %collective-permute-start.14 = (bf16[1024,128]{1,0:T(8,128)(2,1)S(1)}, bf16[1024,128]{1,0:T(8,128)(2,1)S(1)}, u32[]{:S(2)}, u32[]{:S(2)}) collective-permute-start(bf16[1024,128]{1,0:T(8,128)(2,1)S(1)} %reduce_sum.38.mine_ref), channel_id=1, source_target_pairs={{0,4},{4,0},{1,5},{5,1},{2,6},{6,2},{3,7},{7,3},{8,12},{12,8},{9,1... | collective-permute-start | bytes 786440 | tf_op jit(solution)/shard_map/ppermute | solution.py:176
  200.7 17.5 %collective-permute-done.14.other_ref = bf16[1024,128]{1,0:T(8,128)(2,1)S(1)} collective-permute-done((bf16[1024,128]{1,0:T(8,128)(2,1)S(1)}, bf16[1024,128]{1,0:T(8,128)(2,1)S(1)}, u32[]{:S(2)}, u32[]{:S(2)}) %collective-permute-start.14) | collective-permute-done | bytes 262176 | tf_op jit(solution)/shard_map/ppermute | solution.py:176
  218.9 17.9 %all_to_all.38 = bf16[4,1024,128]{2,1,0:T(8,128)(2,1)S(1)} all-to-all(bf16[4,1024,128]{2,1,0:T(8,128)(2,1)S(1)} %shard_map.71), channel_id=1, replica_groups=mesh['x'=4,'h'=2,'l'=4,'c'=2,'w'=2,'y'=4] {'y'}, dimensions={0} | all-to-all | bytes 2097152 | tf_op jit(solution)/shard_map/all_to_all | solution.py:235
  (82 shorter events, 33.8 us)
Async XLA Ops:
  4.0 25.1 %all-to-all-start = ((bf16[8,64,256]{2,1,0:T(8,128)(2,1)}), bf16[8,64,256]{2,1,0:T(8,128)(2,1)S(1)}, u32[]{:S(2)}, u32[]{:S(2)}) async-start(bf16[8,64,256]{2,1,0:T(8,128)(2,1)} %broadcast_in_dim.4), calls=%async_computation | async-start | bytes 524288 | tf_op jit(solution)/shard_map/all_to_all | solution.py:172
  14.8 9.8 %collective-permute-start.2 = (bf16[64,1024]{1,0:T(8,128)(2,1)S(1)}, bf16[64,1024]{1,0:T(8,128)(2,1)S(1)}, u32[]{:S(2)}, u32[]{:S(2)}) collective-permute-start(bf16[64,1024]{1,0:T(8,128)(2,1)S(1)} %pad_maximum_fusion.1.refs_0_), channel_id=1, source_target_pairs={{0,384},{128,256},{256,128},{384,0},{1,385},{129,257},{257,129},{3... | collective-permute-start | bytes 393224 | tf_op jit(solution)/shard_map/ppermute | solution.py:176
  19.4 9.3 %collective-permute-start.1 = (bf16[64,1024]{1,0:T(8,128)(2,1)S(1)}, bf16[64,1024]{1,0:T(8,128)(2,1)S(1)}, u32[]{:S(2)}, u32[]{:S(2)}) collective-permute-start(bf16[64,1024]{1,0:T(8,128)(2,1)S(1)} %pad_maximum_fusion.1.refs_0_), channel_id=1, source_target_pairs={{0,256},{128,384},{256,0},{384,128},{1,257},{129,385},{257,1},{385... | collective-permute-start | bytes 393224 | tf_op jit(solution)/shard_map/ppermute | solution.py:176
  22.2 6.9 %collective-permute-start = (bf16[64,1024]{1,0:T(8,128)(2,1)S(1)}, bf16[64,1024]{1,0:T(8,128)(2,1)S(1)}, u32[]{:S(2)}, u32[]{:S(2)}) collective-permute-start(bf16[64,1024]{1,0:T(8,128)(2,1)S(1)} %pad_maximum_fusion.1.refs_0_), channel_id=1, source_target_pairs={{0,128},{128,0},{256,384},{384,256},{1,129},{129,1},{257,385},{385... | collective-permute-start | bytes 393224 | tf_op jit(solution)/shard_map/ppermute | solution.py:176
  29.0 3.4 %collective-permute-start.3 = (bf16[512,256]{1,0:T(8,128)(2,1)S(1)}, bf16[512,256]{1,0:T(8,128)(2,1)S(1)}, u32[]{:S(2)}, u32[]{:S(2)}) collective-permute-start(bf16[512,256]{1,0:T(8,128)(2,1)S(1)} %bitcast.27), channel_id=1, source_target_pairs={{0,8},{8,0},{1,9},{9,1},{2,10},{10,2},{3,11},{11,3},{4,12},{12,4},... | collective-permute-start | bytes 786440 | tf_op jit(solution)/shard_map/ppermute | solution.py:176
  35.3 9.6 %all-to-all-start.1 = ((f32[4,16,256]{2,1,0:T(8,128)}), f32[4,16,256]{2,1,0:T(8,128)S(1)}, u32[]{:S(2)}, u32[]{:S(2)}) async-start(f32[4,16,256]{2,1,0:T(8,128)} %shard_map.68), calls=%async_computation.1 | async-start | bytes 131072 | tf_op jit(solution)/shard_map/all_to_all | solution.py:208
  49.0 12.0 %collective-permute-start.4 = (bf16[512,256]{1,0:T(8,128)(2,1)S(1)}, bf16[512,256]{1,0:T(8,128)(2,1)S(1)}, u32[]{:S(2)}, u32[]{:S(2)}) collective-permute-start(bf16[512,256]{1,0:T(8,128)(2,1)S(1)} %get-tuple-element.30), channel_id=1, source_target_pairs={{0,8},{8,0},{1,9},{9,1},{2,10},{10,2},{3,11},{11,3},{4,12},{12,4},... | collective-permute-start | bytes 786440 | tf_op jit(solution)/shard_map/ppermute | solution.py:176
  61.8 15.5 %all-to-all-start.3 = ((bf16[2,4,64,256]{3,2,0,1:T(8,128)(2,1)}), bf16[2,4,64,256]{3,2,0,1:T(8,128)(2,1)S(1)}, u32[]{:S(2)}, u32[]{:S(2)}) async-start(bf16[2,4,64,256]{3,2,0,1:T(8,128)(2,1)} %copy.20), calls=%async_computation.3 | async-start | bytes 524288 | tf_op jit(solution)/shard_map/all_to_all | solution.py:215
  66.9 10.3 %collective-permute-start.5 = (bf16[64,512]{1,0:T(8,128)(2,1)S(1)}, bf16[64,512]{1,0:T(8,128)(2,1)S(1)}, u32[]{:S(2)}, u32[]{:S(2)}) collective-permute-start(bf16[64,512]{1,0:T(8,128)(2,1)S(1)} %reduce_sum.36), channel_id=1, source_target_pairs={{0,64},{64,0},{1,65},{65,1},{2,66},{66,2},{3,67},{67,3},{4,68},{68... | collective-permute-start | bytes 196616 | tf_op jit(solution)/shard_map/ppermute | solution.py:176
  77.3 10.5 %collective-permute-start.6 = (bf16[2,64,256]{2,1,0:T(8,128)(2,1)S(1)}, bf16[2,64,256]{2,1,0:T(8,128)(2,1)S(1)}, u32[]{:S(2)}, u32[]{:S(2)}) collective-permute-start(bf16[2,64,256]{2,1,0:T(8,128)(2,1)S(1)} %reduce_sum.37), channel_id=1, source_target_pairs={{0,64},{64,0},{1,65},{65,1},{2,66},{66,2},{3,67},{67,3},{4,68},{68... | collective-permute-start | bytes 196616 | tf_op jit(solution)/shard_map/ppermute | solution.py:176
  87.9 72.9 %copy-start.9 = (bf16[128,768]{1,0:T(8,128)(2,1)S(1)}, bf16[128,768]{1,0:T(8,128)(2,1)}, u32[]{:S(2)}) copy-start(bf16[128,768]{1,0:T(8,128)(2,1)} %refs_8_.1) | copy-start | bytes 589828
  114.1 38.1 %collective-permute-start.9 = (bf16[512,768]{1,0:T(8,128)(2,1)S(1)}, bf16[512,768]{1,0:T(8,128)(2,1)S(1)}, u32[]{:S(2)}, u32[]{:S(2)}) collective-permute-start(bf16[512,768]{1,0:T(8,128)(2,1)S(1)} %bitcast.20), channel_id=1, source_target_pairs={{0,384},{128,256},{256,128},{384,0},{1,385},{129,257},{257,129},{3... | collective-permute-start | bytes 2359304 | tf_op jit(solution)/shard_map/ppermute | solution.py:176
  117.2 37.0 %collective-permute-start.8 = (bf16[512,768]{1,0:T(8,128)(2,1)S(1)}, bf16[512,768]{1,0:T(8,128)(2,1)S(1)}, u32[]{:S(2)}, u32[]{:S(2)}) collective-permute-start(bf16[512,768]{1,0:T(8,128)(2,1)S(1)} %bitcast.21), channel_id=1, source_target_pairs={{0,256},{128,384},{256,0},{384,128},{1,257},{129,385},{257,1},{385... | collective-permute-start | bytes 2359304 | tf_op jit(solution)/shard_map/ppermute | solution.py:176
  120.6 36.0 %collective-permute-start.7 = (bf16[512,768]{1,0:T(8,128)(2,1)S(1)}, bf16[512,768]{1,0:T(8,128)(2,1)S(1)}, u32[]{:S(2)}, u32[]{:S(2)}) collective-permute-start(bf16[512,768]{1,0:T(8,128)(2,1)S(1)} %bitcast.22), channel_id=1, source_target_pairs={{0,128},{128,0},{256,384},{384,256},{1,129},{129,1},{257,385},{385... | collective-permute-start | bytes 2359304 | tf_op jit(solution)/shard_map/ppermute | solution.py:176
  123.9 34.6 %collective-permute-start.10 = (bf16[512,768]{1,0:T(8,128)(2,1)S(1)}, bf16[512,768]{1,0:T(8,128)(2,1)S(1)}, u32[]{:S(2)}, u32[]{:S(2)}) collective-permute-start(bf16[512,768]{1,0:T(8,128)(2,1)S(1)} %bitcast.23), channel_id=1, source_target_pairs={{0,8},{8,0},{1,9},{9,1},{2,10},{10,2},{3,11},{11,3},{4,12},{12,4},... | collective-permute-start | bytes 2359304 | tf_op jit(solution)/shard_map/ppermute | solution.py:176
  152.2 6.3 %collective-permute-start.13 = (bf16[512,768]{1,0:T(8,128)(2,1)S(1)}, bf16[512,768]{1,0:T(8,128)(2,1)S(1)}, u32[]{:S(2)}, u32[]{:S(2)}) collective-permute-start(bf16[512,768]{1,0:T(8,128)(2,1)S(1)} %collective-permute-done.9.refs_3_), channel_id=1, source_target_pairs={{0,8},{8,0},{1,9},{9,1},{2,10},{10,2},{3,11},{11,3},{4,12},{12,4},... | collective-permute-start | bytes 2359304 | tf_op jit(solution)/shard_map/ppermute | solution.py:176
  154.2 4.4 %collective-permute-start.12 = (bf16[512,768]{1,0:T(8,128)(2,1)S(1)}, bf16[512,768]{1,0:T(8,128)(2,1)S(1)}, u32[]{:S(2)}, u32[]{:S(2)}) collective-permute-start(bf16[512,768]{1,0:T(8,128)(2,1)S(1)} %collective-permute-done.8.refs_2_), channel_id=1, source_target_pairs={{0,8},{8,0},{1,9},{9,1},{2,10},{10,2},{3,11},{11,3},{4,12},{12,4},... | collective-permute-start | bytes 2359304 | tf_op jit(solution)/shard_map/ppermute | solution.py:176
  156.6 4.2 %collective-permute-start.11 = (bf16[512,768]{1,0:T(8,128)(2,1)S(1)}, bf16[512,768]{1,0:T(8,128)(2,1)S(1)}, u32[]{:S(2)}, u32[]{:S(2)}) collective-permute-start(bf16[512,768]{1,0:T(8,128)(2,1)S(1)} %collective-permute-done.7.refs_1_), channel_id=1, source_target_pairs={{0,8},{8,0},{1,9},{9,1},{2,10},{10,2},{3,11},{11,3},{4,12},{12,4},... | collective-permute-start | bytes 2359304 | tf_op jit(solution)/shard_map/ppermute | solution.py:176
  158.5 4.6 %copy-start = (bf16[512,768]{1,0:T(8,128)(2,1)}, bf16[512,768]{1,0:T(8,128)(2,1)S(1)}, u32[]{:S(2)}) copy-start(bf16[512,768]{1,0:T(8,128)(2,1)S(1)} %collective-permute-done.10.refs_4_) | copy-start | bytes 2359300
  158.6 4.6 %copy-start.2 = (bf16[512,768]{1,0:T(8,128)(2,1)}, bf16[512,768]{1,0:T(8,128)(2,1)S(1)}, u32[]{:S(2)}) copy-start(bf16[512,768]{1,0:T(8,128)(2,1)S(1)} %collective-permute-done.13.refs_7_) | copy-start | bytes 2359300
  158.6 4.6 %copy-start.4 = (bf16[512,768]{1,0:T(8,128)(2,1)}, bf16[512,768]{1,0:T(8,128)(2,1)S(1)}, u32[]{:S(2)}) copy-start(bf16[512,768]{1,0:T(8,128)(2,1)S(1)} %collective-permute-done.12.refs_6_) | copy-start | bytes 2359300
  160.8 2.4 %copy-start.6 = (bf16[512,768]{1,0:T(8,128)(2,1)}, bf16[512,768]{1,0:T(8,128)(2,1)S(1)}, u32[]{:S(2)}) copy-start(bf16[512,768]{1,0:T(8,128)(2,1)S(1)} %collective-permute-done.11.refs_5_) | copy-start | bytes 2359300
  184.4 33.8 %collective-permute-start.14 = (bf16[1024,128]{1,0:T(8,128)(2,1)S(1)}, bf16[1024,128]{1,0:T(8,128)(2,1)S(1)}, u32[]{:S(2)}, u32[]{:S(2)}) collective-permute-start(bf16[1024,128]{1,0:T(8,128)(2,1)S(1)} %reduce_sum.38.mine_ref), channel_id=1, source_target_pairs={{0,4},{4,0},{1,5},{5,1},{2,6},{6,2},{3,7},{7,3},{8,12},{12,8},{9,1... | collective-permute-start | bytes 786440 | tf_op jit(solution)/shard_map/ppermute | solution.py:176
  197.2 1.2 copy-start.8
  (8 other events, 7.7 us)

commit v4 on v3

--- a/solution.py
+++ b/solution.py
@@ -128,26 +128,38 @@
     )(at, stats, own, other, kpos, qpos, *qg)
 
 
+def combine_kernel(at_ref, mine_ref, other_ref, out_ref):
+    high = at_ref[2]
+    pair = mine_ref.shape[2]
+    wide = GROUP * HEAD_DIM
+    for n in range(2):
+        total = (mine_ref[n].astype(F32) + other_ref[n].astype(F32)).astype(BF)
+        for copy in range(out_ref.shape[0]):
+            out_ref[copy, n, :, wide:] = total
+            out_ref[copy, high, :, n * pair : (n + 1) * pair] = mine_ref[2 + n]
+            out_ref[copy, 1 - high, :, n * pair : (n + 1) * pair] = other_ref[2 + n]
+
+
 def project_kernel(at_ref, *refs):
-    piece_refs, weight_ref, out_ref = refs[: 2 * X], refs[2 * X], refs[2 * X + 1]
-    rows = out_ref.shape[3]
+    piece_refs, weight_refs, out_ref = refs[:C], refs[C : C + X], refs[C + X]
+    rows = out_ref.shape[4]
     for k in range(X):
         for side in range(C):
-            part = dot(piece_refs[side * X + k][...], weight_ref[...], ((1,), (1,))).astype(BF)
+            part = dot(piece_refs[side][...], weight_refs[k][...], ((1,), (1,))).astype(BF)
             for n in range(Z):
-                block = part[n * rows : (n + 1) * rows]
-                out_ref[at_ref[0] ^ k, n % 2 * (Z // 2) + n // 2, at_ref[1] ^ side] = block
+                z = n % 2 * (Z // 2) + n // 2
+                half, odd = z // (Z // Y), z % (Z // Y)
+                out_ref[at_ref[0] ^ k, half, odd, at_ref[1] ^ side] = part[n * rows : (n + 1) * rows]
 
 
 def weight_kernel(at_ref, *refs):
-    piece_refs, states_ref, out_ref = refs[: 2 * X], refs[2 * X], refs[2 * X + 1]
-    total = jnp.zeros(out_ref.shape, F32)
-    for k in range(X):
+    piece_refs, states_refs, out_ref = refs[:C], refs[C : C + X], refs[C + X]
+    for k in range(X):
+        total = jnp.zeros(out_ref.shape[1:], F32)
         for side in range(C):
-            place, core = at_ref[0] ^ k, at_ref[1] ^ side
-            rows = [states_ref[place, n % 2 * (Z // 2) + n // 2, core] for n in range(Z)]
-            total = total + dot(jnp.concatenate(rows, axis=0), piece_refs[side * X + k][...], ((0,), (0,)))
-    out_ref[...] = total
+            states = [states_refs[k][n % 2 * (Z // 2) + n // 2, at_ref[1] ^ side] for n in range(Z)]
+            total = total + dot(jnp.concatenate(states, axis=0), piece_refs[side][...], ((0,), (0,)))
+        out_ref[at_ref[0] ^ k] = total.astype(out_ref.dtype)
 
 
 def add_kernel(at_ref, mine_ref, other_ref, out_ref):
@@ -185,7 +197,7 @@
     mine = lax.axis_index("x")
     high = lax.axis_index("h")
     deep = high * (Z // 2) + lax.axis_index("l")
-    where = jnp.stack([mine, core]).astype(jnp.int32)
+    where = jnp.stack([mine, core, high]).astype(jnp.int32)
     slab = jnp.arange(half, dtype=jnp.int32)
     starts = offsets.reshape(X, Z, C, 2)
     row_start = lax.dynamic_index_in_dim(lax.dynamic_index_in_dim(starts, deep, 1, False), core, 1, False)
@@ -198,10 +210,9 @@
 
     qg = jnp.concatenate([qkv[:, :wide], grad_out], axis=1)
     pairs = qkv[:, wide:]
-    qg, pairs, key_pos, query_pos = lax.optimization_barrier((qg, pairs, key_pos, query_pos))
     qg_x = [qg] + [swap(qg, "x", X, k) for k in range(1, X)]
     own = gather(pairs, ("h", "l"), Z).reshape(Z * rows, pair)
-    own, *qg_x = lax.optimization_barrier((own, *qg_x))
+    own, key_pos, query_pos, *qg_x = lax.optimization_barrier((own, key_pos, query_pos, *qg_x))
     other = swap(own, "c")
 
     stats = attention_stats(own, other, key_pos, query_pos, qg_x)
@@ -211,29 +222,31 @@
     dkv_in = swap(dkv_give, "c")
     dq = jnp.sum(lax.all_to_all(dq, "x", 0, 0, tiled=True).astype(F32), axis=0).astype(BF)
     dkv = (dkv.astype(F32) + dkv_in.astype(F32)).astype(BF)
-    dkv, dq = lax.optimization_barrier((dkv, dq))
+    dkv, dq, weight = lax.optimization_barrier((dkv, dq, weight))
+    weights = [weight] + [swap(weight, "x", X, k) for k in range(1, X)]
     dkv = lax.all_to_all(dkv.reshape(2, Z // 2, rows, pair), "l", 1, 1, tiled=True)
-    dq_h = jnp.stack([dq, swap(dq, "h")])
-    dq_h = jnp.where(high == 0, dq_h, dq_h[::-1])
     dkv = jnp.sum(dkv.astype(F32), axis=1).astype(BF)
-    dkv, dq_h = lax.optimization_barrier((dkv, dq_h))
-    dkv = (dkv.astype(F32) + swap(dkv, "h").astype(F32)).astype(BF)
-
-    grads = gather(jnp.concatenate([dq_h, dkv], axis=2), "l", Z // 2).reshape(Z * rows, columns)
-    pieces = [grads] + [swap(grads, "x", X, k) for k in range(1, X)]
-    pieces = pieces + [swap(piece, "c") for piece in pieces]
-
+    joint = jnp.concatenate([dkv, dq[None, :, :pair], dq[None, :, pair:]], axis=0)
+    grads = local_call(combine_kernel, (Z // 2, 2, rows, columns), BF, where, joint, swap(joint, "h"))
+    grads, states, *weights = lax.optimization_barrier((grads, states, *weights))
+
+    grads = lax.all_to_all(grads, "l", 0, 0, tiled=True).reshape(Z * rows, columns)
     depth = weight.shape[0]
-    part = local_call(project_kernel, (X, Z, C, rows, depth), BF, where, *pieces, weight)
-    part = lax.all_to_all(part.reshape(Y, Z * C * rows, depth), "y", 0, 0, tiled=True)
-    part = jnp.sum(part.astype(F32), axis=0).astype(BF)
-    grad_weight = local_call(
-        weight_kernel, (depth, columns), F32, where, *pieces, states.reshape(X, Z, C, rows, depth)
-    )
+    blocks = states.reshape(X, Z, C, rows, depth)
+    blocks = [lax.dynamic_index_in_dim(blocks, mine ^ k, 0, keepdims=False) for k in range(X)]
+    blocks = [blocks[0]] + [swap(blocks[k], "x", X, k) for k in range(1, X)]
+    grads, *blocks = lax.optimization_barrier((grads, *blocks))
+    pieces = [grads, swap(grads, "c")]
+
+    part = local_call(project_kernel, (X, Y, Z // Y, C, rows, depth), BF, where, *pieces, *weights)
+    part = lax.all_to_all(part.reshape(X * Y, -1, depth), ("x", "y"), 0, 0, tiled=True)
+    part = jnp.sum(part.reshape(X, Y, -1, depth).astype(F32), axis=1).astype(BF)
+    grad_weight = local_call(weight_kernel, (X, depth, columns), BF, where, *pieces, *blocks)
+    grad_weight = jnp.sum(lax.all_to_all(grad_weight, "x", 0, 0, tiled=True).astype(F32), axis=0)
     part = local_call(add_kernel, (Y,) + part.shape, BF, where, part, swap(part, "w"))
     part, grad_weight = lax.optimization_barrier((part, grad_weight))
     grad_states = lax.all_to_all(part, "y", 0, 0, tiled=True)
-    return grad_states.reshape(-1, depth), grad_weight
+    return jnp.moveaxis(grad_states, 0, 1).reshape(-1, depth), grad_weight
 
 
 def solution(mesh):

time: 239 us -> 208 us (0.87)
  the two profiles are of different devices: /device:TPU:160 before, /device:TPU:162 now
where the time goes in v4:
time: 208 us; the launch traced here: 207 us
  starting transfers between devices  91.3 us (44%)
  waiting for transfers between devices  63.9 us (31%)
  blocking collectives  28.3 us (14%)
  Pallas kernels  14.6 us (7%)
  local copies, waits for them, and re-layouts  5.74 us (3%)
  other arithmetic  2.57 us (1%)
    ppermute x14, waiting for transfers between devices, swap(): return lax.ppermute(x, axis, [(n, n ^ bit) for n in range(size)])  46.9 us
    ppermute x14, starting transfers between devices, swap(): return lax.ppermute(x, axis, [(n, n ^ bit) for n in range(size)])  46.8 us
    all_to_all x1, blocking collectives, body(): grad_states = lax.all_to_all(part, 'y', 0, 0, tiled=True)  18.3 us
    all_to_all x1, waiting for transfers between devices, body(): lax.all_to_all(part.reshape(X * Y, -1, depth), ('x', 'y'), 0, 0, tiled=True)  13 us
    all_to_all x1, starting transfers between devices, gather(): return lax.all_to_all(copies, axis, 0, 0, tiled=True)  10.8 us
    all_to_all x1, starting transfers between devices, body(): lax.all_to_all(grads, 'l', 0, 0, tiled=True).reshape(Z * rows, columns)  10.5 us
    all_to_all x1, blocking collectives, body(): lax.all_to_all(dq, 'x', 0, 0, tiled=True).astype(F32)  10 us
    pallas_call x4, Pallas kernels, local_call(): pl.pallas_call(kernel, out_shape=jax.ShapeDtypeStruct(shape, dtype), in_s...  7.85 us
  transfers between devices with their start and end apart: 20, of which 10 were waited for; matrix products, arithmetic and copies ran while one was open for 2% of the time, Pallas kernels for 2%

profile of v4, /device:TPU:162, one launch (start us, length us, event | category | flops | bytes accessed | tf_op | source)
XLA Modules:
  0.0 207.4 jit_solution(5084358071910714274)
XLA Ops:
  2.2 10.8 %all-to-all-start = ((bf16[8,64,256]{2,1,0:T(8,128)(2,1)}), bf16[8,64,256]{2,1,0:T(8,128)(2,1)S(1)}, u32[]{:S(2)}, u32[]{:S(2)}) async-start(bf16[8,64,256]{2,1,0:T(8,128)(2,1)} %broadcast_in_dim.6), calls=%async_computation | async-start | bytes 524288 | tf_op jit(solution)/shard_map/all_to_all | solution.py:184
  13.0 3.4 %collective-permute-start.2 = (bf16[64,1024]{1,0:T(8,128)(2,1)S(1)}, bf16[64,1024]{1,0:T(8,128)(2,1)S(1)}, u32[]{:S(2)}, u32[]{:S(2)}) collective-permute-start(bf16[64,1024]{1,0:T(8,128)(2,1)S(1)} %pad_maximum_fusion.refs_0_), channel_id=1, source_target_pairs={{0,384},{128,256},{256,128},{384,0},{1,385},{129,257},{257,129},{3... | collective-permute-start | bytes 393224 | tf_op jit(solution)/shard_map/ppermute | solution.py:188
  16.4 3.0 %collective-permute-start.1 = (bf16[64,1024]{1,0:T(8,128)(2,1)S(1)}, bf16[64,1024]{1,0:T(8,128)(2,1)S(1)}, u32[]{:S(2)}, u32[]{:S(2)}) collective-permute-start(bf16[64,1024]{1,0:T(8,128)(2,1)S(1)} %pad_maximum_fusion.refs_0_), channel_id=1, source_target_pairs={{0,256},{128,384},{256,0},{384,128},{1,257},{129,385},{257,1},{385... | collective-permute-start | bytes 393224 | tf_op jit(solution)/shard_map/ppermute | solution.py:188
  19.5 3.4 %collective-permute-start = (bf16[64,1024]{1,0:T(8,128)(2,1)S(1)}, bf16[64,1024]{1,0:T(8,128)(2,1)S(1)}, u32[]{:S(2)}, u32[]{:S(2)}) collective-permute-start(bf16[64,1024]{1,0:T(8,128)(2,1)S(1)} %pad_maximum_fusion.refs_0_), channel_id=1, source_target_pairs={{0,128},{128,0},{256,384},{384,256},{1,129},{129,1},{257,385},{385... | collective-permute-start | bytes 393224 | tf_op jit(solution)/shard_map/ppermute | solution.py:188
  30.1 2.7 %shard_map.68 = f32[4,16,256]{2,1,0:T(8,128)} custom-call(bf16[512,256]{1,0:T(8,128)(2,1)S(1)} %bitcast.38, bf16[512,256]{1,0:T(8,128)(2,1)S(1)} %collective-permute-done.3.other_ref, s32[1024,1]{1,0:T(8,128)S(1)} %copy.19.kpos_ref, s32[4,256]{1,0:T(4,128)S(1)} %tile.9.qpos_ref, bf16[64,1024]{1,0:T(8,128)(2,1)S(1)} %pad_maximum_fusion.refs_0_, ...), custom_call_target="tpu_custom_call" | custom-call | tf_op jit(solution)/shard_map/pallas_call | solution.py:107
  32.9 5.1 %all-to-all-start.1 = ((f32[4,16,256]{2,1,0:T(8,128)}), f32[4,16,256]{2,1,0:T(8,128)S(1)}, u32[]{:S(2)}, u32[]{:S(2)}) async-start(f32[4,16,256]{2,1,0:T(8,128)} %shard_map.68), calls=%async_computation.1 | async-start | bytes 131072 | tf_op jit(solution)/shard_map/all_to_all | solution.py:219
  38.1 4.1 %all-to-all-done.1.stats_ref = f32[4,16,256]{2,1,0:T(8,128)S(1)} async-done(((f32[4,16,256]{2,1,0:T(8,128)}), f32[4,16,256]{2,1,0:T(8,128)S(1)}, u32[]{:S(2)}, u32[]{:S(2)}) %all-to-all-start.1) | async-done | bytes 65568 | tf_op jit(solution)/shard_map/all_to_all | solution.py:219
  42.1 4.0 %shard_map.69 = (bf16[4,64,512]{2,1,0:T(8,128)(2,1)S(1)}, bf16[512,256]{1,0:T(8,128)(2,1)S(1)}, bf16[512,256]{1,0:T(8,128)(2,1)S(1)}) custom-call(s32[3]{0:T(128)S(1)} %pad_add_fusion.2.at_ref, f32[4,16,256]{2,1,0:T(8,128)S(1)} %all-to-all-done.1.stats_ref, bf16[512,256]{1,0:T(8,128)(2,1)S(1)} %bitcast.39, ...), custom_call_target="tpu_custom_call" | custom-call | tf_op jit(solution)/shard_map/pallas_call | solution.py:120
  48.0 10.0 %all_to_all.40 = bf16[4,64,512]{2,1,0:T(8,128)(2,1)S(1)} all-to-all(bf16[4,64,512]{2,1,0:T(8,128)(2,1)S(1)} %get-tuple-element.37), channel_id=1, replica_groups=mesh['x'=4,'h'=2,'l'=4,'c'=2,'w'=2,'y'=4] {'x'}, dimensions={0} | all-to-all | bytes 524288 | tf_op jit(solution)/shard_map/all_to_all | solution.py:223
  58.9 5.1 %all-to-all-start.3 = ((bf16[2,4,64,256]{3,2,0,1:T(8,128)(2,1)}), bf16[2,4,64,256]{3,2,0,1:T(8,128)(2,1)S(1)}, u32[]{:S(2)}, u32[]{:S(2)}) async-start(bf16[2,4,64,256]{3,2,0,1:T(8,128)(2,1)} %copy.21), calls=%async_computation.3 | async-start | bytes 524288 | tf_op jit(solution)/shard_map/all_to_all | solution.py:227
  66.1 5.2 %collective-permute-start.7 = (bf16[128,768]{1,0:T(8,128)(2,1)S(1)}, bf16[128,768]{1,0:T(8,128)(2,1)S(1)}, u32[]{:S(2)}, u32[]{:S(2)}) collective-permute-start(bf16[128,768]{1,0:T(8,128)(2,1)S(1)} %copy-done), channel_id=1, source_target_pairs={{0,256},{128,384},{256,0},{384,128},{1,257},{129,385},{257,1},{385... | collective-permute-start | bytes 589832 | tf_op jit(solution)/shard_map/ppermute | solution.py:188
  73.9 3.4 %collective-permute-start.5 = (bf16[4,64,256]{2,1,0:T(8,128)(2,1)S(1)}, bf16[4,64,256]{2,1,0:T(8,128)(2,1)S(1)}, u32[]{:S(2)}, u32[]{:S(2)}) collective-permute-start(bf16[4,64,256]{2,1,0:T(8,128)(2,1)S(1)} %pad_maximum_fusion.1.mine_ref), channel_id=1, source_target_pairs={{0,64},{64,0},{1,65},{65,1},{2,66},{66,2},{3,67},{67,3},{4,68},{68... | collective-permute-start | bytes 393224 | tf_op jit(solution)/shard_map/ppermute | solution.py:188
  77.4 8.5 %collective-permute-done.5.other_ref = bf16[4,64,256]{2,1,0:T(8,128)(2,1)S(1)} collective-permute-done((bf16[4,64,256]{2,1,0:T(8,128)(2,1)S(1)}, bf16[4,64,256]{2,1,0:T(8,128)(2,1)S(1)}, u32[]{:S(2)}, u32[]{:S(2)}) %collective-permute-start.5) | collective-permute-done | bytes 131104 | tf_op jit(solution)/shard_map/ppermute | solution.py:188
  87.4 10.5 %all-to-all-start.4 = ((bf16[4,2,64,768]{3,2,1,0:T(8,128)(2,1)}), bf16[4,2,64,768]{3,2,1,0:T(8,128)(2,1)S(1)}, u32[]{:S(2)}, u32[]{:S(2)}) async-start(bf16[4,2,64,768]{3,2,1,0:T(8,128)(2,1)} %shard_map.70), calls=%async_computation.4 | async-start | bytes 1572864 | tf_op jit(solution)/shard_map/all_to_all | solution.py:233
  101.4 5.1 %collective-permute-start.10 = (bf16[8,2,64,128]{3,2,1,0:T(8,128)(2,1)S(1)}, bf16[8,2,64,128]{3,2,1,0:T(8,128)(2,1)S(1)}, u32[]{:S(2)}, u32[]{:S(2)}) collective-permute-start(bf16[8,2,64,128]{3,2,1,0:T(8,128)(2,1)S(1)} %get-tuple-element.55), channel_id=1, source_target_pairs={{0,256},{128,384},{256,0},{384,128},{1,257},{129,385},{257,1},{385... | collective-permute-start | bytes 786440 | tf_op jit(solution)/shard_map/ppermute | solution.py:188
  109.0 5.3 %collective-permute-done.11.refs_5_ = bf16[8,2,64,128]{3,2,1,0:T(8,128)(2,1)S(1)} collective-permute-done((bf16[8,2,64,128]{3,2,1,0:T(8,128)(2,1)S(1)}, bf16[8,2,64,128]{3,2,1,0:T(8,128)(2,1)S(1)}, u32[]{:S(2)}, u32[]{:S(2)}) %collective-permute-start.11) | collective-permute-done | bytes 262176 | tf_op jit(solution)/shard_map/ppermute | solution.py:188
  114.3 3.7 %collective-permute-done.9.refs_3_ = bf16[8,2,64,128]{3,2,1,0:T(8,128)(2,1)S(1)} collective-permute-done((bf16[8,2,64,128]{3,2,1,0:T(8,128)(2,1)S(1)}, bf16[8,2,64,128]{3,2,1,0:T(8,128)(2,1)S(1)}, u32[]{:S(2)}, u32[]{:S(2)}) %collective-permute-start.9) | collective-permute-done | bytes 262176 | tf_op jit(solution)/shard_map/ppermute | solution.py:188
  122.2 3.3 %shard_map.71 = bf16[4,4,2,2,64,128]{5,4,3,2,1,0:T(8,128)(2,1)} custom-call(s32[3]{0:T(128)S(1)} %pad_add_fusion.2.at_ref, bf16[512,768]{1,0:T(8,128)(2,1)S(1)} %bitcast.35, bf16[512,768]{1,0:T(8,128)(2,1)S(1)} %collective-permute-done.12.refs_1_, bf16[128,768]{1,0:T(8,128)(2,1)S(1)} %copy-done, bf16[128,768]{1,0:T(8,128)(2,1)S(1)} %collective-permute-done.6.refs_3_, ...), custom_call_target="tpu_custom_call" | custom-call | tf_op jit(solution)/shard_map/pallas_call | solution.py:173
  125.6 6.6 %all-to-all-start.5 = ((bf16[16,256,128]{2,1,0:T(8,128)(2,1)}), bf16[16,256,128]{2,1,0:T(8,128)(2,1)}, u32[]{:S(2)}, u32[]{:S(2)}) async-start(bf16[16,256,128]{2,1,0:T(8,128)(2,1)} %bitcast.19), calls=%async_computation.5 | async-start | bytes 2097152 | tf_op jit(solution)/shard_map/all_to_all | solution.py:242
  134.6 13.0 %all-to-all-done.5 = bf16[16,256,128]{2,1,0:T(8,128)(2,1)} async-done(((bf16[16,256,128]{2,1,0:T(8,128)(2,1)}), bf16[16,256,128]{2,1,0:T(8,128)(2,1)}, u32[]{:S(2)}, u32[]{:S(2)}) %all-to-all-start.5) | async-done | bytes 1048608 | tf_op jit(solution)/shard_map/all_to_all | solution.py:242
  147.5 6.3 %all-to-all-start.6 = ((bf16[4,128,768]{2,1,0:T(8,128)(2,1)}), bf16[4,128,768]{2,1,0:T(8,128)(2,1)S(1)}, u32[]{:S(2)}, u32[]{:S(2)}) async-start(bf16[4,128,768]{2,1,0:T(8,128)(2,1)} %shard_map.73), calls=%async_computation.6 | async-start | bytes 1572864 | tf_op jit(solution)/shard_map/all_to_all | solution.py:245
  155.3 8.2 %collective-permute-start.13 = (bf16[4,256,128]{2,1,0:T(8,128)(2,1)S(1)}, bf16[4,256,128]{2,1,0:T(8,128)(2,1)S(1)}, u32[]{:S(2)}, u32[]{:S(2)}) collective-permute-start(bf16[4,256,128]{2,1,0:T(8,128)(2,1)S(1)} %bitcast_reduce_fusion.mine_ref), channel_id=1, source_target_pairs={{0,4},{4,0},{1,5},{5,1},{2,6},{6,2},{3,7},{7,3},{8,12},{12,8},{9,1... | collective-permute-start | bytes 786440 | tf_op jit(solution)/shard_map/ppermute | solution.py:188
  164.3 23.1 %collective-permute-done.13.other_ref = bf16[4,256,128]{2,1,0:T(8,128)(2,1)S(1)} collective-permute-done((bf16[4,256,128]{2,1,0:T(8,128)(2,1)S(1)}, bf16[4,256,128]{2,1,0:T(8,128)(2,1)S(1)}, u32[]{:S(2)}, u32[]{:S(2)}) %collective-permute-start.13) | collective-permute-done | bytes 262176 | tf_op jit(solution)/shard_map/ppermute | solution.py:188
  188.0 18.3 %all_to_all.41 = bf16[4,4,256,128]{3,2,1,0:T(8,128)(2,1)S(1)} all-to-all(bf16[4,4,256,128]{3,2,1,0:T(8,128)(2,1)S(1)} %shard_map.72), channel_id=1, replica_groups=mesh['x'=4,'h'=2,'l'=4,'c'=2,'w'=2,'y'=4] {'y'}, dimensions={0} | all-to-all | bytes 2097152 | tf_op jit(solution)/shard_map/all_to_all | solution.py:248
  (65 shorter events, 34.1 us)
Async XLA Ops:
  0.6 12.4 %slice-start = ((bf16[64,768]{1,0:T(8,128)(2,1)}), bf16[64,512]{1,0:T(8,128)(2,1)S(1)}, s32[]{:S(2)}) async-start(bf16[64,768]{1,0:T(8,128)(2,1)} %param.6), calls=%async_computation.8 | async-start | bytes 131072 | tf_op jit(solution)/shard_map/slice | solution.py:211
  0.6 12.4 %copy-start.1 = (bf16[64,512]{1,0:T(8,128)(2,1)S(1)}, bf16[64,512]{1,0:T(8,128)(2,1)}, u32[]{:S(2)}) copy-start(bf16[64,512]{1,0:T(8,128)(2,1)} %param.7) | copy-start | bytes 196612
  0.7 22.4 %copy-start.2 = (s32[128]{0:T(128)S(1)}, s32[128]{0:T(128)}, u32[]{:S(2)}) copy-start(s32[128]{0:T(128)} %param.9) | copy-start | bytes 1540
  2.2 24.5 %all-to-all-start = ((bf16[8,64,256]{2,1,0:T(8,128)(2,1)}), bf16[8,64,256]{2,1,0:T(8,128)(2,1)S(1)}, u32[]{:S(2)}, u32[]{:S(2)}) async-start(bf16[8,64,256]{2,1,0:T(8,128)(2,1)} %broadcast_in_dim.6), calls=%async_computation | async-start | bytes 524288 | tf_op jit(solution)/shard_map/all_to_all | solution.py:184
  13.0 11.0 %collective-permute-start.2 = (bf16[64,1024]{1,0:T(8,128)(2,1)S(1)}, bf16[64,1024]{1,0:T(8,128)(2,1)S(1)}, u32[]{:S(2)}, u32[]{:S(2)}) collective-permute-start(bf16[64,1024]{1,0:T(8,128)(2,1)S(1)} %pad_maximum_fusion.refs_0_), channel_id=1, source_target_pairs={{0,384},{128,256},{256,128},{384,0},{1,385},{129,257},{257,129},{3... | collective-permute-start | bytes 393224 | tf_op jit(solution)/shard_map/ppermute | solution.py:188
  16.4 8.9 %collective-permute-start.1 = (bf16[64,1024]{1,0:T(8,128)(2,1)S(1)}, bf16[64,1024]{1,0:T(8,128)(2,1)S(1)}, u32[]{:S(2)}, u32[]{:S(2)}) collective-permute-start(bf16[64,1024]{1,0:T(8,128)(2,1)S(1)} %pad_maximum_fusion.refs_0_), channel_id=1, source_target_pairs={{0,256},{128,384},{256,0},{384,128},{1,257},{129,385},{257,1},{385... | collective-permute-start | bytes 393224 | tf_op jit(solution)/shard_map/ppermute | solution.py:188
  19.5 7.2 %collective-permute-start = (bf16[64,1024]{1,0:T(8,128)(2,1)S(1)}, bf16[64,1024]{1,0:T(8,128)(2,1)S(1)}, u32[]{:S(2)}, u32[]{:S(2)}) collective-permute-start(bf16[64,1024]{1,0:T(8,128)(2,1)S(1)} %pad_maximum_fusion.refs_0_), channel_id=1, source_target_pairs={{0,128},{128,0},{256,384},{384,256},{1,129},{129,1},{257,385},{385... | collective-permute-start | bytes 393224 | tf_op jit(solution)/shard_map/ppermute | solution.py:188
  26.7 3.4 %collective-permute-start.3 = (bf16[512,256]{1,0:T(8,128)(2,1)S(1)}, bf16[512,256]{1,0:T(8,128)(2,1)S(1)}, u32[]{:S(2)}, u32[]{:S(2)}) collective-permute-start(bf16[512,256]{1,0:T(8,128)(2,1)S(1)} %bitcast.37), channel_id=1, source_target_pairs={{0,8},{8,0},{1,9},{9,1},{2,10},{10,2},{3,11},{11,3},{4,12},{12,4},... | collective-permute-start | bytes 786440 | tf_op jit(solution)/shard_map/ppermute | solution.py:188
  32.9 9.3 %all-to-all-start.1 = ((f32[4,16,256]{2,1,0:T(8,128)}), f32[4,16,256]{2,1,0:T(8,128)S(1)}, u32[]{:S(2)}, u32[]{:S(2)}) async-start(f32[4,16,256]{2,1,0:T(8,128)} %shard_map.68), calls=%async_computation.1 | async-start | bytes 131072 | tf_op jit(solution)/shard_map/all_to_all | solution.py:219
  46.1 12.0 %collective-permute-start.4 = (bf16[512,256]{1,0:T(8,128)(2,1)S(1)}, bf16[512,256]{1,0:T(8,128)(2,1)S(1)}, u32[]{:S(2)}, u32[]{:S(2)}) collective-permute-start(bf16[512,256]{1,0:T(8,128)(2,1)S(1)} %get-tuple-element.36), channel_id=1, source_target_pairs={{0,8},{8,0},{1,9},{9,1},{2,10},{10,2},{3,11},{11,3},{4,12},{12,4},... | collective-permute-start | bytes 786440 | tf_op jit(solution)/shard_map/ppermute | solution.py:188
  58.0 5.9 %copy-start = (bf16[128,768]{1,0:T(8,128)(2,1)S(1)}, bf16[128,768]{1,0:T(8,128)(2,1)}, u32[]{:S(2)}) copy-start(bf16[128,768]{1,0:T(8,128)(2,1)} %refs_2_) | copy-start | bytes 589828
  58.9 14.9 %all-to-all-start.3 = ((bf16[2,4,64,256]{3,2,0,1:T(8,128)(2,1)}), bf16[2,4,64,256]{3,2,0,1:T(8,128)(2,1)S(1)}, u32[]{:S(2)}, u32[]{:S(2)}) async-start(bf16[2,4,64,256]{3,2,0,1:T(8,128)(2,1)} %copy.21), calls=%async_computation.3 | async-start | bytes 524288 | tf_op jit(solution)/shard_map/all_to_all | solution.py:227
  64.0 23.4 %collective-permute-start.8 = (bf16[128,768]{1,0:T(8,128)(2,1)S(1)}, bf16[128,768]{1,0:T(8,128)(2,1)S(1)}, u32[]{:S(2)}, u32[]{:S(2)}) collective-permute-start(bf16[128,768]{1,0:T(8,128)(2,1)S(1)} %copy-done), channel_id=1, source_target_pairs={{0,384},{128,256},{256,128},{384,0},{1,385},{129,257},{257,129},{3... | collective-permute-start | bytes 589832 | tf_op jit(solution)/shard_map/ppermute | solution.py:188
  66.1 21.2 %collective-permute-start.7 = (bf16[128,768]{1,0:T(8,128)(2,1)S(1)}, bf16[128,768]{1,0:T(8,128)(2,1)S(1)}, u32[]{:S(2)}, u32[]{:S(2)}) collective-permute-start(bf16[128,768]{1,0:T(8,128)(2,1)S(1)} %copy-done), channel_id=1, source_target_pairs={{0,256},{128,384},{256,0},{384,128},{1,257},{129,385},{257,1},{385... | collective-permute-start | bytes 589832 | tf_op jit(solution)/shard_map/ppermute | solution.py:188
  71.3 16.0 %collective-permute-start.6 = (bf16[128,768]{1,0:T(8,128)(2,1)S(1)}, bf16[128,768]{1,0:T(8,128)(2,1)S(1)}, u32[]{:S(2)}, u32[]{:S(2)}) collective-permute-start(bf16[128,768]{1,0:T(8,128)(2,1)S(1)} %copy-done), channel_id=1, source_target_pairs={{0,128},{128,0},{256,384},{384,256},{1,129},{129,1},{257,385},{385... | collective-permute-start | bytes 589832 | tf_op jit(solution)/shard_map/ppermute | solution.py:188
  73.9 11.9 %collective-permute-start.5 = (bf16[4,64,256]{2,1,0:T(8,128)(2,1)S(1)}, bf16[4,64,256]{2,1,0:T(8,128)(2,1)S(1)}, u32[]{:S(2)}, u32[]{:S(2)}) collective-permute-start(bf16[4,64,256]{2,1,0:T(8,128)(2,1)S(1)} %pad_maximum_fusion.1.mine_ref), channel_id=1, source_target_pairs={{0,64},{64,0},{1,65},{65,1},{2,66},{66,2},{3,67},{67,3},{4,68},{68... | collective-permute-start | bytes 393224 | tf_op jit(solution)/shard_map/ppermute | solution.py:188
  87.4 30.7 %all-to-all-start.4 = ((bf16[4,2,64,768]{3,2,1,0:T(8,128)(2,1)}), bf16[4,2,64,768]{3,2,1,0:T(8,128)(2,1)S(1)}, u32[]{:S(2)}, u32[]{:S(2)}) async-start(bf16[4,2,64,768]{3,2,1,0:T(8,128)(2,1)} %shard_map.70), calls=%async_computation.4 | async-start | bytes 1572864 | tf_op jit(solution)/shard_map/all_to_all | solution.py:233
  99.1 15.2 %collective-permute-start.11 = (bf16[8,2,64,128]{3,2,1,0:T(8,128)(2,1)S(1)}, bf16[8,2,64,128]{3,2,1,0:T(8,128)(2,1)S(1)}, u32[]{:S(2)}, u32[]{:S(2)}) collective-permute-start(bf16[8,2,64,128]{3,2,1,0:T(8,128)(2,1)S(1)} %get-tuple-element.54), channel_id=1, source_target_pairs={{0,384},{128,256},{256,128},{384,0},{1,385},{129,257},{257,129},{3... | collective-permute-start | bytes 786440 | tf_op jit(solution)/shard_map/ppermute | solution.py:188
  101.4 13.0 %collective-permute-start.10 = (bf16[8,2,64,128]{3,2,1,0:T(8,128)(2,1)S(1)}, bf16[8,2,64,128]{3,2,1,0:T(8,128)(2,1)S(1)}, u32[]{:S(2)}, u32[]{:S(2)}) collective-permute-start(bf16[8,2,64,128]{3,2,1,0:T(8,128)(2,1)S(1)} %get-tuple-element.55), channel_id=1, source_target_pairs={{0,256},{128,384},{256,0},{384,128},{1,257},{129,385},{257,1},{385... | collective-permute-start | bytes 786440 | tf_op jit(solution)/shard_map/ppermute | solution.py:188
  106.5 11.6 %collective-permute-start.9 = (bf16[8,2,64,128]{3,2,1,0:T(8,128)(2,1)S(1)}, bf16[8,2,64,128]{3,2,1,0:T(8,128)(2,1)S(1)}, u32[]{:S(2)}, u32[]{:S(2)}) collective-permute-start(bf16[8,2,64,128]{3,2,1,0:T(8,128)(2,1)S(1)} %get-tuple-element.56), channel_id=1, source_target_pairs={{0,128},{128,0},{256,384},{384,256},{1,129},{129,1},{257,385},{385... | collective-permute-start | bytes 786440 | tf_op jit(solution)/shard_map/ppermute | solution.py:188
  118.1 4.2 %collective-permute-start.12 = (bf16[512,768]{1,0:T(8,128)(2,1)S(1)}, bf16[512,768]{1,0:T(8,128)(2,1)S(1)}, u32[]{:S(2)}, u32[]{:S(2)}) collective-permute-start(bf16[512,768]{1,0:T(8,128)(2,1)S(1)} %bitcast.34), channel_id=1, source_target_pairs={{0,8},{8,0},{1,9},{9,1},{2,10},{10,2},{3,11},{11,3},{4,12},{12,4},... | collective-permute-start | bytes 2359304 | tf_op jit(solution)/shard_map/ppermute | solution.py:188
  125.6 22.0 %all-to-all-start.5 = ((bf16[16,256,128]{2,1,0:T(8,128)(2,1)}), bf16[16,256,128]{2,1,0:T(8,128)(2,1)}, u32[]{:S(2)}, u32[]{:S(2)}) async-start(bf16[16,256,128]{2,1,0:T(8,128)(2,1)} %bitcast.19), calls=%async_computation.5 | async-start | bytes 2097152 | tf_op jit(solution)/shard_map/all_to_all | solution.py:242
  147.5 15.9 %all-to-all-start.6 = ((bf16[4,128,768]{2,1,0:T(8,128)(2,1)}), bf16[4,128,768]{2,1,0:T(8,128)(2,1)S(1)}, u32[]{:S(2)}, u32[]{:S(2)}) async-start(bf16[4,128,768]{2,1,0:T(8,128)(2,1)} %shard_map.73), calls=%async_computation.6 | async-start | bytes 1572864 | tf_op jit(solution)/shard_map/all_to_all | solution.py:245
  155.3 32.1 %collective-permute-start.13 = (bf16[4,256,128]{2,1,0:T(8,128)(2,1)S(1)}, bf16[4,256,128]{2,1,0:T(8,128)(2,1)S(1)}, u32[]{:S(2)}, u32[]{:S(2)}) collective-permute-start(bf16[4,256,128]{2,1,0:T(8,128)(2,1)S(1)} %bitcast_reduce_fusion.mine_ref), channel_id=1, source_target_pairs={{0,4},{4,0},{1,5},{5,1},{2,6},{6,2},{3,7},{7,3},{8,12},{12,8},{9,1... | collective-permute-start | bytes 786440 | tf_op jit(solution)/shard_map/ppermute | solution.py:188

commit v5 on v4

--- a/solution.py
+++ b/solution.py
@@ -153,13 +153,13 @@
 
 
 def weight_kernel(at_ref, *refs):
-    piece_refs, states_refs, out_ref = refs[:C], refs[C : C + X], refs[C + X]
-    for k in range(X):
-        total = jnp.zeros(out_ref.shape[1:], F32)
+    piece_refs, states_refs, out_refs = refs[:C], refs[C : C + X], refs[C + X :]
+    for k in range(X):
+        total = jnp.zeros(out_refs[k].shape, F32)
         for side in range(C):
             states = [states_refs[k][n % 2 * (Z // 2) + n // 2, at_ref[1] ^ side] for n in range(Z)]
             total = total + dot(jnp.concatenate(states, axis=0), piece_refs[side][...], ((0,), (0,)))
-        out_ref[at_ref[0] ^ k] = total.astype(out_ref.dtype)
+        out_refs[k][...] = total.astype(out_refs[k].dtype)
 
 
 def add_kernel(at_ref, mine_ref, other_ref, out_ref):
@@ -175,6 +175,17 @@
         out_shape=jax.ShapeDtypeStruct(shape, dtype),
         in_specs=[pl.BlockSpec(memory_space=pltpu.SMEM)] + [vmem] * (len(operands) - 1),
         out_specs=vmem,
+        compiler_params=pltpu.CompilerParams(vmem_limit_bytes=40 * 1024 * 1024),
+    )(*operands)
+
+
+def weight_call(shape, *operands):
+    vmem = pl.BlockSpec(memory_space=pltpu.VMEM)
+    return pl.pallas_call(
+        weight_kernel,
+        out_shape=[jax.ShapeDtypeStruct(shape, BF)] * X,
+        in_specs=[pl.BlockSpec(memory_space=pltpu.SMEM)] + [vmem] * (len(operands) - 1),
+        out_specs=[vmem] * X,
         compiler_params=pltpu.CompilerParams(vmem_limit_bytes=40 * 1024 * 1024),
     )(*operands)
 
@@ -206,12 +217,13 @@
     query_pos = jnp.tile(query_pos, (1, GROUP))
     key_start = lax.dynamic_index_in_dim(starts, mine, 0, False)
     key_start = jnp.stack([lax.dynamic_index_in_dim(key_start, core ^ k, 1, False) for k in range(C)])
+    key_start = jnp.moveaxis(key_start.reshape(C, 2, Z // 2, 2), 1, 2)
     key_pos = (key_start.reshape(-1)[:, None] + slab[None, :]).reshape(-1, 1)
 
     qg = jnp.concatenate([qkv[:, :wide], grad_out], axis=1)
     pairs = qkv[:, wide:]
     qg_x = [qg] + [swap(qg, "x", X, k) for k in range(1, X)]
-    own = gather(pairs, ("h", "l"), Z).reshape(Z * rows, pair)
+    own = gather(pairs, ("l", "h"), Z).reshape(Z * rows, pair)
     own, key_pos, query_pos, *qg_x = lax.optimization_barrier((own, key_pos, query_pos, *qg_x))
     other = swap(own, "c")
 
@@ -222,27 +234,29 @@
     dkv_in = swap(dkv_give, "c")
     dq = jnp.sum(lax.all_to_all(dq, "x", 0, 0, tiled=True).astype(F32), axis=0).astype(BF)
     dkv = (dkv.astype(F32) + dkv_in.astype(F32)).astype(BF)
-    dkv, dq, weight = lax.optimization_barrier((dkv, dq, weight))
-    weights = [weight] + [swap(weight, "x", X, k) for k in range(1, X)]
-    dkv = lax.all_to_all(dkv.reshape(2, Z // 2, rows, pair), "l", 1, 1, tiled=True)
-    dkv = jnp.sum(dkv.astype(F32), axis=1).astype(BF)
-    joint = jnp.concatenate([dkv, dq[None, :, :pair], dq[None, :, pair:]], axis=0)
-    grads = local_call(combine_kernel, (Z // 2, 2, rows, columns), BF, where, joint, swap(joint, "h"))
-    grads, states, *weights = lax.optimization_barrier((grads, states, *weights))
-
-    grads = lax.all_to_all(grads, "l", 0, 0, tiled=True).reshape(Z * rows, columns)
+    dkv, dq, weight, states = lax.optimization_barrier((dkv, dq, weight, states))
     depth = weight.shape[0]
     blocks = states.reshape(X, Z, C, rows, depth)
     blocks = [lax.dynamic_index_in_dim(blocks, mine ^ k, 0, keepdims=False) for k in range(X)]
     blocks = [blocks[0]] + [swap(blocks[k], "x", X, k) for k in range(1, X)]
-    grads, *blocks = lax.optimization_barrier((grads, *blocks))
+    dkv = lax.all_to_all(dkv.reshape(Z // 2, 2, rows, pair), "l", 0, 0, tiled=True)
+    dkv = jnp.sum(dkv.astype(F32), axis=0).astype(BF)
+    joint = jnp.concatenate([dkv, dq[None, :, :pair], dq[None, :, pair:]], axis=0)
+    grads = local_call(combine_kernel, (Z // 2, 2, rows, columns), BF, where, joint, swap(joint, "h"))
+    grads, weight, *blocks = lax.optimization_barrier((grads, weight, *blocks))
+    weights = [weight] + [swap(weight, "x", X, k) for k in range(1, X)]
+
+    grads = lax.all_to_all(grads, "l", 0, 0, tiled=True).reshape(Z * rows, columns)
+    grads, *weights = lax.optimization_barrier((grads, *weights))
     pieces = [grads, swap(grads, "c")]
 
     part = local_call(project_kernel, (X, Y, Z // Y, C, rows, depth), BF, where, *pieces, *weights)
     part = lax.all_to_all(part.reshape(X * Y, -1, depth), ("x", "y"), 0, 0, tiled=True)
     part = jnp.sum(part.reshape(X, Y, -1, depth).astype(F32), axis=1).astype(BF)
-    grad_weight = local_call(weight_kernel, (X, depth, columns), BF, where, *pieces, *blocks)
-    grad_weight = jnp.sum(lax.all_to_all(grad_weight, "x", 0, 0, tiled=True).astype(F32), axis=0)
+    gw = weight_call((depth, columns), where, *pieces, *blocks)
+    grad_weight = gw[0].astype(F32)
+    for k in range(1, X):
+        grad_weight = grad_weight + swap(gw[k], "x", X, k).astype(F32)
     part = local_call(add_kernel, (Y,) + part.shape, BF, where, part, swap(part, "w"))
     part, grad_weight = lax.optimization_barrier((part, grad_weight))
     grad_states = lax.all_to_all(part, "y", 0, 0, tiled=True)

time: 208 us -> 203 us (0.976)
  the two profiles are of different devices: /device:TPU:162 before, /device:TPU:160 now
where the time goes in v5:
time: 203 us; the launch traced here: 202 us
  starting transfers between devices  92.9 us (46%)
  waiting for transfers between devices  57.1 us (28%)
  blocking collectives  28.5 us (14%)
  Pallas kernels  13.7 us (7%)
  local copies, waits for them, and re-layouts  5.29 us (3%)
  other arithmetic  3.26 us (2%)
    ppermute x17, starting transfers between devices, swap(): return lax.ppermute(x, axis, [(n, n ^ bit) for n in range(size)])  57.1 us
    ppermute x17, waiting for transfers between devices, swap(): return lax.ppermute(x, axis, [(n, n ^ bit) for n in range(size)])  44.5 us
    all_to_all x1, blocking collectives, body(): grad_states = lax.all_to_all(part, 'y', 0, 0, tiled=True)  18.3 us
    all_to_all x1, starting transfers between devices, gather(): return lax.all_to_all(copies, axis, 0, 0, tiled=True)  10.8 us
    all_to_all x1, starting transfers between devices, body(): lax.all_to_all(grads, 'l', 0, 0, tiled=True).reshape(Z * rows, columns)  10.7 us
    all_to_all x1, blocking collectives, body(): lax.all_to_all(dq, 'x', 0, 0, tiled=True).astype(F32)  10.1 us
    all_to_all x1, waiting for transfers between devices, body(): lax.all_to_all(part.reshape(X * Y, -1, depth), ('x', 'y'), 0, 0, tiled=True)  6.15 us
    all_to_all x1, waiting for transfers between devices, body(): stats = lax.all_to_all(stats, 'x', 0, 0, tiled=True)  5.55 us
  transfers between devices with their start and end apart: 22, of which 12 were waited for; matrix products, arithmetic and copies ran while one was open for 2% of the time, Pallas kernels for 2%

profile of v5, /device:TPU:160, one launch (start us, length us, event | category | flops | bytes accessed | tf_op | source)
XLA Modules:
  0.0 201.7 jit_solution(15520587122534811605)
XLA Ops:
  2.1 10.8 %all-to-all-start = ((bf16[8,64,256]{2,1,0:T(8,128)(2,1)}), bf16[8,64,256]{2,1,0:T(8,128)(2,1)S(1)}, u32[]{:S(2)}, u32[]{:S(2)}) async-start(bf16[8,64,256]{2,1,0:T(8,128)(2,1)} %broadcast_in_dim.6), calls=%async_computation | async-start | bytes 524288 | tf_op jit(solution)/shard_map/all_to_all | solution.py:195
  13.8 4.7 %collective-permute-start.2 = (bf16[64,1024]{1,0:T(8,128)(2,1)S(1)}, bf16[64,1024]{1,0:T(8,128)(2,1)S(1)}, u32[]{:S(2)}, u32[]{:S(2)}) collective-permute-start(bf16[64,1024]{1,0:T(8,128)(2,1)S(1)} %pad_maximum_fusion.refs_0_), channel_id=1, source_target_pairs={{0,384},{128,256},{256,128},{384,0},{1,385},{129,257},{257,129},{3... | collective-permute-start | bytes 393224 | tf_op jit(solution)/shard_map/ppermute | solution.py:199
  34.2 4.0 %all-to-all-start.1 = ((f32[4,16,256]{2,1,0:T(8,128)}), f32[4,16,256]{2,1,0:T(8,128)S(1)}, u32[]{:S(2)}, u32[]{:S(2)}) async-start(f32[4,16,256]{2,1,0:T(8,128)} %shard_map.68), calls=%async_computation.1 | async-start | bytes 131072 | tf_op jit(solution)/shard_map/all_to_all | solution.py:231
  38.3 5.5 %all-to-all-done.1.stats_ref = f32[4,16,256]{2,1,0:T(8,128)S(1)} async-done(((f32[4,16,256]{2,1,0:T(8,128)}), f32[4,16,256]{2,1,0:T(8,128)S(1)}, u32[]{:S(2)}, u32[]{:S(2)}) %all-to-all-start.1) | async-done | bytes 65568 | tf_op jit(solution)/shard_map/all_to_all | solution.py:231
  43.9 4.0 %shard_map.69 = (bf16[4,64,512]{2,1,0:T(8,128)(2,1)S(1)}, bf16[512,256]{1,0:T(8,128)(2,1)S(1)}, bf16[512,256]{1,0:T(8,128)(2,1)S(1)}) custom-call(s32[3]{0:T(128)S(1)} %pad_add_fusion.1.at_ref, f32[4,16,256]{2,1,0:T(8,128)S(1)} %all-to-all-done.1.stats_ref, bf16[512,256]{1,0:T(8,128)(2,1)S(1)} %bitcast.41, ...), custom_call_target="tpu_custom_call" | custom-call | tf_op jit(solution)/shard_map/pallas_call | solution.py:120
  49.8 10.1 %all_to_all.35 = bf16[4,64,512]{2,1,0:T(8,128)(2,1)S(1)} all-to-all(bf16[4,64,512]{2,1,0:T(8,128)(2,1)S(1)} %get-tuple-element.42), channel_id=1, replica_groups=mesh['x'=4,'h'=2,'l'=4,'c'=2,'w'=2,'y'=4] {'x'}, dimensions={0} | all-to-all | bytes 524288 | tf_op jit(solution)/shard_map/all_to_all | solution.py:235
  60.7 5.1 %all-to-all-start.3 = ((bf16[4,2,64,256]{3,2,1,0:T(8,128)(2,1)}), bf16[4,2,64,256]{3,2,1,0:T(8,128)(2,1)S(1)}, u32[]{:S(2)}, u32[]{:S(2)}) async-start(bf16[4,2,64,256]{3,2,1,0:T(8,128)(2,1)} %bitcast.11), calls=%async_computation.3 | async-start | bytes 524288 | tf_op jit(solution)/shard_map/all_to_all | solution.py:242
  65.9 3.1 %collective-permute-start.8 = (bf16[8,2,64,128]{3,2,1,0:T(8,128)(2,1)S(1)}, bf16[8,2,64,128]{3,2,1,0:T(8,128)(2,1)S(1)}, u32[]{:S(2)}, u32[]{:S(2)}) collective-permute-start(bf16[8,2,64,128]{3,2,1,0:T(8,128)(2,1)S(1)} %get-tuple-element.64), channel_id=1, source_target_pairs={{0,384},{128,256},{256,128},{384,0},{1,385},{129,257},{257,129},{3... | collective-permute-start | bytes 786440 | tf_op jit(solution)/shard_map/ppermute | solution.py:199
  69.0 3.4 %collective-permute-start.7 = (bf16[8,2,64,128]{3,2,1,0:T(8,128)(2,1)S(1)}, bf16[8,2,64,128]{3,2,1,0:T(8,128)(2,1)S(1)}, u32[]{:S(2)}, u32[]{:S(2)}) collective-permute-start(bf16[8,2,64,128]{3,2,1,0:T(8,128)(2,1)S(1)} %get-tuple-element.65), channel_id=1, source_target_pairs={{0,256},{128,384},{256,0},{384,128},{1,257},{129,385},{257,1},{385... | collective-permute-start | bytes 786440 | tf_op jit(solution)/shard_map/ppermute | solution.py:199
  72.4 3.4 %collective-permute-start.6 = (bf16[8,2,64,128]{3,2,1,0:T(8,128)(2,1)S(1)}, bf16[8,2,64,128]{3,2,1,0:T(8,128)(2,1)S(1)}, u32[]{:S(2)}, u32[]{:S(2)}) collective-permute-start(bf16[8,2,64,128]{3,2,1,0:T(8,128)(2,1)S(1)} %get-tuple-element.66), channel_id=1, source_target_pairs={{0,128},{128,0},{256,384},{384,256},{1,129},{129,1},{257,385},{385... | collective-permute-start | bytes 786440 | tf_op jit(solution)/shard_map/ppermute | solution.py:199
  75.8 3.2 %collective-permute-start.5 = (bf16[4,64,256]{2,1,0:T(8,128)(2,1)S(1)}, bf16[4,64,256]{2,1,0:T(8,128)(2,1)S(1)}, u32[]{:S(2)}, u32[]{:S(2)}) collective-permute-start(bf16[4,64,256]{2,1,0:T(8,128)(2,1)S(1)} %pad_maximum_fusion.1.mine_ref), channel_id=1, source_target_pairs={{0,64},{64,0},{1,65},{65,1},{2,66},{66,2},{3,67},{67,3},{4,68},{68... | collective-permute-start | bytes 393224 | tf_op jit(solution)/shard_map/ppermute | solution.py:199
  79.1 8.7 %collective-permute-done.5.other_ref = bf16[4,64,256]{2,1,0:T(8,128)(2,1)S(1)} collective-permute-done((bf16[4,64,256]{2,1,0:T(8,128)(2,1)S(1)}, bf16[4,64,256]{2,1,0:T(8,128)(2,1)S(1)}, u32[]{:S(2)}, u32[]{:S(2)}) %collective-permute-start.5) | collective-permute-done | bytes 131104 | tf_op jit(solution)/shard_map/ppermute | solution.py:199
  89.3 10.7 %all-to-all-start.4 = ((bf16[4,2,64,768]{3,2,1,0:T(8,128)(2,1)}), bf16[4,2,64,768]{3,2,1,0:T(8,128)(2,1)S(1)}, u32[]{:S(2)}, u32[]{:S(2)}) async-start(bf16[4,2,64,768]{3,2,1,0:T(8,128)(2,1)} %shard_map.70), calls=%async_computation.4 | async-start | bytes 1572864 | tf_op jit(solution)/shard_map/all_to_all | solution.py:249
  100.0 3.1 %collective-permute-start.11 = (bf16[128,768]{1,0:T(8,128)(2,1)S(1)}, bf16[128,768]{1,0:T(8,128)(2,1)S(1)}, u32[]{:S(2)}, u32[]{:S(2)}) collective-permute-start(bf16[128,768]{1,0:T(8,128)(2,1)S(1)} %copy-done), channel_id=1, source_target_pairs={{0,384},{128,256},{256,128},{384,0},{1,385},{129,257},{257,129},{3... | collective-permute-start | bytes 589832 | tf_op jit(solution)/shard_map/ppermute | solution.py:199
  103.0 3.4 %collective-permute-start.10 = (bf16[128,768]{1,0:T(8,128)(2,1)S(1)}, bf16[128,768]{1,0:T(8,128)(2,1)S(1)}, u32[]{:S(2)}, u32[]{:S(2)}) collective-permute-start(bf16[128,768]{1,0:T(8,128)(2,1)S(1)} %copy-done), channel_id=1, source_target_pairs={{0,256},{128,384},{256,0},{384,128},{1,257},{129,385},{257,1},{385... | collective-permute-start | bytes 589832 | tf_op jit(solution)/shard_map/ppermute | solution.py:199
  106.4 3.4 %collective-permute-start.9 = (bf16[128,768]{1,0:T(8,128)(2,1)S(1)}, bf16[128,768]{1,0:T(8,128)(2,1)S(1)}, u32[]{:S(2)}, u32[]{:S(2)}) collective-permute-start(bf16[128,768]{1,0:T(8,128)(2,1)S(1)} %copy-done), channel_id=1, source_target_pairs={{0,128},{128,0},{256,384},{384,256},{1,129},{129,1},{257,385},{385... | collective-permute-start | bytes 589832 | tf_op jit(solution)/shard_map/ppermute | solution.py:199
  121.1 3.3 %shard_map.71 = bf16[4,4,2,2,64,128]{5,4,3,2,1,0:T(8,128)(2,1)} custom-call(s32[3]{0:T(128)S(1)} %pad_add_fusion.1.at_ref, bf16[512,768]{1,0:T(8,128)(2,1)S(1)} %bitcast.37, bf16[512,768]{1,0:T(8,128)(2,1)S(1)} %collective-permute-done.12.refs_1_, bf16[128,768]{1,0:T(8,128)(2,1)S(1)} %copy-done, bf16[128,768]{1,0:T(8,128)(2,1)S(1)} %collective-permute-done.9.refs_3_, ...), custom_call_target="tpu_custom_call" | custom-call | tf_op jit(solution)/shard_map/pallas_call | solution.py:173
  124.4 5.2 %all-to-all-start.5 = ((bf16[16,256,128]{2,1,0:T(8,128)(2,1)}), bf16[16,256,128]{2,1,0:T(8,128)(2,1)}, u32[]{:S(2)}, u32[]{:S(2)}) async-start(bf16[16,256,128]{2,1,0:T(8,128)(2,1)} %bitcast.20), calls=%async_computation.5 | async-start | bytes 2097152 | tf_op jit(solution)/shard_map/all_to_all | solution.py:254
  131.2 3.8 %collective-permute-start.14 = (bf16[128,768]{1,0:T(8,128)(2,1)S(1)}, bf16[128,768]{1,0:T(8,128)(2,1)S(1)}, u32[]{:S(2)}, u32[]{:S(2)}) collective-permute-start(bf16[128,768]{1,0:T(8,128)(2,1)S(1)} %get-tuple-element.59), channel_id=1, source_target_pairs={{0,128},{128,0},{256,384},{384,256},{1,129},{129,1},{257,385},{385... | collective-permute-start | bytes 589832 | tf_op jit(solution)/shard_map/ppermute | solution.py:199
  135.0 4.6 %collective-permute-start.15 = (bf16[128,768]{1,0:T(8,128)(2,1)S(1)}, bf16[128,768]{1,0:T(8,128)(2,1)S(1)}, u32[]{:S(2)}, u32[]{:S(2)}) collective-permute-start(bf16[128,768]{1,0:T(8,128)(2,1)S(1)} %get-tuple-element.60), channel_id=1, source_target_pairs={{0,256},{128,384},{256,0},{384,128},{1,257},{129,385},{257,1},{385... | collective-permute-start | bytes 589832 | tf_op jit(solution)/shard_map/ppermute | solution.py:199
  141.7 6.2 %all-to-all-done.5 = bf16[16,256,128]{2,1,0:T(8,128)(2,1)} async-done(((bf16[16,256,128]{2,1,0:T(8,128)(2,1)}), bf16[16,256,128]{2,1,0:T(8,128)(2,1)}, u32[]{:S(2)}, u32[]{:S(2)}) %all-to-all-start.5) | async-done | bytes 1048608 | tf_op jit(solution)/shard_map/all_to_all | solution.py:254
  149.2 8.2 %collective-permute-start.13 = (bf16[4,256,128]{2,1,0:T(8,128)(2,1)S(1)}, bf16[4,256,128]{2,1,0:T(8,128)(2,1)S(1)}, u32[]{:S(2)}, u32[]{:S(2)}) collective-permute-start(bf16[4,256,128]{2,1,0:T(8,128)(2,1)S(1)} %bitcast_reduce_fusion.mine_ref), channel_id=1, source_target_pairs={{0,4},{4,0},{1,5},{5,1},{2,6},{6,2},{3,7},{7,3},{8,12},{12,8},{9,1... | collective-permute-start | bytes 786440 | tf_op jit(solution)/shard_map/ppermute | solution.py:199
  158.3 23.3 %collective-permute-done.13.other_ref = bf16[4,256,128]{2,1,0:T(8,128)(2,1)S(1)} collective-permute-done((bf16[4,256,128]{2,1,0:T(8,128)(2,1)S(1)}, bf16[4,256,128]{2,1,0:T(8,128)(2,1)S(1)}, u32[]{:S(2)}, u32[]{:S(2)}) %collective-permute-start.13) | collective-permute-done | bytes 262176 | tf_op jit(solution)/shard_map/ppermute | solution.py:199
  182.3 18.3 %all_to_all.36 = bf16[4,4,256,128]{3,2,1,0:T(8,128)(2,1)S(1)} all-to-all(bf16[4,4,256,128]{3,2,1,0:T(8,128)(2,1)S(1)} %shard_map.72), channel_id=1, replica_groups=mesh['x'=4,'h'=2,'l'=4,'c'=2,'w'=2,'y'=4] {'y'}, dimensions={0} | all-to-all | bytes 2097152 | tf_op jit(solution)/shard_map/all_to_all | solution.py:262
  (71 shorter events, 41.2 us)
Async XLA Ops:
  2.1 26.0 %all-to-all-start = ((bf16[8,64,256]{2,1,0:T(8,128)(2,1)}), bf16[8,64,256]{2,1,0:T(8,128)(2,1)S(1)}, u32[]{:S(2)}, u32[]{:S(2)}) async-start(bf16[8,64,256]{2,1,0:T(8,128)(2,1)} %broadcast_in_dim.6), calls=%async_computation | async-start | bytes 524288 | tf_op jit(solution)/shard_map/all_to_all | solution.py:195
  13.8 11.6 %collective-permute-start.2 = (bf16[64,1024]{1,0:T(8,128)(2,1)S(1)}, bf16[64,1024]{1,0:T(8,128)(2,1)S(1)}, u32[]{:S(2)}, u32[]{:S(2)}) collective-permute-start(bf16[64,1024]{1,0:T(8,128)(2,1)S(1)} %pad_maximum_fusion.refs_0_), channel_id=1, source_target_pairs={{0,384},{128,256},{256,128},{384,0},{1,385},{129,257},{257,129},{3... | collective-permute-start | bytes 393224 | tf_op jit(solution)/shard_map/ppermute | solution.py:199
  18.5 9.3 %collective-permute-start.1 = (bf16[64,1024]{1,0:T(8,128)(2,1)S(1)}, bf16[64,1024]{1,0:T(8,128)(2,1)S(1)}, u32[]{:S(2)}, u32[]{:S(2)}) collective-permute-start(bf16[64,1024]{1,0:T(8,128)(2,1)S(1)} %pad_maximum_fusion.refs_0_), channel_id=1, source_target_pairs={{0,256},{128,384},{256,0},{384,128},{1,257},{129,385},{257,1},{385... | collective-permute-start | bytes 393224 | tf_op jit(solution)/shard_map/ppermute | solution.py:199
  21.2 6.9 %collective-permute-start = (bf16[64,1024]{1,0:T(8,128)(2,1)S(1)}, bf16[64,1024]{1,0:T(8,128)(2,1)S(1)}, u32[]{:S(2)}, u32[]{:S(2)}) collective-permute-start(bf16[64,1024]{1,0:T(8,128)(2,1)S(1)} %pad_maximum_fusion.refs_0_), channel_id=1, source_target_pairs={{0,128},{128,0},{256,384},{384,256},{1,129},{129,1},{257,385},{385... | collective-permute-start | bytes 393224 | tf_op jit(solution)/shard_map/ppermute | solution.py:199
  28.1 3.4 %collective-permute-start.3 = (bf16[512,256]{1,0:T(8,128)(2,1)S(1)}, bf16[512,256]{1,0:T(8,128)(2,1)S(1)}, u32[]{:S(2)}, u32[]{:S(2)}) collective-permute-start(bf16[512,256]{1,0:T(8,128)(2,1)S(1)} %bitcast.39), channel_id=1, source_target_pairs={{0,8},{8,0},{1,9},{9,1},{2,10},{10,2},{3,11},{11,3},{4,12},{12,4},... | collective-permute-start | bytes 786440 | tf_op jit(solution)/shard_map/ppermute | solution.py:199
  34.2 9.6 %all-to-all-start.1 = ((f32[4,16,256]{2,1,0:T(8,128)}), f32[4,16,256]{2,1,0:T(8,128)S(1)}, u32[]{:S(2)}, u32[]{:S(2)}) async-start(f32[4,16,256]{2,1,0:T(8,128)} %shard_map.68), calls=%async_computation.1 | async-start | bytes 131072 | tf_op jit(solution)/shard_map/all_to_all | solution.py:231
  47.8 12.1 %collective-permute-start.4 = (bf16[512,256]{1,0:T(8,128)(2,1)S(1)}, bf16[512,256]{1,0:T(8,128)(2,1)S(1)}, u32[]{:S(2)}, u32[]{:S(2)}) collective-permute-start(bf16[512,256]{1,0:T(8,128)(2,1)S(1)} %get-tuple-element.41), channel_id=1, source_target_pairs={{0,8},{8,0},{1,9},{9,1},{2,10},{10,2},{3,11},{11,3},{4,12},{12,4},... | collective-permute-start | bytes 786440 | tf_op jit(solution)/shard_map/ppermute | solution.py:199
  49.7 16.1 %copy-start.1 = (bf16[4096,128]{1,0:T(8,128)(2,1)S(1)}, bf16[4096,128]{1,0:T(8,128)(2,1)}, u32[]{:S(2)}) copy-start(bf16[4096,128]{1,0:T(8,128)(2,1)} %param.5) | copy-start | bytes 3145732
  60.7 15.1 %all-to-all-start.3 = ((bf16[4,2,64,256]{3,2,1,0:T(8,128)(2,1)}), bf16[4,2,64,256]{3,2,1,0:T(8,128)(2,1)S(1)}, u32[]{:S(2)}, u32[]{:S(2)}) async-start(bf16[4,2,64,256]{3,2,1,0:T(8,128)(2,1)} %bitcast.11), calls=%async_computation.3 | async-start | bytes 524288 | tf_op jit(solution)/shard_map/all_to_all | solution.py:242
  65.9 23.4 %collective-permute-start.8 = (bf16[8,2,64,128]{3,2,1,0:T(8,128)(2,1)S(1)}, bf16[8,2,64,128]{3,2,1,0:T(8,128)(2,1)S(1)}, u32[]{:S(2)}, u32[]{:S(2)}) collective-permute-start(bf16[8,2,64,128]{3,2,1,0:T(8,128)(2,1)S(1)} %get-tuple-element.64), channel_id=1, source_target_pairs={{0,384},{128,256},{256,128},{384,0},{1,385},{129,257},{257,129},{3... | collective-permute-start | bytes 786440 | tf_op jit(solution)/shard_map/ppermute | solution.py:199
  69.0 20.3 %collective-permute-start.7 = (bf16[8,2,64,128]{3,2,1,0:T(8,128)(2,1)S(1)}, bf16[8,2,64,128]{3,2,1,0:T(8,128)(2,1)S(1)}, u32[]{:S(2)}, u32[]{:S(2)}) collective-permute-start(bf16[8,2,64,128]{3,2,1,0:T(8,128)(2,1)S(1)} %get-tuple-element.65), channel_id=1, source_target_pairs={{0,256},{128,384},{256,0},{384,128},{1,257},{129,385},{257,1},{385... | collective-permute-start | bytes 786440 | tf_op jit(solution)/shard_map/ppermute | solution.py:199
  72.4 16.9 %collective-permute-start.6 = (bf16[8,2,64,128]{3,2,1,0:T(8,128)(2,1)S(1)}, bf16[8,2,64,128]{3,2,1,0:T(8,128)(2,1)S(1)}, u32[]{:S(2)}, u32[]{:S(2)}) collective-permute-start(bf16[8,2,64,128]{3,2,1,0:T(8,128)(2,1)S(1)} %get-tuple-element.66), channel_id=1, source_target_pairs={{0,128},{128,0},{256,384},{384,256},{1,129},{129,1},{257,385},{385... | collective-permute-start | bytes 786440 | tf_op jit(solution)/shard_map/ppermute | solution.py:199
  75.8 11.9 %collective-permute-start.5 = (bf16[4,64,256]{2,1,0:T(8,128)(2,1)S(1)}, bf16[4,64,256]{2,1,0:T(8,128)(2,1)S(1)}, u32[]{:S(2)}, u32[]{:S(2)}) collective-permute-start(bf16[4,64,256]{2,1,0:T(8,128)(2,1)S(1)} %pad_maximum_fusion.1.mine_ref), channel_id=1, source_target_pairs={{0,64},{64,0},{1,65},{65,1},{2,66},{66,2},{3,67},{67,3},{4,68},{68... | collective-permute-start | bytes 393224 | tf_op jit(solution)/shard_map/ppermute | solution.py:199
  89.3 10.7 %copy-start = (bf16[128,768]{1,0:T(8,128)(2,1)S(1)}, bf16[128,768]{1,0:T(8,128)(2,1)}, u32[]{:S(2)}) copy-start(bf16[128,768]{1,0:T(8,128)(2,1)} %refs_2_) | copy-start | bytes 589828
  89.3 27.7 %all-to-all-start.4 = ((bf16[4,2,64,768]{3,2,1,0:T(8,128)(2,1)}), bf16[4,2,64,768]{3,2,1,0:T(8,128)(2,1)S(1)}, u32[]{:S(2)}, u32[]{:S(2)}) async-start(bf16[4,2,64,768]{3,2,1,0:T(8,128)(2,1)} %shard_map.70), calls=%async_computation.4 | async-start | bytes 1572864 | tf_op jit(solution)/shard_map/all_to_all | solution.py:249
  100.0 12.8 %collective-permute-start.11 = (bf16[128,768]{1,0:T(8,128)(2,1)S(1)}, bf16[128,768]{1,0:T(8,128)(2,1)S(1)}, u32[]{:S(2)}, u32[]{:S(2)}) collective-permute-start(bf16[128,768]{1,0:T(8,128)(2,1)S(1)} %copy-done), channel_id=1, source_target_pairs={{0,384},{128,256},{256,128},{384,0},{1,385},{129,257},{257,129},{3... | collective-permute-start | bytes 589832 | tf_op jit(solution)/shard_map/ppermute | solution.py:199
  103.0 11.2 %collective-permute-start.10 = (bf16[128,768]{1,0:T(8,128)(2,1)S(1)}, bf16[128,768]{1,0:T(8,128)(2,1)S(1)}, u32[]{:S(2)}, u32[]{:S(2)}) collective-permute-start(bf16[128,768]{1,0:T(8,128)(2,1)S(1)} %copy-done), channel_id=1, source_target_pairs={{0,256},{128,384},{256,0},{384,128},{1,257},{129,385},{257,1},{385... | collective-permute-start | bytes 589832 | tf_op jit(solution)/shard_map/ppermute | solution.py:199
  106.4 9.7 %collective-permute-start.9 = (bf16[128,768]{1,0:T(8,128)(2,1)S(1)}, bf16[128,768]{1,0:T(8,128)(2,1)S(1)}, u32[]{:S(2)}, u32[]{:S(2)}) collective-permute-start(bf16[128,768]{1,0:T(8,128)(2,1)S(1)} %copy-done), channel_id=1, source_target_pairs={{0,128},{128,0},{256,384},{384,256},{1,129},{129,1},{257,385},{385... | collective-permute-start | bytes 589832 | tf_op jit(solution)/shard_map/ppermute | solution.py:199
  117.0 4.2 %collective-permute-start.12 = (bf16[512,768]{1,0:T(8,128)(2,1)S(1)}, bf16[512,768]{1,0:T(8,128)(2,1)S(1)}, u32[]{:S(2)}, u32[]{:S(2)}) collective-permute-start(bf16[512,768]{1,0:T(8,128)(2,1)S(1)} %bitcast.36), channel_id=1, source_target_pairs={{0,8},{8,0},{1,9},{9,1},{2,10},{10,2},{3,11},{11,3},{4,12},{12,4},... | collective-permute-start | bytes 2359304 | tf_op jit(solution)/shard_map/ppermute | solution.py:199
  124.4 23.4 %all-to-all-start.5 = ((bf16[16,256,128]{2,1,0:T(8,128)(2,1)}), bf16[16,256,128]{2,1,0:T(8,128)(2,1)}, u32[]{:S(2)}, u32[]{:S(2)}) async-start(bf16[16,256,128]{2,1,0:T(8,128)(2,1)} %bitcast.20), calls=%async_computation.5 | async-start | bytes 2097152 | tf_op jit(solution)/shard_map/all_to_all | solution.py:254
  131.2 26.2 %collective-permute-start.14 = (bf16[128,768]{1,0:T(8,128)(2,1)S(1)}, bf16[128,768]{1,0:T(8,128)(2,1)S(1)}, u32[]{:S(2)}, u32[]{:S(2)}) collective-permute-start(bf16[128,768]{1,0:T(8,128)(2,1)S(1)} %get-tuple-element.59), channel_id=1, source_target_pairs={{0,128},{128,0},{256,384},{384,256},{1,129},{129,1},{257,385},{385... | collective-permute-start | bytes 589832 | tf_op jit(solution)/shard_map/ppermute | solution.py:199
  135.0 22.4 %collective-permute-start.15 = (bf16[128,768]{1,0:T(8,128)(2,1)S(1)}, bf16[128,768]{1,0:T(8,128)(2,1)S(1)}, u32[]{:S(2)}, u32[]{:S(2)}) collective-permute-start(bf16[128,768]{1,0:T(8,128)(2,1)S(1)} %get-tuple-element.60), channel_id=1, source_target_pairs={{0,256},{128,384},{256,0},{384,128},{1,257},{129,385},{257,1},{385... | collective-permute-start | bytes 589832 | tf_op jit(solution)/shard_map/ppermute | solution.py:199
  139.6 17.9 %collective-permute-start.16 = (bf16[128,768]{1,0:T(8,128)(2,1)S(1)}, bf16[128,768]{1,0:T(8,128)(2,1)S(1)}, u32[]{:S(2)}, u32[]{:S(2)}) collective-permute-start(bf16[128,768]{1,0:T(8,128)(2,1)S(1)} %get-tuple-element.61), channel_id=1, source_target_pairs={{0,384},{128,256},{256,128},{384,0},{1,385},{129,257},{257,129},{3... | collective-permute-start | bytes 589832 | tf_op jit(solution)/shard_map/ppermute | solution.py:199
  149.2 32.5 %collective-permute-start.13 = (bf16[4,256,128]{2,1,0:T(8,128)(2,1)S(1)}, bf16[4,256,128]{2,1,0:T(8,128)(2,1)S(1)}, u32[]{:S(2)}, u32[]{:S(2)}) collective-permute-start(bf16[4,256,128]{2,1,0:T(8,128)(2,1)S(1)} %bitcast_reduce_fusion.mine_ref), channel_id=1, source_target_pairs={{0,4},{4,0},{1,5},{5,1},{2,6},{6,2},{3,7},{7,3},{8,12},{12,8},{9,1... | collective-permute-start | bytes 786440 | tf_op jit(solution)/shard_map/ppermute | solution.py:199
  (4 other events, 3.1 us)

commit v6 on v5

--- a/solution.py
+++ b/solution.py
@@ -253,13 +253,15 @@
     part = local_call(project_kernel, (X, Y, Z // Y, C, rows, depth), BF, where, *pieces, *weights)
     part = lax.all_to_all(part.reshape(X * Y, -1, depth), ("x", "y"), 0, 0, tiled=True)
     part = jnp.sum(part.reshape(X, Y, -1, depth).astype(F32), axis=1).astype(BF)
+    part, *pieces = lax.optimization_barrier((part, *pieces))
+    other = swap(part, "w")
     gw = weight_call((depth, columns), where, *pieces, *blocks)
-    grad_weight = gw[0].astype(F32)
-    for k in range(1, X):
-        grad_weight = grad_weight + swap(gw[k], "x", X, k).astype(F32)
-    part = local_call(add_kernel, (Y,) + part.shape, BF, where, part, swap(part, "w"))
-    part, grad_weight = lax.optimization_barrier((part, grad_weight))
+    gw = [gw[0]] + [swap(gw[k], "x", X, k) for k in range(1, X)]
+    part = local_call(add_kernel, (Y,) + part.shape, BF, where, part, other)
+    part, *gw = lax.optimization_barrier((part, *gw))
     grad_states = lax.all_to_all(part, "y", 0, 0, tiled=True)
+    grad_states, *gw = lax.optimization_barrier((grad_states, *gw))
+    grad_weight = sum(piece.astype(F32) for piece in gw)
     return jnp.moveaxis(grad_states, 0, 1).reshape(-1, depth), grad_weight
 
 

time: 203 us -> 202 us (level)
  blocking collectives: 28.5 us -> 50.4 us
  waiting for transfers between devices: 57.1 us -> 41.5 us
  starting transfers between devices: 92.9 us -> 87.6 us
    all_to_all x0 -> x1, blocking collectives: none -> 22.4 us  [body(): lax.all_to_all(part.reshape(X * Y, -1, depth), ('x', 'y'), 0, 0, tiled=True)]
    ppermute x17, waiting for transfers between devices: 44.5 us -> 35.1 us  [swap(): return lax.ppermute(x, axis, [(n, n ^ bit) for n in range(size)])]
    all_to_all x1 -> x0, waiting for transfers between devices: 6.15 us -> none  [body(): lax.all_to_all(part.reshape(X * Y, -1, depth), ('x', 'y'), 0, 0, tiled=True)]
    all_to_all x1 -> x0, starting transfers between devices: 5.22 us -> none  [body(): lax.all_to_all(part.reshape(X * Y, -1, depth), ('x', 'y'), 0, 0, tiled=True)]
  transfers between devices with their start and end apart: 22 -> 21, of which waited for: 12 -> 11; matrix products, arithmetic and copies ran while one was open for 2% -> 1% of each run, Pallas kernels for 2% -> 2%
where the time goes in v6:
time: 202 us; the launch traced here: 201 us
  starting transfers between devices  87.6 us (43%)
  blocking collectives  50.4 us (25%)
  waiting for transfers between devices  41.5 us (21%)
  Pallas kernels  12.8 us (6%)
  local copies, waits for them, and re-layouts  5.31 us (3%)
  other arithmetic  2.03 us (1%)
    ppermute x17, starting transfers between devices, swap(): return lax.ppermute(x, axis, [(n, n ^ bit) for n in range(size)])  57.1 us
    ppermute x17, waiting for transfers between devices, swap(): return lax.ppermute(x, axis, [(n, n ^ bit) for n in range(size)])  35.1 us
    all_to_all x1, blocking collectives, body(): lax.all_to_all(part.reshape(X * Y, -1, depth), ('x', 'y'), 0, 0, tiled=True)  22.4 us
    all_to_all x1, blocking collectives, body(): grad_states = lax.all_to_all(part, 'y', 0, 0, tiled=True)  17.9 us
    all_to_all x1, starting transfers between devices, gather(): return lax.all_to_all(copies, axis, 0, 0, tiled=True)  10.8 us
    all_to_all x1, starting transfers between devices, body(): lax.all_to_all(grads, 'l', 0, 0, tiled=True).reshape(Z * rows, columns)  10.7 us
    all_to_all x1, blocking collectives, body(): lax.all_to_all(dq, 'x', 0, 0, tiled=True).astype(F32)  10.1 us
    all_to_all x1, waiting for transfers between devices, body(): stats = lax.all_to_all(stats, 'x', 0, 0, tiled=True)  5.55 us
  transfers between devices with their start and end apart: 21, of which 11 were waited for; matrix products, arithmetic and copies ran while one was open for 1% of the time, Pallas kernels for 2%

profile of v6, /device:TPU:160, one launch (start us, length us, event | category | flops | bytes accessed | tf_op | source)
XLA Modules:
  0.0 200.8 jit_solution(12252305356747062829)
XLA Ops:
  2.1 10.8 %all-to-all-start = ((bf16[8,64,256]{2,1,0:T(8,128)(2,1)}), bf16[8,64,256]{2,1,0:T(8,128)(2,1)S(1)}, u32[]{:S(2)}, u32[]{:S(2)}) async-start(bf16[8,64,256]{2,1,0:T(8,128)(2,1)} %broadcast_in_dim.6), calls=%async_computation | async-start | bytes 524288 | tf_op jit(solution)/shard_map/all_to_all | solution.py:195
  13.8 4.7 %collective-permute-start.2 = (bf16[64,1024]{1,0:T(8,128)(2,1)S(1)}, bf16[64,1024]{1,0:T(8,128)(2,1)S(1)}, u32[]{:S(2)}, u32[]{:S(2)}) collective-permute-start(bf16[64,1024]{1,0:T(8,128)(2,1)S(1)} %pad_maximum_fusion.refs_0_), channel_id=1, source_target_pairs={{0,384},{128,256},{256,128},{384,0},{1,385},{129,257},{257,129},{3... | collective-permute-start | bytes 393224 | tf_op jit(solution)/shard_map/ppermute | solution.py:199
  31.5 2.8 %shard_map.68 = f32[4,16,256]{2,1,0:T(8,128)} custom-call(bf16[512,256]{1,0:T(8,128)(2,1)S(1)} %bitcast.41, bf16[512,256]{1,0:T(8,128)(2,1)S(1)} %collective-permute-done.3.other_ref, s32[1024,1]{1,0:T(8,128)S(1)} %copy.13.kpos_ref, s32[4,256]{1,0:T(4,128)S(1)} %tile.9.qpos_ref, bf16[64,1024]{1,0:T(8,128)(2,1)S(1)} %pad_maximum_fusion.refs_0_, ...), custom_call_target="tpu_custom_call" | custom-call | tf_op jit(solution)/shard_map/pallas_call | solution.py:107
  34.3 4.0 %all-to-all-start.1 = ((f32[4,16,256]{2,1,0:T(8,128)}), f32[4,16,256]{2,1,0:T(8,128)S(1)}, u32[]{:S(2)}, u32[]{:S(2)}) async-start(f32[4,16,256]{2,1,0:T(8,128)} %shard_map.68), calls=%async_computation.1 | async-start | bytes 131072 | tf_op jit(solution)/shard_map/all_to_all | solution.py:231
  38.4 5.5 %all-to-all-done.1.stats_ref = f32[4,16,256]{2,1,0:T(8,128)S(1)} async-done(((f32[4,16,256]{2,1,0:T(8,128)}), f32[4,16,256]{2,1,0:T(8,128)S(1)}, u32[]{:S(2)}, u32[]{:S(2)}) %all-to-all-start.1) | async-done | bytes 65568 | tf_op jit(solution)/shard_map/all_to_all | solution.py:231
  43.9 4.0 %shard_map.69 = (bf16[4,64,512]{2,1,0:T(8,128)(2,1)S(1)}, bf16[512,256]{1,0:T(8,128)(2,1)S(1)}, bf16[512,256]{1,0:T(8,128)(2,1)S(1)}) custom-call(s32[3]{0:T(128)S(1)} %pad_add_fusion.1.at_ref, f32[4,16,256]{2,1,0:T(8,128)S(1)} %all-to-all-done.1.stats_ref, bf16[512,256]{1,0:T(8,128)(2,1)S(1)} %bitcast.42, ...), custom_call_target="tpu_custom_call" | custom-call | tf_op jit(solution)/shard_map/pallas_call | solution.py:120
  49.9 10.1 %all_to_all.35 = bf16[4,64,512]{2,1,0:T(8,128)(2,1)S(1)} all-to-all(bf16[4,64,512]{2,1,0:T(8,128)(2,1)S(1)} %get-tuple-element.53), channel_id=1, replica_groups=mesh['x'=4,'h'=2,'l'=4,'c'=2,'w'=2,'y'=4] {'x'}, dimensions={0} | all-to-all | bytes 524288 | tf_op jit(solution)/shard_map/all_to_all | solution.py:235
  60.9 5.1 %all-to-all-start.3 = ((bf16[4,2,64,256]{3,2,1,0:T(8,128)(2,1)}), bf16[4,2,64,256]{3,2,1,0:T(8,128)(2,1)S(1)}, u32[]{:S(2)}, u32[]{:S(2)}) async-start(bf16[4,2,64,256]{3,2,1,0:T(8,128)(2,1)} %bitcast.11), calls=%async_computation.3 | async-start | bytes 524288 | tf_op jit(solution)/shard_map/all_to_all | solution.py:242
  66.0 3.1 %collective-permute-start.8 = (bf16[8,2,64,128]{3,2,1,0:T(8,128)(2,1)S(1)}, bf16[8,2,64,128]{3,2,1,0:T(8,128)(2,1)S(1)}, u32[]{:S(2)}, u32[]{:S(2)}) collective-permute-start(bf16[8,2,64,128]{3,2,1,0:T(8,128)(2,1)S(1)} %get-tuple-element.86), channel_id=1, source_target_pairs={{0,384},{128,256},{256,128},{384,0},{1,385},{129,257},{257,129},{3... | collective-permute-start | bytes 786440 | tf_op jit(solution)/shard_map/ppermute | solution.py:199
  69.1 3.4 %collective-permute-start.7 = (bf16[8,2,64,128]{3,2,1,0:T(8,128)(2,1)S(1)}, bf16[8,2,64,128]{3,2,1,0:T(8,128)(2,1)S(1)}, u32[]{:S(2)}, u32[]{:S(2)}) collective-permute-start(bf16[8,2,64,128]{3,2,1,0:T(8,128)(2,1)S(1)} %get-tuple-element.87), channel_id=1, source_target_pairs={{0,256},{128,384},{256,0},{384,128},{1,257},{129,385},{257,1},{385... | collective-permute-start | bytes 786440 | tf_op jit(solution)/shard_map/ppermute | solution.py:199
  72.5 3.4 %collective-permute-start.6 = (bf16[8,2,64,128]{3,2,1,0:T(8,128)(2,1)S(1)}, bf16[8,2,64,128]{3,2,1,0:T(8,128)(2,1)S(1)}, u32[]{:S(2)}, u32[]{:S(2)}) collective-permute-start(bf16[8,2,64,128]{3,2,1,0:T(8,128)(2,1)S(1)} %get-tuple-element.88), channel_id=1, source_target_pairs={{0,128},{128,0},{256,384},{384,256},{1,129},{129,1},{257,385},{385... | collective-permute-start | bytes 786440 | tf_op jit(solution)/shard_map/ppermute | solution.py:199
  76.0 3.3 %collective-permute-start.5 = (bf16[4,64,256]{2,1,0:T(8,128)(2,1)S(1)}, bf16[4,64,256]{2,1,0:T(8,128)(2,1)S(1)}, u32[]{:S(2)}, u32[]{:S(2)}) collective-permute-start(bf16[4,64,256]{2,1,0:T(8,128)(2,1)S(1)} %pad_maximum_fusion.1.mine_ref), channel_id=1, source_target_pairs={{0,64},{64,0},{1,65},{65,1},{2,66},{66,2},{3,67},{67,3},{4,68},{68... | collective-permute-start | bytes 393224 | tf_op jit(solution)/shard_map/ppermute | solution.py:199
  79.3 8.7 %collective-permute-done.5.other_ref = bf16[4,64,256]{2,1,0:T(8,128)(2,1)S(1)} collective-permute-done((bf16[4,64,256]{2,1,0:T(8,128)(2,1)S(1)}, bf16[4,64,256]{2,1,0:T(8,128)(2,1)S(1)}, u32[]{:S(2)}, u32[]{:S(2)}) %collective-permute-start.5) | collective-permute-done | bytes 131104 | tf_op jit(solution)/shard_map/ppermute | solution.py:199
  89.4 10.7 %all-to-all-start.4 = ((bf16[4,2,64,768]{3,2,1,0:T(8,128)(2,1)}), bf16[4,2,64,768]{3,2,1,0:T(8,128)(2,1)S(1)}, u32[]{:S(2)}, u32[]{:S(2)}) async-start(bf16[4,2,64,768]{3,2,1,0:T(8,128)(2,1)} %shard_map.70), calls=%async_computation.4 | async-start | bytes 1572864 | tf_op jit(solution)/shard_map/all_to_all | solution.py:249
  100.1 3.1 %collective-permute-start.11 = (bf16[128,768]{1,0:T(8,128)(2,1)S(1)}, bf16[128,768]{1,0:T(8,128)(2,1)S(1)}, u32[]{:S(2)}, u32[]{:S(2)}) collective-permute-start(bf16[128,768]{1,0:T(8,128)(2,1)S(1)} %copy-done), channel_id=1, source_target_pairs={{0,384},{128,256},{256,128},{384,0},{1,385},{129,257},{257,129},{3... | collective-permute-start | bytes 589832 | tf_op jit(solution)/shard_map/ppermute | solution.py:199
  103.2 3.4 %collective-permute-start.10 = (bf16[128,768]{1,0:T(8,128)(2,1)S(1)}, bf16[128,768]{1,0:T(8,128)(2,1)S(1)}, u32[]{:S(2)}, u32[]{:S(2)}) collective-permute-start(bf16[128,768]{1,0:T(8,128)(2,1)S(1)} %copy-done), channel_id=1, source_target_pairs={{0,256},{128,384},{256,0},{384,128},{1,257},{129,385},{257,1},{385... | collective-permute-start | bytes 589832 | tf_op jit(solution)/shard_map/ppermute | solution.py:199
  106.6 3.4 %collective-permute-start.9 = (bf16[128,768]{1,0:T(8,128)(2,1)S(1)}, bf16[128,768]{1,0:T(8,128)(2,1)S(1)}, u32[]{:S(2)}, u32[]{:S(2)}) collective-permute-start(bf16[128,768]{1,0:T(8,128)(2,1)S(1)} %copy-done), channel_id=1, source_target_pairs={{0,128},{128,0},{256,384},{384,256},{1,129},{129,1},{257,385},{385... | collective-permute-start | bytes 589832 | tf_op jit(solution)/shard_map/ppermute | solution.py:199
  109.9 3.0 %collective-permute-done.11.refs_5_ = bf16[128,768]{1,0:T(8,128)(2,1)S(1)} collective-permute-done((bf16[128,768]{1,0:T(8,128)(2,1)S(1)}, bf16[128,768]{1,0:T(8,128)(2,1)S(1)}, u32[]{:S(2)}, u32[]{:S(2)}) %collective-permute-start.11) | collective-permute-done | bytes 196640 | tf_op jit(solution)/shard_map/ppermute | solution.py:199
  123.6 22.4 %all_to_all.36 = bf16[16,256,128]{2,1,0:T(8,128)(2,1)S(1)} all-to-all(bf16[16,256,128]{2,1,0:T(8,128)(2,1)S(1)} %bitcast.39), channel_id=1, replica_groups=mesh['x'=4,'h'=2,'l'=4,'c'=2,'w'=2,'y'=4] {'x','y'}, dimensions={0} | all-to-all | bytes 2097152 | tf_op jit(solution)/shard_map/all_to_all | solution.py:254
  146.2 8.2 %collective-permute-start.13 = (bf16[4,256,128]{2,1,0:T(8,128)(2,1)S(1)}, bf16[4,256,128]{2,1,0:T(8,128)(2,1)S(1)}, u32[]{:S(2)}, u32[]{:S(2)}) collective-permute-start(bf16[4,256,128]{2,1,0:T(8,128)(2,1)S(1)} %bitcast_reduce_fusion.mine_ref), channel_id=1, source_target_pairs={{0,4},{4,0},{1,5},{5,1},{2,6},{6,2},{3,7},{7,3},{8,12},{12,8},{9,1... | collective-permute-start | bytes 786440 | tf_op jit(solution)/shard_map/ppermute | solution.py:199
  157.9 4.5 %collective-permute-start.15 = (bf16[128,768]{1,0:T(8,128)(2,1)S(1)}, bf16[128,768]{1,0:T(8,128)(2,1)S(1)}, u32[]{:S(2)}, u32[]{:S(2)}) collective-permute-start(bf16[128,768]{1,0:T(8,128)(2,1)S(1)} %get-tuple-element.74), channel_id=1, source_target_pairs={{0,256},{128,384},{256,0},{384,128},{1,257},{129,385},{257,1},{385... | collective-permute-start | bytes 589832 | tf_op jit(solution)/shard_map/ppermute | solution.py:199
  162.4 4.0 %collective-permute-start.16 = (bf16[128,768]{1,0:T(8,128)(2,1)S(1)}, bf16[128,768]{1,0:T(8,128)(2,1)S(1)}, u32[]{:S(2)}, u32[]{:S(2)}) collective-permute-start(bf16[128,768]{1,0:T(8,128)(2,1)S(1)} %get-tuple-element.75), channel_id=1, source_target_pairs={{0,384},{128,256},{256,128},{384,0},{1,385},{129,257},{257,129},{3... | collective-permute-start | bytes 589832 | tf_op jit(solution)/shard_map/ppermute | solution.py:199
  166.4 13.9 %collective-permute-done.13.other_ref = bf16[4,256,128]{2,1,0:T(8,128)(2,1)S(1)} collective-permute-done((bf16[4,256,128]{2,1,0:T(8,128)(2,1)S(1)}, bf16[4,256,128]{2,1,0:T(8,128)(2,1)S(1)}, u32[]{:S(2)}, u32[]{:S(2)}) %collective-permute-start.13) | collective-permute-done | bytes 262176 | tf_op jit(solution)/shard_map/ppermute | solution.py:199
  181.0 17.9 %all_to_all.37 = bf16[4,4,256,128]{3,2,1,0:T(8,128)(2,1)S(1)} all-to-all(bf16[4,4,256,128]{3,2,1,0:T(8,128)(2,1)S(1)} %shard_map.72), channel_id=1, replica_groups=mesh['x'=4,'h'=2,'l'=4,'c'=2,'w'=2,'y'=4] {'y'}, dimensions={0} | all-to-all | bytes 2097152 | tf_op jit(solution)/shard_map/all_to_all | solution.py:262
  (70 shorter events, 36.5 us)
Async XLA Ops:
  2.1 26.0 %all-to-all-start = ((bf16[8,64,256]{2,1,0:T(8,128)(2,1)}), bf16[8,64,256]{2,1,0:T(8,128)(2,1)S(1)}, u32[]{:S(2)}, u32[]{:S(2)}) async-start(bf16[8,64,256]{2,1,0:T(8,128)(2,1)} %broadcast_in_dim.6), calls=%async_computation | async-start | bytes 524288 | tf_op jit(solution)/shard_map/all_to_all | solution.py:195
  12.9 0.9 copy-start.2
  13.8 11.6 %collective-permute-start.2 = (bf16[64,1024]{1,0:T(8,128)(2,1)S(1)}, bf16[64,1024]{1,0:T(8,128)(2,1)S(1)}, u32[]{:S(2)}, u32[]{:S(2)}) collective-permute-start(bf16[64,1024]{1,0:T(8,128)(2,1)S(1)} %pad_maximum_fusion.refs_0_), channel_id=1, source_target_pairs={{0,384},{128,256},{256,128},{384,0},{1,385},{129,257},{257,129},{3... | collective-permute-start | bytes 393224 | tf_op jit(solution)/shard_map/ppermute | solution.py:199
  18.5 9.3 %collective-permute-start.1 = (bf16[64,1024]{1,0:T(8,128)(2,1)S(1)}, bf16[64,1024]{1,0:T(8,128)(2,1)S(1)}, u32[]{:S(2)}, u32[]{:S(2)}) collective-permute-start(bf16[64,1024]{1,0:T(8,128)(2,1)S(1)} %pad_maximum_fusion.refs_0_), channel_id=1, source_target_pairs={{0,256},{128,384},{256,0},{384,128},{1,257},{129,385},{257,1},{385... | collective-permute-start | bytes 393224 | tf_op jit(solution)/shard_map/ppermute | solution.py:199
  21.2 6.9 %collective-permute-start = (bf16[64,1024]{1,0:T(8,128)(2,1)S(1)}, bf16[64,1024]{1,0:T(8,128)(2,1)S(1)}, u32[]{:S(2)}, u32[]{:S(2)}) collective-permute-start(bf16[64,1024]{1,0:T(8,128)(2,1)S(1)} %pad_maximum_fusion.refs_0_), channel_id=1, source_target_pairs={{0,128},{128,0},{256,384},{384,256},{1,129},{129,1},{257,385},{385... | collective-permute-start | bytes 393224 | tf_op jit(solution)/shard_map/ppermute | solution.py:199
  28.1 3.4 %collective-permute-start.3 = (bf16[512,256]{1,0:T(8,128)(2,1)S(1)}, bf16[512,256]{1,0:T(8,128)(2,1)S(1)}, u32[]{:S(2)}, u32[]{:S(2)}) collective-permute-start(bf16[512,256]{1,0:T(8,128)(2,1)S(1)} %bitcast.40), channel_id=1, source_target_pairs={{0,8},{8,0},{1,9},{9,1},{2,10},{10,2},{3,11},{11,3},{4,12},{12,4},... | collective-permute-start | bytes 786440 | tf_op jit(solution)/shard_map/ppermute | solution.py:199
  34.3 9.6 %all-to-all-start.1 = ((f32[4,16,256]{2,1,0:T(8,128)}), f32[4,16,256]{2,1,0:T(8,128)S(1)}, u32[]{:S(2)}, u32[]{:S(2)}) async-start(f32[4,16,256]{2,1,0:T(8,128)} %shard_map.68), calls=%async_computation.1 | async-start | bytes 131072 | tf_op jit(solution)/shard_map/all_to_all | solution.py:231
  48.0 12.1 %collective-permute-start.4 = (bf16[512,256]{1,0:T(8,128)(2,1)S(1)}, bf16[512,256]{1,0:T(8,128)(2,1)S(1)}, u32[]{:S(2)}, u32[]{:S(2)}) collective-permute-start(bf16[512,256]{1,0:T(8,128)(2,1)S(1)} %get-tuple-element.52), channel_id=1, source_target_pairs={{0,8},{8,0},{1,9},{9,1},{2,10},{10,2},{3,11},{11,3},{4,12},{12,4},... | collective-permute-start | bytes 786440 | tf_op jit(solution)/shard_map/ppermute | solution.py:199
  49.9 16.1 %copy-start.1 = (bf16[4096,128]{1,0:T(8,128)(2,1)S(1)}, bf16[4096,128]{1,0:T(8,128)(2,1)}, u32[]{:S(2)}) copy-start(bf16[4096,128]{1,0:T(8,128)(2,1)} %param.5) | copy-start | bytes 3145732
  60.9 15.1 %all-to-all-start.3 = ((bf16[4,2,64,256]{3,2,1,0:T(8,128)(2,1)}), bf16[4,2,64,256]{3,2,1,0:T(8,128)(2,1)S(1)}, u32[]{:S(2)}, u32[]{:S(2)}) async-start(bf16[4,2,64,256]{3,2,1,0:T(8,128)(2,1)} %bitcast.11), calls=%async_computation.3 | async-start | bytes 524288 | tf_op jit(solution)/shard_map/all_to_all | solution.py:242
  66.0 23.4 %collective-permute-start.8 = (bf16[8,2,64,128]{3,2,1,0:T(8,128)(2,1)S(1)}, bf16[8,2,64,128]{3,2,1,0:T(8,128)(2,1)S(1)}, u32[]{:S(2)}, u32[]{:S(2)}) collective-permute-start(bf16[8,2,64,128]{3,2,1,0:T(8,128)(2,1)S(1)} %get-tuple-element.86), channel_id=1, source_target_pairs={{0,384},{128,256},{256,128},{384,0},{1,385},{129,257},{257,129},{3... | collective-permute-start | bytes 786440 | tf_op jit(solution)/shard_map/ppermute | solution.py:199
  69.1 20.3 %collective-permute-start.7 = (bf16[8,2,64,128]{3,2,1,0:T(8,128)(2,1)S(1)}, bf16[8,2,64,128]{3,2,1,0:T(8,128)(2,1)S(1)}, u32[]{:S(2)}, u32[]{:S(2)}) collective-permute-start(bf16[8,2,64,128]{3,2,1,0:T(8,128)(2,1)S(1)} %get-tuple-element.87), channel_id=1, source_target_pairs={{0,256},{128,384},{256,0},{384,128},{1,257},{129,385},{257,1},{385... | collective-permute-start | bytes 786440 | tf_op jit(solution)/shard_map/ppermute | solution.py:199
  72.5 16.9 %collective-permute-start.6 = (bf16[8,2,64,128]{3,2,1,0:T(8,128)(2,1)S(1)}, bf16[8,2,64,128]{3,2,1,0:T(8,128)(2,1)S(1)}, u32[]{:S(2)}, u32[]{:S(2)}) collective-permute-start(bf16[8,2,64,128]{3,2,1,0:T(8,128)(2,1)S(1)} %get-tuple-element.88), channel_id=1, source_target_pairs={{0,128},{128,0},{256,384},{384,256},{1,129},{129,1},{257,385},{385... | collective-permute-start | bytes 786440 | tf_op jit(solution)/shard_map/ppermute | solution.py:199
  76.0 11.9 %collective-permute-start.5 = (bf16[4,64,256]{2,1,0:T(8,128)(2,1)S(1)}, bf16[4,64,256]{2,1,0:T(8,128)(2,1)S(1)}, u32[]{:S(2)}, u32[]{:S(2)}) collective-permute-start(bf16[4,64,256]{2,1,0:T(8,128)(2,1)S(1)} %pad_maximum_fusion.1.mine_ref), channel_id=1, source_target_pairs={{0,64},{64,0},{1,65},{65,1},{2,66},{66,2},{3,67},{67,3},{4,68},{68... | collective-permute-start | bytes 393224 | tf_op jit(solution)/shard_map/ppermute | solution.py:199
  89.4 10.7 %copy-start = (bf16[128,768]{1,0:T(8,128)(2,1)S(1)}, bf16[128,768]{1,0:T(8,128)(2,1)}, u32[]{:S(2)}) copy-start(bf16[128,768]{1,0:T(8,128)(2,1)} %refs_2_) | copy-start | bytes 589828
  89.4 27.7 %all-to-all-start.4 = ((bf16[4,2,64,768]{3,2,1,0:T(8,128)(2,1)}), bf16[4,2,64,768]{3,2,1,0:T(8,128)(2,1)S(1)}, u32[]{:S(2)}, u32[]{:S(2)}) async-start(bf16[4,2,64,768]{3,2,1,0:T(8,128)(2,1)} %shard_map.70), calls=%async_computation.4 | async-start | bytes 1572864 | tf_op jit(solution)/shard_map/all_to_all | solution.py:249
  100.1 12.8 %collective-permute-start.11 = (bf16[128,768]{1,0:T(8,128)(2,1)S(1)}, bf16[128,768]{1,0:T(8,128)(2,1)S(1)}, u32[]{:S(2)}, u32[]{:S(2)}) collective-permute-start(bf16[128,768]{1,0:T(8,128)(2,1)S(1)} %copy-done), channel_id=1, source_target_pairs={{0,384},{128,256},{256,128},{384,0},{1,385},{129,257},{257,129},{3... | collective-permute-start | bytes 589832 | tf_op jit(solution)/shard_map/ppermute | solution.py:199
  103.2 11.2 %collective-permute-start.10 = (bf16[128,768]{1,0:T(8,128)(2,1)S(1)}, bf16[128,768]{1,0:T(8,128)(2,1)S(1)}, u32[]{:S(2)}, u32[]{:S(2)}) collective-permute-start(bf16[128,768]{1,0:T(8,128)(2,1)S(1)} %copy-done), channel_id=1, source_target_pairs={{0,256},{128,384},{256,0},{384,128},{1,257},{129,385},{257,1},{385... | collective-permute-start | bytes 589832 | tf_op jit(solution)/shard_map/ppermute | solution.py:199
  106.6 9.7 %collective-permute-start.9 = (bf16[128,768]{1,0:T(8,128)(2,1)S(1)}, bf16[128,768]{1,0:T(8,128)(2,1)S(1)}, u32[]{:S(2)}, u32[]{:S(2)}) collective-permute-start(bf16[128,768]{1,0:T(8,128)(2,1)S(1)} %copy-done), channel_id=1, source_target_pairs={{0,128},{128,0},{256,384},{384,256},{1,129},{129,1},{257,385},{385... | collective-permute-start | bytes 589832 | tf_op jit(solution)/shard_map/ppermute | solution.py:199
  117.1 4.2 %collective-permute-start.12 = (bf16[512,768]{1,0:T(8,128)(2,1)S(1)}, bf16[512,768]{1,0:T(8,128)(2,1)S(1)}, u32[]{:S(2)}, u32[]{:S(2)}) collective-permute-start(bf16[512,768]{1,0:T(8,128)(2,1)S(1)} %bitcast.36), channel_id=1, source_target_pairs={{0,8},{8,0},{1,9},{9,1},{2,10},{10,2},{3,11},{11,3},{4,12},{12,4},... | collective-permute-start | bytes 2359304 | tf_op jit(solution)/shard_map/ppermute | solution.py:199
  146.2 34.2 %collective-permute-start.13 = (bf16[4,256,128]{2,1,0:T(8,128)(2,1)S(1)}, bf16[4,256,128]{2,1,0:T(8,128)(2,1)S(1)}, u32[]{:S(2)}, u32[]{:S(2)}) collective-permute-start(bf16[4,256,128]{2,1,0:T(8,128)(2,1)S(1)} %bitcast_reduce_fusion.mine_ref), channel_id=1, source_target_pairs={{0,4},{4,0},{1,5},{5,1},{2,6},{6,2},{3,7},{7,3},{8,12},{12,8},{9,1... | collective-permute-start | bytes 786440 | tf_op jit(solution)/shard_map/ppermute | solution.py:199
  156.0 25.0 %collective-permute-start.14 = (bf16[128,768]{1,0:T(8,128)(2,1)S(1)}, bf16[128,768]{1,0:T(8,128)(2,1)S(1)}, u32[]{:S(2)}, u32[]{:S(2)}) collective-permute-start(bf16[128,768]{1,0:T(8,128)(2,1)S(1)} %get-tuple-element.73), channel_id=1, source_target_pairs={{0,128},{128,0},{256,384},{384,256},{1,129},{129,1},{257,385},{385... | collective-permute-start | bytes 589832 | tf_op jit(solution)/shard_map/ppermute | solution.py:199
  157.9 23.1 %collective-permute-start.15 = (bf16[128,768]{1,0:T(8,128)(2,1)S(1)}, bf16[128,768]{1,0:T(8,128)(2,1)S(1)}, u32[]{:S(2)}, u32[]{:S(2)}) collective-permute-start(bf16[128,768]{1,0:T(8,128)(2,1)S(1)} %get-tuple-element.74), channel_id=1, source_target_pairs={{0,256},{128,384},{256,0},{384,128},{1,257},{129,385},{257,1},{385... | collective-permute-start | bytes 589832 | tf_op jit(solution)/shard_map/ppermute | solution.py:199
  162.4 18.6 %collective-permute-start.16 = (bf16[128,768]{1,0:T(8,128)(2,1)S(1)}, bf16[128,768]{1,0:T(8,128)(2,1)S(1)}, u32[]{:S(2)}, u32[]{:S(2)}) collective-permute-start(bf16[128,768]{1,0:T(8,128)(2,1)S(1)} %get-tuple-element.75), channel_id=1, source_target_pairs={{0,384},{128,256},{256,128},{384,0},{1,385},{129,257},{257,129},{3... | collective-permute-start | bytes 589832 | tf_op jit(solution)/shard_map/ppermute | solution.py:199
  (3 other events, 2.3 us)
